TPU v7x, 512 devices: a whole 4x4x16 slice. The times are simulated.
512 devices in a mesh: seq: 32 (over y, x, core), head: 16 (over z).
Axes of the slice: x: 4, y: 4, z: 16, core: 2. Of those that a mesh axis runs over, the one named last changes fastest.
Arguments:
- queries: bfloat16 [65536, 2048], P('seq', 'head'), may hold values from -6 to 6
- keys: bfloat16 [65536, 2048], P('seq', 'head'), may hold values from -6 to 6
- values: bfloat16 [65536, 2048], P('seq', 'head'), may hold values from -6 to 6
- level_ids: int32 [65536], P('seq'), may hold values from 0 to 63
- level_table: float32 [64, 17], replicated, may hold values from 0 to 4, as said below
- out_cotangent: bfloat16 [65536, 2048], P('seq', 'head'), may hold values from -6 to 6
Outputs:
- attn_out: bfloat16 [65536, 2048], P('seq', 'head')
- weight_grad: float32 [2048, 2048], P('seq', 'head')
Inputs may be any that keep to these rules, and one draw needn't show every extreme that they name: `level_table`: positive coefficients.
All inputs are finite; a program needn't handle non-finite values.
Results may differ from a plain program's by a relative error of at most 0.0043.
Values may be sent and summed in bfloat16 or wider, within the bound.
No kernel may reach another device: no remote copies, remote signals or barrier semaphores. Data moves between devices by JAX's collectives and lax.ppermute only.
A program may use at most 64 MiB of HBM per device.

v0:
```python
import functools

import jax
import jax.numpy as jnp
from jax import lax
from jax.experimental import pallas as pl
from jax.experimental.pallas import tpu as pltpu
from jax.sharding import PartitionSpec as P

EPSILON = 1e-06
HIGHEST = lax.Precision.HIGHEST
PIECE = 512
TILE = 128
RING_ROWS = 40
STREAMS = 1


def dot_t(a, b):
    return lax.dot_general(a, b, (((1,), (1,)), ((), ())), preferred_element_type=jnp.float32)


def dot(a, b):
    return jnp.dot(a, b, preferred_element_type=jnp.float32)


def local_kernel(piece, q_ref, k_ref, v_ref, c_ref, out_ref):
    base = piece * PIECE
    piece_bits = PIECE.bit_length() - 1
    tile_bits = TILE.bit_length() - 1
    q = q_ref[...]
    total = jnp.zeros((PIECE, q.shape[1]), jnp.float32)
    first = 0
    for bit in reversed(range(max(piece.bit_length(), 1))):
        if not (piece >> bit) & 1:
            continue
        last = first + (PIECE << bit)
        level = piece_bits + bit + 1
        scores = dot_t(q, k_ref[first:last, :])
        mixed = (scores * c_ref[:, level : level + 1]).astype(jnp.bfloat16)
        total = total + dot(mixed, v_ref[first:last, :])
        first = last
    out_ref[...] = total
    for bit in reversed(range(piece_bits - tile_bits)):
        half = TILE << bit
        level = tile_bits + bit + 1
        for start in range(0, PIECE, 2 * half):
            rows = slice(start + half, start + 2 * half)
            cols = slice(base + start, base + start + half)
            scores = dot_t(q_ref[rows, :], k_ref[cols, :])
            mixed = (scores * c_ref[rows, level : level + 1]).astype(jnp.bfloat16)
            out_ref[rows, :] += dot(mixed, v_ref[cols, :])
    row = lax.broadcasted_iota(jnp.int32, (TILE, TILE), 0)
    col = lax.broadcasted_iota(jnp.int32, (TILE, TILE), 1)
    apart = jnp.bitwise_xor(row, col)
    causal = col <= row
    for start in range(0, PIECE, TILE):
        rows = slice(start, start + TILE)
        cols = slice(base + start, base + start + TILE)
        weights = jnp.broadcast_to(c_ref[rows, 0:1], (TILE, TILE))
        for level in range(1, tile_bits + 1):
            weights = jnp.where(apart >= 1 << (level - 1), c_ref[rows, level : level + 1], weights)
        weights = jnp.where(causal, weights, 0.0)
        mixed = (dot_t(q_ref[rows, :], k_ref[cols, :]) * weights).astype(jnp.bfloat16)
        out_ref[rows, :] += dot(mixed, v_ref[cols, :])


def local_piece(piece, queries, keys, values, coeff):
    head_dim = queries.shape[1]
    upto = (piece + 1) * PIECE
    levels = coeff.shape[1]
    return pl.pallas_call(
        functools.partial(local_kernel, piece),
        out_shape=jax.ShapeDtypeStruct((PIECE, head_dim), jnp.float32),
        grid=(1,),
        in_specs=[
            pl.BlockSpec((PIECE, head_dim), lambda i: (piece, 0)),
            pl.BlockSpec((upto, head_dim), lambda i: (0, 0)),
            pl.BlockSpec((upto, head_dim), lambda i: (0, 0)),
            pl.BlockSpec((PIECE, levels), lambda i: (piece, 0)),
        ],
        out_specs=pl.BlockSpec((PIECE, head_dim), lambda i: (0, 0)),
        compiler_params=pltpu.CompilerParams(vmem_limit_bytes=32 * 1024 * 1024),
        cost_estimate=pl.CostEstimate(
            flops=4 * PIECE * upto * head_dim, bytes_accessed=4 * upto * head_dim, transcendentals=0
        ),
    )(queries, keys, values, coeff)


def finish_kernel(first_level, seq_bits, l0, l1, l2, l3, q_ref, c_ref, hi_ref, lo_ref, out_ref):
    locals_ = (l0, l1, l2, l3)
    for piece in range(4):
        rows = slice(piece * PIECE, (piece + 1) * PIECE)
        q = q_ref[rows, :]
        total = locals_[piece][...]
        cross = jnp.zeros_like(total)
        for j in range(seq_bits):
            readout = dot(q, hi_ref[j]) + dot(q, lo_ref[j])
            level = first_level + j
            cross = cross + readout * c_ref[rows, level : level + 1]
        total = total + cross
        mean = jnp.mean(total * total, axis=1, keepdims=True)
        out_ref[rows, :] = (total * lax.rsqrt(mean + EPSILON)).astype(jnp.bfloat16)


def finish(pieces, queries, coeff, states, first_level):
    hi = states.astype(jnp.bfloat16)
    lo = (states - hi.astype(jnp.float32)).astype(jnp.bfloat16)
    return pl.pallas_call(
        functools.partial(finish_kernel, first_level, states.shape[0]),
        out_shape=jax.ShapeDtypeStruct(queries.shape, jnp.bfloat16),
        compiler_params=pltpu.CompilerParams(vmem_limit_bytes=32 * 1024 * 1024),
        cost_estimate=pl.CostEstimate(
            flops=20 * queries.shape[0] * 128 * 128, bytes_accessed=4 << 20, transcendentals=0
        ),
    )(*pieces, queries, coeff, hi, lo)


def ring_gather(shard, axis, streams):
    size = lax.axis_size(axis)
    right = [(i, (i + 1) % size) for i in range(size)]
    left = [(i, (i - 1) % size) for i in range(size)]
    rows = shard.shape[0] // streams
    parts = []
    for stream in range(streams):
        own = shard[stream * rows : (stream + 1) * rows]
        arrived = {0: own}
        up, down = own, own
        for step in range(1, size // 2):
            up = lax.ppermute(up, axis, right)
            down = lax.ppermute(down, axis, left)
            arrived[size - step] = up
            arrived[step] = down
        if stream % 2 == 0:
            arrived[size // 2] = lax.ppermute(up, axis, right)
        else:
            arrived[size // 2] = lax.ppermute(down, axis, left)
        parts.append([arrived[k] for k in range(size)])
    return parts


def body(queries, keys, values, level_ids, level_table, out_cotangent):
    block_len, head_dim = queries.shape
    n_seq = lax.axis_size("seq")
    n_head = lax.axis_size("head")
    local_bits = block_len.bit_length() - 1
    seq_bits = n_seq.bit_length() - 1
    table_rows = level_table.shape[0]
    own_index = lax.axis_index("seq")
    own_head = lax.axis_index("head")

    cot = out_cotangent.T.reshape(2, head_dim // 2, block_len)
    ring_part = cot[:, :RING_ROWS].reshape(2 * RING_ROWS, block_len)
    gather_part = cot[:, RING_ROWS:].reshape(head_dim - 2 * RING_ROWS, block_len)
    gathered = lax.all_gather(gather_part, "head", axis=0)
    ring = ring_gather(ring_part, "head", STREAMS)

    state = lax.dot_general(
        keys, values, (((0,), (0,)), ((), ())), preferred_element_type=jnp.float32
    )
    states = lax.all_to_all(
        jnp.broadcast_to(state, (n_seq, head_dim, head_dim)), "seq", 0, 0, tiled=True
    )
    source = jnp.arange(n_seq, dtype=jnp.int32)
    apart = jnp.bitwise_xor(own_index, source)
    select = jnp.stack(
        [
            ((jnp.right_shift(apart, level) == 1) & (source < own_index)).astype(jnp.float32)
            for level in range(seq_bits)
        ]
    )
    level_states = jnp.einsum("ji,ide->jde", select, states, precision=HIGHEST)

    onehot = (level_ids[:, None] == jnp.arange(table_rows, dtype=jnp.int32)[None, :]).astype(
        jnp.float32
    )
    coeff = jnp.dot(onehot, level_table, precision=HIGHEST, preferred_element_type=jnp.float32)
    pieces = [
        local_piece(piece, queries, keys, values, coeff) for piece in range(block_len // PIECE)
    ]
    attn_out = finish(pieces, queries, coeff, level_states, local_bits + 1)

    scale = (block_len * n_seq) ** (-0.5)

    def own_share(products):
        rows = products.shape[2]
        sent = products.reshape(n_seq, rows, head_dim).astype(jnp.bfloat16)
        arrived = lax.all_to_all(sent, "seq", 0, 0, tiled=True)
        return arrived.astype(jnp.float32).sum(axis=0) * scale

    streams = []
    for parts in ring:
        products = jnp.stack([dot(part, attn_out) for part in parts])
        doubled = jnp.concatenate([products, products], axis=0).astype(jnp.bfloat16)
        streams.append(lax.dynamic_slice_in_dim(doubled, n_head - own_head, n_head, 0))
    products = jnp.concatenate(streams, axis=1).reshape(n_head, 2, RING_ROWS, head_dim)
    upper = own_share(products)
    rest = dot(gathered.reshape(-1, block_len), attn_out)
    lower = own_share(rest.reshape(n_head, 2, head_dim // 2 - RING_ROWS, head_dim))
    return attn_out, jnp.concatenate([upper, lower], axis=0)


def solution(mesh):
    in_specs = (
        P("seq", "head"),
        P("seq", "head"),
        P("seq", "head"),
        P("seq"),
        P(),
        P("seq", "head"),
    )
    out_specs = (P("seq", "head"), P("seq", "head"))
    return jax.shard_map(body, mesh=mesh, in_specs=in_specs, out_specs=out_specs, check_vma=False)
```

profile of v0, /device:TPU:1, one launch (start us, length us, event | category | flops | bytes accessed | tf_op | source)
XLA Modules:
  0.0 182.9 jit_solution(980206887852884976)
XLA Ops:
  7.2 1.5 fusion.22
  8.7 1.6 broadcast_in_dim.2
  10.3 11.3 %all-to-all-start = ((f32[32,128,128]{2,1,0:T(8,128)}), f32[32,128,128]{2,1,0:T(8,128)}, u32[]{:S(2)}, u32[]{:S(2)}) async-start(f32[32,128,128]{2,1,0:T(8,128)} %broadcast_in_dim.2), calls=%async_computation | async-start | bytes 4194304 | tf_op jit(solution)/shard_map/all_to_all | solution.py:160
  21.8 0.2 copy.32
  22.0 8.7 %collective-permute-start = (bf16[80,2048]{1,0:T(8,128)(2,1)S(1)}, bf16[80,2048]{1,0:T(8,128)(2,1)S(1)}, u32[]{:S(2)}, u32[]{:S(2)}) collective-permute-start(bf16[80,2048]{1,0:T(8,128)(2,1)S(1)} %bitcast.117), channel_id=1, source_target_pairs={{0,15},{1,0},{2,1},{3,2},{4,3},{5,4},{6,5},{7,6},{8,7},{9,8},{10,9... | collective-permute-start | bytes 983048 | tf_op jit(solution)/shard_map/ppermute | solution.py:130
  30.7 1.9 %collective-permute-start.7 = (bf16[80,2048]{1,0:T(8,128)(2,1)S(1)}, bf16[80,2048]{1,0:T(8,128)(2,1)S(1)}, u32[]{:S(2)}, u32[]{:S(2)}) collective-permute-start(bf16[80,2048]{1,0:T(8,128)(2,1)S(1)} %bitcast.118), channel_id=1, source_target_pairs={{0,1},{1,2},{2,3},{3,4},{4,5},{5,6},{6,7},{7,8},{8,9},{9,10},{10,1... | collective-permute-start | bytes 983048 | tf_op jit(solution)/shard_map/ppermute | solution.py:129
  32.7 4.8 %collective-permute-done = bf16[80,2048]{1,0:T(8,128)(2,1)S(1)} collective-permute-done((bf16[80,2048]{1,0:T(8,128)(2,1)S(1)}, bf16[80,2048]{1,0:T(8,128)(2,1)S(1)}, u32[]{:S(2)}, u32[]{:S(2)}) %collective-permute-start) | collective-permute-done | bytes 327712 | tf_op jit(solution)/shard_map/ppermute | solution.py:130
  37.5 5.4 %collective-permute-start.1 = (bf16[80,2048]{1,0:T(8,128)(2,1)S(1)}, bf16[80,2048]{1,0:T(8,128)(2,1)S(1)}, u32[]{:S(2)}, u32[]{:S(2)}) collective-permute-start(bf16[80,2048]{1,0:T(8,128)(2,1)S(1)} %collective-permute-done), channel_id=1, source_target_pairs={{0,15},{1,0},{2,1},{3,2},{4,3},{5,4},{6,5},{7,6},{8,7},{9,8},{10,9... | collective-permute-start | bytes 983048 | tf_op jit(solution)/shard_map/ppermute | solution.py:130
  42.9 0.7 copy-done.10
  43.7 1.9 %collective-permute-start.8 = (bf16[80,2048]{1,0:T(8,128)(2,1)S(1)}, bf16[80,2048]{1,0:T(8,128)(2,1)S(1)}, u32[]{:S(2)}, u32[]{:S(2)}) collective-permute-start(bf16[80,2048]{1,0:T(8,128)(2,1)S(1)} %collective-permute-done.7), channel_id=1, source_target_pairs={{0,1},{1,2},{2,3},{3,4},{4,5},{5,6},{6,7},{7,8},{8,9},{9,10},{10,1... | collective-permute-start | bytes 983048 | tf_op jit(solution)/shard_map/ppermute | solution.py:129
  45.6 3.3 %collective-permute-done.1 = bf16[80,2048]{1,0:T(8,128)(2,1)S(1)} collective-permute-done((bf16[80,2048]{1,0:T(8,128)(2,1)S(1)}, bf16[80,2048]{1,0:T(8,128)(2,1)S(1)}, u32[]{:S(2)}, u32[]{:S(2)}) %collective-permute-start.1) | collective-permute-done | bytes 327712 | tf_op jit(solution)/shard_map/ppermute | solution.py:130
  48.9 5.4 %collective-permute-start.2 = (bf16[80,2048]{1,0:T(8,128)(2,1)S(1)}, bf16[80,2048]{1,0:T(8,128)(2,1)S(1)}, u32[]{:S(2)}, u32[]{:S(2)}) collective-permute-start(bf16[80,2048]{1,0:T(8,128)(2,1)S(1)} %collective-permute-done.1), channel_id=1, source_target_pairs={{0,15},{1,0},{2,1},{3,2},{4,3},{5,4},{6,5},{7,6},{8,7},{9,8},{10,9... | collective-permute-start | bytes 983048 | tf_op jit(solution)/shard_map/ppermute | solution.py:130
  54.3 0.4 collective-permute-done.8
  54.7 0.7 copy-done.12
  55.4 1.9 %collective-permute-start.9 = (bf16[80,2048]{1,0:T(8,128)(2,1)S(1)}, bf16[80,2048]{1,0:T(8,128)(2,1)S(1)}, u32[]{:S(2)}, u32[]{:S(2)}) collective-permute-start(bf16[80,2048]{1,0:T(8,128)(2,1)S(1)} %collective-permute-done.8), channel_id=1, source_target_pairs={{0,1},{1,2},{2,3},{3,4},{4,5},{5,6},{6,7},{7,8},{8,9},{9,10},{10,1... | collective-permute-start | bytes 983048 | tf_op jit(solution)/shard_map/ppermute | solution.py:129
  57.3 2.1 %collective-permute-done.2 = bf16[80,2048]{1,0:T(8,128)(2,1)S(1)} collective-permute-done((bf16[80,2048]{1,0:T(8,128)(2,1)S(1)}, bf16[80,2048]{1,0:T(8,128)(2,1)S(1)}, u32[]{:S(2)}, u32[]{:S(2)}) %collective-permute-start.2) | collective-permute-done | bytes 327712 | tf_op jit(solution)/shard_map/ppermute | solution.py:130
  59.4 5.3 %collective-permute-start.3 = (bf16[80,2048]{1,0:T(8,128)(2,1)S(1)}, bf16[80,2048]{1,0:T(8,128)(2,1)S(1)}, u32[]{:S(2)}, u32[]{:S(2)}) collective-permute-start(bf16[80,2048]{1,0:T(8,128)(2,1)S(1)} %collective-permute-done.2), channel_id=1, source_target_pairs={{0,15},{1,0},{2,1},{3,2},{4,3},{5,4},{6,5},{7,6},{8,7},{9,8},{10,9... | collective-permute-start | bytes 983048 | tf_op jit(solution)/shard_map/ppermute | solution.py:130
  64.7 0.7 collective-permute-done.9
  65.5 1.9 %collective-permute-start.10 = (bf16[80,2048]{1,0:T(8,128)(2,1)S(1)}, bf16[80,2048]{1,0:T(8,128)(2,1)S(1)}, u32[]{:S(2)}, u32[]{:S(2)}) collective-permute-start(bf16[80,2048]{1,0:T(8,128)(2,1)S(1)} %collective-permute-done.9), channel_id=1, source_target_pairs={{0,1},{1,2},{2,3},{3,4},{4,5},{5,6},{6,7},{7,8},{8,9},{9,10},{10,1... | collective-permute-start | bytes 983048 | tf_op jit(solution)/shard_map/ppermute | solution.py:129
  67.4 0.7 slice.9
  68.1 0.8 collective-permute-done.3
  69.0 5.3 %collective-permute-start.4 = (bf16[80,2048]{1,0:T(8,128)(2,1)S(1)}, bf16[80,2048]{1,0:T(8,128)(2,1)}, u32[]{:S(2)}, u32[]{:S(2)}) collective-permute-start(bf16[80,2048]{1,0:T(8,128)(2,1)S(1)} %collective-permute-done.3), channel_id=1, source_target_pairs={{0,15},{1,0},{2,1},{3,2},{4,3},{5,4},{6,5},{7,6},{8,7},{9,8},{10,9... | collective-permute-start | bytes 983048 | tf_op jit(solution)/shard_map/ppermute | solution.py:130
  74.3 0.2 collective-permute-done.10
  74.5 1.9 %collective-permute-start.11 = (bf16[80,2048]{1,0:T(8,128)(2,1)S(1)}, bf16[80,2048]{1,0:T(8,128)(2,1)}, u32[]{:S(2)}, u32[]{:S(2)}) collective-permute-start(bf16[80,2048]{1,0:T(8,128)(2,1)S(1)} %collective-permute-done.10), channel_id=1, source_target_pairs={{0,1},{1,2},{2,3},{3,4},{4,5},{5,6},{6,7},{7,8},{8,9},{9,10},{10,1... | collective-permute-start | bytes 983048 | tf_op jit(solution)/shard_map/ppermute | solution.py:129
  76.5 1.8 collective-permute-done.4
  78.3 5.1 %collective-permute-start.5 = (bf16[80,2048]{1,0:T(8,128)(2,1)}, bf16[80,2048]{1,0:T(8,128)(2,1)}, u32[]{:S(2)}, u32[]{:S(2)}) collective-permute-start(bf16[80,2048]{1,0:T(8,128)(2,1)} %collective-permute-done.4), channel_id=1, source_target_pairs={{0,15},{1,0},{2,1},{3,2},{4,3},{5,4},{6,5},{7,6},{8,7},{9,8},{10,9... | collective-permute-start | bytes 983048 | tf_op jit(solution)/shard_map/ppermute | solution.py:130
  83.4 0.2 collective-permute-done.11
  83.6 1.9 %collective-permute-start.12 = (bf16[80,2048]{1,0:T(8,128)(2,1)}, bf16[80,2048]{1,0:T(8,128)(2,1)}, u32[]{:S(2)}, u32[]{:S(2)}) collective-permute-start(bf16[80,2048]{1,0:T(8,128)(2,1)} %collective-permute-done.11), channel_id=1, source_target_pairs={{0,1},{1,2},{2,3},{3,4},{4,5},{5,6},{6,7},{7,8},{8,9},{9,10},{10,1... | collective-permute-start | bytes 983048 | tf_op jit(solution)/shard_map/ppermute | solution.py:129
  85.6 1.0 fusion.19.c_ref
  86.6 1.1 shard_map.77.l0
  87.7 1.2 shard_map.78.l1
  88.9 1.7 shard_map.79.l2
  90.6 1.9 %shard_map.80.l3 = f32[512,128]{1,0:T(8,128)S(1)} custom-call(bf16[2048,128]{1,0:T(8,128)(2,1)S(1)} %copy-done.3, bf16[2048,128]{1,0:T(8,128)(2,1)S(1)} %copy-done.1, bf16[2048,128]{1,0:T(8,128)(2,1)S(1)} %copy-done.2, f32[2048,17]{1,0:T(8,128)S(1)} %fusion.19.c_ref), custom_call_target="tpu_custom_call" | custom-call | flops 536870912 | bytes 1048576 | tf_op jit(solution)/shard_map/pallas_call | solution.py:71
  92.5 0.7 copy-done.4
  93.2 4.7 %collective-permute-start.6 = (bf16[80,2048]{1,0:T(8,128)(2,1)}, bf16[80,2048]{1,0:T(8,128)(2,1)}, u32[]{:S(2)}, u32[]{:S(2)}) collective-permute-start(bf16[80,2048]{1,0:T(8,128)(2,1)} %collective-permute-done.5), channel_id=1, source_target_pairs={{0,15},{1,0},{2,1},{3,2},{4,3},{5,4},{6,5},{7,6},{8,7},{9,8},{10,9... | collective-permute-start | bytes 983048 | tf_op jit(solution)/shard_map/ppermute | solution.py:130
  97.9 2.1 %collective-permute-start.13 = (bf16[80,2048]{1,0:T(8,128)(2,1)}, bf16[80,2048]{1,0:T(8,128)(2,1)}, u32[]{:S(2)}, u32[]{:S(2)}) collective-permute-start(bf16[80,2048]{1,0:T(8,128)(2,1)} %collective-permute-done.12), channel_id=1, source_target_pairs={{0,1},{1,2},{2,3},{3,4},{4,5},{5,6},{6,7},{7,8},{8,9},{9,10},{10,1... | collective-permute-start | bytes 983048 | tf_op jit(solution)/shard_map/ppermute | solution.py:129
  100.1 3.5 %fusion = f32[5,128,128]{2,0,1:T(8,128)S(1)} fusion(f32[32,128,128]{2,1,0:T(8,128)} %all-to-all-done, pred[5,32]{1,0:T(8,128)(4,1)S(1)} %stack.60), kind=kOutput, calls=%fused_computation | convolution fusion | flops 31457280 | bytes 2424992 | tf_op jit(solution)/shard_map/ji,ide->jde/dot_general | solution.py:171
  103.5 0.1 copy.41.hi_ref
  103.6 0.1 subtract_convert_fusion.lo_ref
  103.7 3.0 %shard_map.81 = bf16[2048,128]{1,0:T(8,128)(2,1)} custom-call(f32[512,128]{1,0:T(8,128)S(1)} %shard_map.77.l0, f32[512,128]{1,0:T(8,128)S(1)} %shard_map.78.l1, f32[512,128]{1,0:T(8,128)S(1)} %shard_map.79.l2, f32[512,128]{1,0:T(8,128)S(1)} %copy-done.5, bf16[2048,128]{1,0:T(8,128)(2,1)S(1)} %copy-done.3, f32[2048,17]{1,0:T(8,128)S(1)} %fusion.19.c_ref, ...), custom_call_target="tpu_custom_call" | custom-call | flops 671088640 | bytes 4194304 | tf_op jit(solution)/shard_map/pallas_call | solution.py:108
  106.7 1.4 constant_dynamic-update-slice_fusion.31
  108.1 1.3 constant_dynamic-update-slice_fusion.30
  109.4 1.3 constant_dynamic-update-slice_fusion.29
  110.7 0.3 constant_dynamic-update-slice_fusion.28
  111.0 0.3 constant_dynamic-update-slice_fusion.27
  111.3 1.2 constant_dynamic-update-slice_fusion.26
  112.5 1.9 %collective-permute-start.14 = (bf16[80,2048]{1,0:T(8,128)(2,1)}, bf16[80,2048]{1,0:T(8,128)(2,1)S(1)}, u32[]{:S(2)}, u32[]{:S(2)}) collective-permute-start(bf16[80,2048]{1,0:T(8,128)(2,1)} %collective-permute-done.13), channel_id=1, source_target_pairs={{0,1},{1,2},{2,3},{3,4},{4,5},{5,6},{6,7},{7,8},{8,9},{9,10},{10,1... | collective-permute-start | bytes 983048 | tf_op jit(solution)/shard_map/ppermute | solution.py:134
  114.4 1.2 constant_dynamic-update-slice_fusion.25
  115.7 1.3 constant_dynamic-update-slice_fusion.24
  117.0 12.1 %collective-permute-done.14 = bf16[80,2048]{1,0:T(8,128)(2,1)S(1)} collective-permute-done((bf16[80,2048]{1,0:T(8,128)(2,1)}, bf16[80,2048]{1,0:T(8,128)(2,1)S(1)}, u32[]{:S(2)}, u32[]{:S(2)}) %collective-permute-start.14) | collective-permute-done | bytes 327712 | tf_op jit(solution)/shard_map/ppermute | solution.py:134
  129.1 0.3 constant_dynamic-update-slice_fusion.23
  129.3 1.3 constant_dynamic-update-slice_fusion.22
  130.6 1.3 constant_dynamic-update-slice_fusion.21
  131.9 1.2 constant_dynamic-update-slice_fusion.20
  133.1 0.3 constant_dynamic-update-slice_fusion.19
  133.4 0.3 constant_dynamic-update-slice_fusion.18
  133.7 0.3 constant_dynamic-update-slice_fusion.17
  134.0 0.3 constant_dynamic-update-slice_fusion.16
  134.5 24.7 %all_to_all.15 = bf16[32,40,128]{2,1,0:T(8,128)(2,1)S(1)} all-to-all(bf16[32,40,128]{2,1,0:T(8,128)(2,1)S(1)} %bitcast.120), channel_id=1, replica_groups=mesh['seq'=32,'head'=16] {'seq'}, dimensions={0} | all-to-all | bytes 655360 | tf_op jit(solution)/shard_map/all_to_all | solution.py:187
  159.2 3.1 %fusion.2 = bf16[768,128]{0,1:T(8,128)(2,1)S(1)} fusion(bf16[2048,128]{1,0:T(8,128)(2,1)S(1)} %copy-done.6, bf16[768,2048]{1,0:T(8,128)(2,1)} %bitcast.114), kind=kOutput, calls=%fused_computation.3 | convolution fusion | flops 402751488 | bytes 3866624 | tf_op jit(solution)/shard_map/dot_general | solution.py:23
  162.3 0.8 copy.33
  163.1 3.8 %all-to-all-start.2 = ((bf16[32,24,128]{2,1,0:T(8,128)(2,1)}), bf16[32,24,128]{2,1,0:T(8,128)(2,1)S(1)}, u32[]{:S(2)}, u32[]{:S(2)}) async-start(bf16[32,24,128]{2,1,0:T(8,128)(2,1)} %bitcast.41), calls=%async_computation.2 | async-start | bytes 393216 | tf_op jit(solution)/shard_map/all_to_all | solution.py:187
  167.0 8.4 %all-to-all-done.2 = bf16[32,24,128]{2,1,0:T(8,128)(2,1)S(1)} async-done(((bf16[32,24,128]{2,1,0:T(8,128)(2,1)}), bf16[32,24,128]{2,1,0:T(8,128)(2,1)S(1)}, u32[]{:S(2)}, u32[]{:S(2)}) %all-to-all-start.2) | async-done | bytes 196640 | tf_op jit(solution)/shard_map/all_to_all | solution.py:187
  175.4 0.6 pad_maximum_fusion
  (86 shorter events, 0.6 us)
Async XLA Ops:
  7.2 78.4 %copy-start = (f32[64,17]{0,1:T(8,128)S(1)}, f32[64,17]{0,1:T(8,128)}, u32[]{:S(2)}) copy-start(f32[64,17]{0,1:T(8,128)} %param.10) | copy-start | bytes 13060
  10.3 11.5 %copy-start.9 = (bf16[2048,128]{1,0:T(8,128)(2,1)S(1)}, bf16[2048,128]{1,0:T(8,128)(2,1)}, u32[]{:S(2)}) copy-start(bf16[2048,128]{1,0:T(8,128)(2,1)} %param.11) | copy-start | bytes 1572868
  10.3 89.7 %all-to-all-start = ((f32[32,128,128]{2,1,0:T(8,128)}), f32[32,128,128]{2,1,0:T(8,128)}, u32[]{:S(2)}, u32[]{:S(2)}) async-start(f32[32,128,128]{2,1,0:T(8,128)} %broadcast_in_dim.2), calls=%async_computation | async-start | bytes 4194304 | tf_op jit(solution)/shard_map/all_to_all | solution.py:160
  21.7 63.9 %copy-start.26 = (s32[2048]{0:T(1024)S(1)}, s32[2048]{0:T(1024)}, u32[]{:S(2)}) copy-start(s32[2048]{0:T(1024)} %param.9) | copy-start | bytes 24580
  21.7 64.9 %copy-start.1 = (bf16[2048,128]{1,0:T(8,128)(2,1)S(1)}, bf16[2048,128]{1,0:T(8,128)(2,1)}, u32[]{:S(2)}) copy-start(bf16[2048,128]{1,0:T(8,128)(2,1)} %k_ref.7) | copy-start | bytes 1572868
  21.7 64.9 %copy-start.2 = (bf16[2048,128]{1,0:T(8,128)(2,1)S(1)}, bf16[2048,128]{1,0:T(8,128)(2,1)}, u32[]{:S(2)}) copy-start(bf16[2048,128]{1,0:T(8,128)(2,1)} %v_ref.7) | copy-start | bytes 1572868
  21.7 64.9 %copy-start.3 = (bf16[2048,128]{1,0:T(8,128)(2,1)S(1)}, bf16[2048,128]{1,0:T(8,128)(2,1)}, u32[]{:S(2)}) copy-start(bf16[2048,128]{1,0:T(8,128)(2,1)} %q_ref.9) | copy-start | bytes 1572868
  21.7 137.5 %all-gather.2.cloned.1.call-start = ((), (), s32[]{:S(2)}) async-start(), calls=%async_computation.3 | async-start | bytes 3342336 | tf_op jit(solution)/shard_map/all_gather | solution.py:154
  22.0 46.1 %copy-start.7 = (bf16[2,40,2048]{2,1,0:T(8,128)(2,1)}, bf16[2,40,2048]{2,1,0:T(8,128)(2,1)S(1)}, u32[]{:S(2)}) copy-start(bf16[2,40,2048]{2,1,0:T(8,128)(2,1)S(1)} %slice.8) | copy-start | bytes 983044
  22.0 15.5 %collective-permute-start = (bf16[80,2048]{1,0:T(8,128)(2,1)S(1)}, bf16[80,2048]{1,0:T(8,128)(2,1)S(1)}, u32[]{:S(2)}, u32[]{:S(2)}) collective-permute-start(bf16[80,2048]{1,0:T(8,128)(2,1)S(1)} %bitcast.117), channel_id=1, source_target_pairs={{0,15},{1,0},{2,1},{3,2},{4,3},{5,4},{6,5},{7,6},{8,7},{9,8},{10,9... | collective-permute-start | bytes 983048 | tf_op jit(solution)/shard_map/ppermute | solution.py:130
  30.7 12.2 %collective-permute-start.7 = (bf16[80,2048]{1,0:T(8,128)(2,1)S(1)}, bf16[80,2048]{1,0:T(8,128)(2,1)S(1)}, u32[]{:S(2)}, u32[]{:S(2)}) collective-permute-start(bf16[80,2048]{1,0:T(8,128)(2,1)S(1)} %bitcast.118), channel_id=1, source_target_pairs={{0,1},{1,2},{2,3},{3,4},{4,5},{5,6},{6,7},{7,8},{8,9},{9,10},{10,1... | collective-permute-start | bytes 983048 | tf_op jit(solution)/shard_map/ppermute | solution.py:129
  37.5 28.0 %copy-start.18 = (bf16[80,2048]{1,0:T(8,128)(2,1)}, bf16[80,2048]{1,0:T(8,128)(2,1)S(1)}, u32[]{:S(2)}) copy-start(bf16[80,2048]{1,0:T(8,128)(2,1)S(1)} %collective-permute-done) | copy-start | bytes 983044
  37.5 11.4 %collective-permute-start.1 = (bf16[80,2048]{1,0:T(8,128)(2,1)S(1)}, bf16[80,2048]{1,0:T(8,128)(2,1)S(1)}, u32[]{:S(2)}, u32[]{:S(2)}) collective-permute-start(bf16[80,2048]{1,0:T(8,128)(2,1)S(1)} %collective-permute-done), channel_id=1, source_target_pairs={{0,15},{1,0},{2,1},{3,2},{4,3},{5,4},{6,5},{7,6},{8,7},{9,8},{10,9... | collective-permute-start | bytes 983048 | tf_op jit(solution)/shard_map/ppermute | solution.py:130
  42.9 0.8 copy-start.10
  43.7 11.0 %collective-permute-start.8 = (bf16[80,2048]{1,0:T(8,128)(2,1)S(1)}, bf16[80,2048]{1,0:T(8,128)(2,1)S(1)}, u32[]{:S(2)}, u32[]{:S(2)}) collective-permute-start(bf16[80,2048]{1,0:T(8,128)(2,1)S(1)} %collective-permute-done.7), channel_id=1, source_target_pairs={{0,1},{1,2},{2,3},{3,4},{4,5},{5,6},{6,7},{7,8},{8,9},{9,10},{10,1... | collective-permute-start | bytes 983048 | tf_op jit(solution)/shard_map/ppermute | solution.py:129
  48.9 16.6 %copy-start.20 = (bf16[80,2048]{1,0:T(8,128)(2,1)}, bf16[80,2048]{1,0:T(8,128)(2,1)S(1)}, u32[]{:S(2)}) copy-start(bf16[80,2048]{1,0:T(8,128)(2,1)S(1)} %collective-permute-done.1) | copy-start | bytes 983044
  48.9 10.6 %collective-permute-start.2 = (bf16[80,2048]{1,0:T(8,128)(2,1)S(1)}, bf16[80,2048]{1,0:T(8,128)(2,1)S(1)}, u32[]{:S(2)}, u32[]{:S(2)}) collective-permute-start(bf16[80,2048]{1,0:T(8,128)(2,1)S(1)} %collective-permute-done.1), channel_id=1, source_target_pairs={{0,15},{1,0},{2,1},{3,2},{4,3},{5,4},{6,5},{7,6},{8,7},{9,8},{10,9... | collective-permute-start | bytes 983048 | tf_op jit(solution)/shard_map/ppermute | solution.py:130
  54.7 0.7 copy-start.12
  55.4 10.1 %collective-permute-start.9 = (bf16[80,2048]{1,0:T(8,128)(2,1)S(1)}, bf16[80,2048]{1,0:T(8,128)(2,1)S(1)}, u32[]{:S(2)}, u32[]{:S(2)}) collective-permute-start(bf16[80,2048]{1,0:T(8,128)(2,1)S(1)} %collective-permute-done.8), channel_id=1, source_target_pairs={{0,1},{1,2},{2,3},{3,4},{4,5},{5,6},{6,7},{7,8},{8,9},{9,10},{10,1... | collective-permute-start | bytes 983048 | tf_op jit(solution)/shard_map/ppermute | solution.py:129
  59.4 26.1 %copy-start.22 = (bf16[80,2048]{1,0:T(8,128)(2,1)}, bf16[80,2048]{1,0:T(8,128)(2,1)S(1)}, u32[]{:S(2)}) copy-start(bf16[80,2048]{1,0:T(8,128)(2,1)S(1)} %collective-permute-done.2) | copy-start | bytes 983044
  59.4 9.5 %collective-permute-start.3 = (bf16[80,2048]{1,0:T(8,128)(2,1)S(1)}, bf16[80,2048]{1,0:T(8,128)(2,1)S(1)}, u32[]{:S(2)}, u32[]{:S(2)}) collective-permute-start(bf16[80,2048]{1,0:T(8,128)(2,1)S(1)} %collective-permute-done.2), channel_id=1, source_target_pairs={{0,15},{1,0},{2,1},{3,2},{4,3},{5,4},{6,5},{7,6},{8,7},{9,8},{10,9... | collective-permute-start | bytes 983048 | tf_op jit(solution)/shard_map/ppermute | solution.py:130
  65.5 18.2 %copy-start.14 = (bf16[80,2048]{1,0:T(8,128)(2,1)}, bf16[80,2048]{1,0:T(8,128)(2,1)S(1)}, u32[]{:S(2)}) copy-start(bf16[80,2048]{1,0:T(8,128)(2,1)S(1)} %collective-permute-done.9) | copy-start | bytes 983044
  65.5 9.0 %collective-permute-start.10 = (bf16[80,2048]{1,0:T(8,128)(2,1)S(1)}, bf16[80,2048]{1,0:T(8,128)(2,1)S(1)}, u32[]{:S(2)}, u32[]{:S(2)}) collective-permute-start(bf16[80,2048]{1,0:T(8,128)(2,1)S(1)} %collective-permute-done.9), channel_id=1, source_target_pairs={{0,1},{1,2},{2,3},{3,4},{4,5},{5,6},{6,7},{7,8},{8,9},{9,10},{10,1... | collective-permute-start | bytes 983048 | tf_op jit(solution)/shard_map/ppermute | solution.py:129
  69.0 17.6 %copy-start.24 = (bf16[80,2048]{1,0:T(8,128)(2,1)}, bf16[80,2048]{1,0:T(8,128)(2,1)S(1)}, u32[]{:S(2)}) copy-start(bf16[80,2048]{1,0:T(8,128)(2,1)S(1)} %collective-permute-done.3) | copy-start | bytes 983044
  69.0 9.3 %collective-permute-start.4 = (bf16[80,2048]{1,0:T(8,128)(2,1)S(1)}, bf16[80,2048]{1,0:T(8,128)(2,1)}, u32[]{:S(2)}, u32[]{:S(2)}) collective-permute-start(bf16[80,2048]{1,0:T(8,128)(2,1)S(1)} %collective-permute-done.3), channel_id=1, source_target_pairs={{0,15},{1,0},{2,1},{3,2},{4,3},{5,4},{6,5},{7,6},{8,7},{9,8},{10,9... | collective-permute-start | bytes 983048 | tf_op jit(solution)/shard_map/ppermute | solution.py:130
  74.5 9.1 %copy-start.16 = (bf16[80,2048]{1,0:T(8,128)(2,1)}, bf16[80,2048]{1,0:T(8,128)(2,1)S(1)}, u32[]{:S(2)}) copy-start(bf16[80,2048]{1,0:T(8,128)(2,1)S(1)} %collective-permute-done.10) | copy-start | bytes 983044
  74.5 9.1 %collective-permute-start.11 = (bf16[80,2048]{1,0:T(8,128)(2,1)S(1)}, bf16[80,2048]{1,0:T(8,128)(2,1)}, u32[]{:S(2)}, u32[]{:S(2)}) collective-permute-start(bf16[80,2048]{1,0:T(8,128)(2,1)S(1)} %collective-permute-done.10), channel_id=1, source_target_pairs={{0,1},{1,2},{2,3},{3,4},{4,5},{5,6},{6,7},{7,8},{8,9},{9,10},{10,1... | collective-permute-start | bytes 983048 | tf_op jit(solution)/shard_map/ppermute | solution.py:129
  78.3 14.9 %collective-permute-start.5 = (bf16[80,2048]{1,0:T(8,128)(2,1)}, bf16[80,2048]{1,0:T(8,128)(2,1)}, u32[]{:S(2)}, u32[]{:S(2)}) collective-permute-start(bf16[80,2048]{1,0:T(8,128)(2,1)} %collective-permute-done.4), channel_id=1, source_target_pairs={{0,15},{1,0},{2,1},{3,2},{4,3},{5,4},{6,5},{7,6},{8,7},{9,8},{10,9... | collective-permute-start | bytes 983048 | tf_op jit(solution)/shard_map/ppermute | solution.py:130
  83.6 14.3 %collective-permute-start.12 = (bf16[80,2048]{1,0:T(8,128)(2,1)}, bf16[80,2048]{1,0:T(8,128)(2,1)}, u32[]{:S(2)}, u32[]{:S(2)}) collective-permute-start(bf16[80,2048]{1,0:T(8,128)(2,1)} %collective-permute-done.11), channel_id=1, source_target_pairs={{0,1},{1,2},{2,3},{3,4},{4,5},{5,6},{6,7},{7,8},{8,9},{9,10},{10,1... | collective-permute-start | bytes 983048 | tf_op jit(solution)/shard_map/ppermute | solution.py:129
  92.5 0.7 copy-start.4
  93.2 10.5 %copy-start.5 = (f32[512,128]{1,0:T(8,128)S(1)}, f32[512,128]{1,0:T(8,128)}, u32[]{:S(2)}) copy-start(f32[512,128]{1,0:T(8,128)} %copy-done.4) | copy-start | bytes 786436
  93.2 22.5 %collective-permute-start.6 = (bf16[80,2048]{1,0:T(8,128)(2,1)}, bf16[80,2048]{1,0:T(8,128)(2,1)}, u32[]{:S(2)}, u32[]{:S(2)}) collective-permute-start(bf16[80,2048]{1,0:T(8,128)(2,1)} %collective-permute-done.5), channel_id=1, source_target_pairs={{0,15},{1,0},{2,1},{3,2},{4,3},{5,4},{6,5},{7,6},{8,7},{9,8},{10,9... | collective-permute-start | bytes 983048 | tf_op jit(solution)/shard_map/ppermute | solution.py:130
  97.9 14.6 %collective-permute-start.13 = (bf16[80,2048]{1,0:T(8,128)(2,1)}, bf16[80,2048]{1,0:T(8,128)(2,1)}, u32[]{:S(2)}, u32[]{:S(2)}) collective-permute-start(bf16[80,2048]{1,0:T(8,128)(2,1)} %collective-permute-done.12), channel_id=1, source_target_pairs={{0,1},{1,2},{2,3},{3,4},{4,5},{5,6},{6,7},{7,8},{8,9},{9,10},{10,1... | collective-permute-start | bytes 983048 | tf_op jit(solution)/shard_map/ppermute | solution.py:129
  103.6 3.1 %copy-start.8 = (bf16[2,40,2048]{2,1,0:T(8,128)(2,1)S(1)}, bf16[2,40,2048]{2,1,0:T(8,128)(2,1)}, u32[]{:S(2)}) copy-start(bf16[2,40,2048]{2,1,0:T(8,128)(2,1)} %copy-done.7) | copy-start | bytes 983044
  103.7 4.4 %copy-start.19 = (bf16[80,2048]{1,0:T(8,128)(2,1)S(1)}, bf16[80,2048]{1,0:T(8,128)(2,1)}, u32[]{:S(2)}) copy-start(bf16[80,2048]{1,0:T(8,128)(2,1)} %copy-done.18) | copy-start | bytes 983044
  103.7 5.7 %copy-start.21 = (bf16[80,2048]{1,0:T(8,128)(2,1)S(1)}, bf16[80,2048]{1,0:T(8,128)(2,1)}, u32[]{:S(2)}) copy-start(bf16[80,2048]{1,0:T(8,128)(2,1)} %copy-done.20) | copy-start | bytes 983044
  106.7 4.0 %copy-start.6 = (bf16[2048,128]{1,0:T(8,128)(2,1)S(1)}, bf16[2048,128]{1,0:T(8,128)(2,1)}, u32[]{:S(2)}) copy-start(bf16[2048,128]{1,0:T(8,128)(2,1)} %shard_map.81) | copy-start | bytes 1572868
  106.7 4.0 %copy-start.23 = (bf16[80,2048]{1,0:T(8,128)(2,1)S(1)}, bf16[80,2048]{1,0:T(8,128)(2,1)}, u32[]{:S(2)}) copy-start(bf16[80,2048]{1,0:T(8,128)(2,1)} %copy-done.22) | copy-start | bytes 983044
  106.7 4.3 %copy-start.25 = (bf16[80,2048]{1,0:T(8,128)(2,1)S(1)}, bf16[80,2048]{1,0:T(8,128)(2,1)}, u32[]{:S(2)}) copy-start(bf16[80,2048]{1,0:T(8,128)(2,1)} %copy-done.24) | copy-start | bytes 983044
  112.5 16.5 %collective-permute-start.14 = (bf16[80,2048]{1,0:T(8,128)(2,1)}, bf16[80,2048]{1,0:T(8,128)(2,1)S(1)}, u32[]{:S(2)}, u32[]{:S(2)}) collective-permute-start(bf16[80,2048]{1,0:T(8,128)(2,1)} %collective-permute-done.13), channel_id=1, source_target_pairs={{0,1},{1,2},{2,3},{3,4},{4,5},{5,6},{6,7},{7,8},{8,9},{9,10},{10,1... | collective-permute-start | bytes 983048 | tf_op jit(solution)/shard_map/ppermute | solution.py:134
  115.7 17.5 %copy-start.17 = (bf16[80,2048]{1,0:T(8,128)(2,1)S(1)}, bf16[80,2048]{1,0:T(8,128)(2,1)}, u32[]{:S(2)}) copy-start(bf16[80,2048]{1,0:T(8,128)(2,1)} %copy-done.16) | copy-start | bytes 983044
  129.1 4.4 %copy-start.15 = (bf16[80,2048]{1,0:T(8,128)(2,1)S(1)}, bf16[80,2048]{1,0:T(8,128)(2,1)}, u32[]{:S(2)}) copy-start(bf16[80,2048]{1,0:T(8,128)(2,1)} %copy-done.14) | copy-start | bytes 983044
  129.3 4.4 %copy-start.13 = (bf16[80,2048]{1,0:T(8,128)(2,1)S(1)}, bf16[80,2048]{1,0:T(8,128)(2,1)}, u32[]{:S(2)}) copy-start(bf16[80,2048]{1,0:T(8,128)(2,1)} %copy-done.12) | copy-start | bytes 983044
  130.6 3.3 %copy-start.11 = (bf16[80,2048]{1,0:T(8,128)(2,1)S(1)}, bf16[80,2048]{1,0:T(8,128)(2,1)}, u32[]{:S(2)}) copy-start(bf16[80,2048]{1,0:T(8,128)(2,1)} %copy-done.10) | copy-start | bytes 983044
  163.1 12.2 %all-to-all-start.2 = ((bf16[32,24,128]{2,1,0:T(8,128)(2,1)}), bf16[32,24,128]{2,1,0:T(8,128)(2,1)S(1)}, u32[]{:S(2)}, u32[]{:S(2)}) async-start(bf16[32,24,128]{2,1,0:T(8,128)(2,1)} %bitcast.41), calls=%async_computation.2 | async-start | bytes 393216 | tf_op jit(solution)/shard_map/all_to_all | solution.py:187
Sparse Core Ops, SparseCore 0:
  68.2 73.5 all-gather.1
where the time goes:
time: 184 us; the launch traced here: 183 us
  starting transfers between devices  70.6 us (38%)
  waiting for transfers between devices  34.9 us (19%)
  blocking collectives  24.7 us (13%)
  matrix products  22.4 us (12%)
  between operations  14.7 us (8%)
  Pallas kernels  8.87 us (5%)
  local copies, waits for them, and re-layouts  5.91 us (3%)
    ppermute x7, starting transfers between devices, ring_gather(): down = lax.ppermute(down, axis, left)  39.9 us
    all_to_all x1, blocking collectives, own_share(): arrived = lax.all_to_all(sent, 'seq', 0, 0, tiled=True)  24.7 us
    dot_general x17, matrix products, dot(): return jnp.dot(a, b, preferred_element_type=jnp.float32)  16.4 us
    ppermute x7, starting transfers between devices, ring_gather(): up = lax.ppermute(up, axis, right)  13.6 us
    ppermute x7, waiting for transfers between devices, ring_gather(): down = lax.ppermute(down, axis, left)  12.8 us
    ppermute x1, waiting for transfers between devices, ring_gather(): arrived[size // 2] = lax.ppermute(up, axis, right)  12.1 us
    all_to_all x1, starting transfers between devices, body(): lax.all_to_all(jnp.broadcast_to(state, (n_seq, head_dim, head_dim)), 'seq...  11.3 us
    all_to_all x1, waiting for transfers between devices, own_share(): arrived = lax.all_to_all(sent, 'seq', 0, 0, tiled=True)  8.36 us
  transfers between devices with their start and end apart: 18, of which 11 were waited for; matrix products, arithmetic and copies ran while one was open for 10% of the time, Pallas kernels for 5%

commit v1 on v0

--- a/solution.py
+++ b/solution.py
@@ -11,8 +11,7 @@
 HIGHEST = lax.Precision.HIGHEST
 PIECE = 512
 TILE = 128
-RING_ROWS = 40
-STREAMS = 1
+GROUP = 2
 
 
 def dot_t(a, b):
@@ -115,44 +114,132 @@
     )(*pieces, queries, coeff, hi, lo)
 
 
-def ring_gather(shard, axis, streams):
-    size = lax.axis_size(axis)
+def exchange(value):
+    size = lax.axis_size("zl")
+    own = lax.axis_index("zl")
+    rows = value.shape[0] // size
+    slots = [lax.dynamic_slice_in_dim(value, own * rows, rows, 0)]
+    for apart in range(1, size):
+        to = lax.rem(own + apart, size)
+        piece = lax.dynamic_slice_in_dim(value, to * rows, rows, 0)
+        slots.append(lax.ppermute(piece, "zl", [(i, (i + apart) % size) for i in range(size)]))
+    return slots
+
+
+def ring_gather(own):
+    size = lax.axis_size("zh")
     right = [(i, (i + 1) % size) for i in range(size)]
     left = [(i, (i - 1) % size) for i in range(size)]
-    rows = shard.shape[0] // streams
-    parts = []
-    for stream in range(streams):
-        own = shard[stream * rows : (stream + 1) * rows]
-        arrived = {0: own}
-        up, down = own, own
-        for step in range(1, size // 2):
-            up = lax.ppermute(up, axis, right)
-            down = lax.ppermute(down, axis, left)
-            arrived[size - step] = up
-            arrived[step] = down
-        if stream % 2 == 0:
-            arrived[size // 2] = lax.ppermute(up, axis, right)
-        else:
-            arrived[size // 2] = lax.ppermute(down, axis, left)
-        parts.append([arrived[k] for k in range(size)])
-    return parts
+    half = own.shape[0] // 2
+    arrived = []
+    up, down = own, own
+    for step in range(1, size // 2):
+        up = lax.ppermute(up, "zh", right)
+        down = lax.ppermute(down, "zh", left)
+        arrived += [(size - step, 0, up), (step, 0, down)]
+    arrived.append((size // 2, 0, lax.ppermute(up[:half], "zh", right)))
+    arrived.append((size // 2, half, lax.ppermute(down[half:], "zh", left)))
+    return arrived
+
+
+def product_store(place, count, blocks, zh, zl, a_refs, b_refs, store):
+    b = jnp.concatenate([ref[...] for ref in b_refs], axis=1)
+    for (away, first, slots), a_ref in zip(blocks, a_refs):
+        group = lax.rem(zh + away, count)
+        for slot in range(slots):
+            a = a_ref[slot]
+            product = lax.dot_general(
+                a, b, (((0,), (0,)), ((), ())), preferred_element_type=jnp.float32
+            ).astype(jnp.bfloat16)
+            block = group * place + lax.rem(zl - (first + slot) + place, place)
+            store(block, product)
+
+
+def early_kernel(place, count, blocks, where_ref, *refs):
+    b_refs, a_refs, out_ref = refs[:place], refs[place:-1], refs[-1]
+    done = [0]
+
+    def store(block, product):
+        out_ref[done[0]] = product
+        done[0] += 1
+
+    product_store(place, count, blocks, where_ref[0], where_ref[1], a_refs, b_refs, store)
+
+
+def late_kernel(place, count, early_blocks, blocks, where_ref, early_ref, *refs):
+    b_refs, a_refs, out_ref = refs[:place], refs[place:-1], refs[-1]
+    zh, zl = where_ref[0], where_ref[1]
+    width = out_ref.shape[-1]
+    rows = out_ref.shape[-2]
+
+    def store(block, product):
+        for half in range(2):
+            for d in range(place):
+                head = lax.rem(zl - d + place, place)
+                out_ref[block, half, head] = product[
+                    half * rows : (half + 1) * rows, d * width : (d + 1) * width
+                ]
+
+    done = 0
+    for away, first, slots in early_blocks:
+        group = lax.rem(zh + away, count)
+        for slot in range(slots):
+            block = group * place + lax.rem(zl - (first + slot) + place, place)
+            store(block, early_ref[done])
+            done += 1
+    product_store(place, count, blocks, zh, zl, a_refs, b_refs, store)
+
+
+def product_cost(blocks, shape, place):
+    count = sum(slots for _, _, slots in blocks)
+    rows, width = shape
+    return pl.CostEstimate(
+        flops=2 * count * rows * width * width * place,
+        bytes_accessed=2 * rows * width * (count + place),
+        transcendentals=0,
+    )
+
+
+def products(early, late, b_slots, zh_count):
+    place = len(b_slots)
+    rows, width = b_slots[0].shape
+    where = jnp.stack([lax.axis_index("zh"), lax.axis_index("zl")]).astype(jnp.int32)
+    early_blocks = [(away, first, a.shape[0]) for away, first, a in early]
+    late_blocks = [(away, first, a.shape[0]) for away, first, a in late]
+    count = sum(slots for _, _, slots in early_blocks)
+    smem = pl.BlockSpec(memory_space=pltpu.SMEM)
+    vmem = pl.BlockSpec(memory_space=pltpu.VMEM)
+    params = pltpu.CompilerParams(vmem_limit_bytes=40 * 1024 * 1024)
+    first = pl.pallas_call(
+        functools.partial(early_kernel, place, zh_count, early_blocks),
+        out_shape=jax.ShapeDtypeStruct((count, width, place * width), jnp.bfloat16),
+        in_specs=[smem] + [vmem] * (place + len(early)),
+        out_specs=vmem,
+        compiler_params=params,
+        cost_estimate=product_cost(early_blocks, (rows, width), place),
+    )(where, *b_slots, *[a for _, _, a in early])
+    return pl.pallas_call(
+        functools.partial(late_kernel, place, zh_count, early_blocks, late_blocks),
+        out_shape=jax.ShapeDtypeStruct(
+            (zh_count * place, 2, place, width // 2, width), jnp.bfloat16
+        ),
+        in_specs=[smem] + [vmem] * (1 + place + len(late)),
+        out_specs=vmem,
+        compiler_params=params,
+        cost_estimate=product_cost(late_blocks, (rows, width), place),
+    )(where, first, *b_slots, *[a for _, _, a in late])
 
 
 def body(queries, keys, values, level_ids, level_table, out_cotangent):
     block_len, head_dim = queries.shape
     n_seq = lax.axis_size("seq")
-    n_head = lax.axis_size("head")
     local_bits = block_len.bit_length() - 1
     seq_bits = n_seq.bit_length() - 1
     table_rows = level_table.shape[0]
     own_index = lax.axis_index("seq")
-    own_head = lax.axis_index("head")
-
-    cot = out_cotangent.T.reshape(2, head_dim // 2, block_len)
-    ring_part = cot[:, :RING_ROWS].reshape(2 * RING_ROWS, block_len)
-    gather_part = cot[:, RING_ROWS:].reshape(head_dim - 2 * RING_ROWS, block_len)
-    gathered = lax.all_gather(gather_part, "head", axis=0)
-    ring = ring_gather(ring_part, "head", STREAMS)
+
+    own = jnp.stack(exchange(out_cotangent))
+    blocks = [(0, 0, own)] + ring_gather(own)
 
     state = lax.dot_general(
         keys, values, (((0,), (0,)), ((), ())), preferred_element_type=jnp.float32
@@ -180,33 +267,24 @@
     attn_out = finish(pieces, queries, coeff, level_states, local_bits + 1)
 
     scale = (block_len * n_seq) ** (-0.5)
-
-    def own_share(products):
-        rows = products.shape[2]
-        sent = products.reshape(n_seq, rows, head_dim).astype(jnp.bfloat16)
-        arrived = lax.all_to_all(sent, "seq", 0, 0, tiled=True)
-        return arrived.astype(jnp.float32).sum(axis=0) * scale
-
-    streams = []
-    for parts in ring:
-        products = jnp.stack([dot(part, attn_out) for part in parts])
-        doubled = jnp.concatenate([products, products], axis=0).astype(jnp.bfloat16)
-        streams.append(lax.dynamic_slice_in_dim(doubled, n_head - own_head, n_head, 0))
-    products = jnp.concatenate(streams, axis=1).reshape(n_head, 2, RING_ROWS, head_dim)
-    upper = own_share(products)
-    rest = dot(gathered.reshape(-1, block_len), attn_out)
-    lower = own_share(rest.reshape(n_head, 2, head_dim // 2 - RING_ROWS, head_dim))
-    return attn_out, jnp.concatenate([upper, lower], axis=0)
+    late = 4
+    partial = products(blocks[:-late], blocks[-late:], exchange(attn_out), lax.axis_size("zh"))
+    sent = partial.reshape(-1, head_dim // 2, head_dim)
+    arrived = lax.all_to_all(sent, ("seq", "zl"), 0, 0, tiled=True)
+    weight_grad = arrived.astype(jnp.float32).sum(axis=0) * scale
+    return attn_out, weight_grad
 
 
 def solution(mesh):
-    in_specs = (
-        P("seq", "head"),
-        P("seq", "head"),
-        P("seq", "head"),
-        P("seq"),
-        P(),
-        P("seq", "head"),
-    )
-    out_specs = (P("seq", "head"), P("seq", "head"))
-    return jax.shard_map(body, mesh=mesh, in_specs=in_specs, out_specs=out_specs, check_vma=False)
+    n_seq, n_head = mesh.devices.shape
+    mesh = jax.sharding.Mesh(
+        mesh.devices.reshape(n_seq, n_head // GROUP, GROUP), ("seq", "zh", "zl")
+    )
+    split = P("seq", ("zh", "zl"))
+    return jax.shard_map(
+        body,
+        mesh=mesh,
+        in_specs=(split, split, split, P("seq"), P(), split),
+        out_specs=(split, split),
+        check_vma=False,
+    )

time: 184 us -> 159 us (0.86)
  matrix products: 22.4 us -> 6.01 us
  starting transfers between devices: 70.6 us -> 54.6 us
  waiting for transfers between devices: 34.9 us -> 50.8 us
  between operations: 14.7 us -> 1.03 us
  blocking collectives: 24.7 us -> 28.5 us
  Pallas kernels: 8.87 us -> 12.5 us
  local copies, waits for them, and re-layouts: 5.91 us -> 3.54 us
    ppermute x15 -> x10, waiting for transfers between devices: 26.5 us -> 50.8 us  [the longest x3 25.5 us: ring_gather(): up = lax.ppermute(up, 'zh', right)]
    dot_general x17 -> x0, matrix products: 16.4 us -> none  [dot(): return jnp.dot(a, b, preferred_element_type=jnp.float32)]
    ppermute x15 -> x10, starting transfers between devices: 55.4 us -> 43.2 us  [the longest x3 20.3 us: ring_gather(): down = lax.ppermute(down, 'zh', left)]
    all_to_all x1 -> x0, waiting for transfers between devices: 8.36 us -> none  [own_share(): arrived = lax.all_to_all(sent, 'seq', 0, 0, tiled=True)]
    all_to_all x1, blocking collectives: 24.7 us -> 28.5 us  [body(): arrived = lax.all_to_all(sent, ('seq', 'zl'), 0, 0, tiled=True)]
    all_to_all x1 -> x0, starting transfers between devices: 3.81 us -> none  [own_share(): arrived = lax.all_to_all(sent, 'seq', 0, 0, tiled=True)]
    pallas_call x0 -> x2, Pallas kernels: none -> 3.66 us  [the longest x1 2.43 us: products(): pl.pallas_call(functools.partial(early_kernel, place, zh_count, early_blo...]
    unnamed x70 -> x24, local copies, waits for them, and re-layouts: 2.66 us -> 0.76 us
  transfers between devices with their start and end apart: 18 -> 11, of which waited for: 11 -> 9; matrix products, arithmetic and copies ran while one was open for 10% -> 4% of each run, Pallas kernels for 5% -> 7%
where the time goes in v1:
time: 159 us; the launch traced here: 158 us
  starting transfers between devices  54.6 us (34%)
  waiting for transfers between devices  50.8 us (32%)
  blocking collectives  28.5 us (18%)
  Pallas kernels  12.5 us (8%)
  matrix products  6.01 us (4%)
  local copies, waits for them, and re-layouts  3.54 us (2%)
    all_to_all x1, blocking collectives, body(): arrived = lax.all_to_all(sent, ('seq', 'zl'), 0, 0, tiled=True)  28.5 us
    ppermute x3, waiting for transfers between devices, ring_gather(): up = lax.ppermute(up, 'zh', right)  25.5 us
    ppermute x3, starting transfers between devices, ring_gather(): down = lax.ppermute(down, 'zh', left)  20.3 us
    ppermute x3, starting transfers between devices, ring_gather(): up = lax.ppermute(up, 'zh', right)  11.5 us
    all_to_all x1, starting transfers between devices, body(): lax.all_to_all(jnp.broadcast_to(state, (n_seq, head_dim, head_dim)), 'seq...  11.3 us
    ppermute x3, waiting for transfers between devices, ring_gather(): down = lax.ppermute(down, 'zh', left)  9.95 us
    ppermute x2, waiting for transfers between devices, exchange(): lax.ppermute(piece, 'zl', [(i, (i + apart) % size) for i in range(size)])  9.19 us
    ppermute x1, waiting for transfers between devices, ring_gather(): arrived.append((size // 2, 0, lax.ppermute(up[:half], 'zh', right)))  6.21 us
  transfers between devices with their start and end apart: 11, of which 9 were waited for; matrix products, arithmetic and copies ran while one was open for 4% of the time, Pallas kernels for 7%

profile of v1, /device:TPU:1, one launch (start us, length us, event | category | flops | bytes accessed | tf_op | source)
XLA Modules:
  0.0 158.0 jit_solution(15848243063305080380)
XLA Ops:
  0.6 0.0 copy-start
  0.6 1.5 fusion.5
  2.2 1.5 broadcast_in_dim.2
  3.7 11.3 %all-to-all-start = ((f32[32,128,128]{2,1,0:T(8,128)}), f32[32,128,128]{2,1,0:T(8,128)}, u32[]{:S(2)}, u32[]{:S(2)}) async-start(f32[32,128,128]{2,1,0:T(8,128)} %broadcast_in_dim.2), calls=%async_computation | async-start | bytes 4194304 | tf_op jit(solution)/shard_map/all_to_all | solution.py:247
  15.1 0.0 copy-start.11
  15.1 0.0 copy-start.1
  15.1 0.0 copy-start.2
  15.1 0.0 copy-start.3
  15.2 0.0 copy-done.10
  15.2 2.1 %collective-permute-start.1 = (bf16[1024,128]{1,0:T(8,128)(2,1)S(1)}, bf16[1024,128]{1,0:T(8,128)(2,1)S(1)}, u32[]{:S(2)}, u32[]{:S(2)}) collective-permute-start(bf16[1024,128]{1,0:T(8,128)(2,1)S(1)} %get-tuple-element.3), channel_id=1, source_target_pairs={{0,1},{1,0},{2,3},{3,2},{4,5},{5,4},{6,7},{7,6},{8,9},{9,8},{10,11... | collective-permute-start | bytes 786440 | tf_op jit(solution)/shard_map/ppermute | solution.py:125
  17.3 7.5 %collective-permute-done.1 = bf16[1024,128]{1,0:T(8,128)(2,1)S(1)} collective-permute-done((bf16[1024,128]{1,0:T(8,128)(2,1)S(1)}, bf16[1024,128]{1,0:T(8,128)(2,1)S(1)}, u32[]{:S(2)}, u32[]{:S(2)}) %collective-permute-start.1) | collective-permute-done | bytes 262176 | tf_op jit(solution)/shard_map/ppermute | solution.py:125
  24.8 0.1 pad_maximum_fusion.refs_2_
  24.9 2.9 %collective-permute-start.2 = (bf16[2,1024,128]{2,1,0:T(8,128)(2,1)S(1)}, bf16[2,1024,128]{2,1,0:T(8,128)(2,1)}, u32[]{:S(2)}, u32[]{:S(2)}) collective-permute-start(bf16[2,1024,128]{2,1,0:T(8,128)(2,1)S(1)} %pad_maximum_fusion.refs_2_), channel_id=1, source_target_pairs={{0,2},{2,4},{4,6},{6,8},{8,10},{10,12},{12,14},{14,0},{1,3},{3,5},... | collective-permute-start | bytes 1572872 | tf_op jit(solution)/shard_map/ppermute | solution.py:137
  27.7 8.2 %collective-permute-start.3 = (bf16[2,1024,128]{2,1,0:T(8,128)(2,1)S(1)}, bf16[2,1024,128]{2,1,0:T(8,128)(2,1)}, u32[]{:S(2)}, u32[]{:S(2)}) collective-permute-start(bf16[2,1024,128]{2,1,0:T(8,128)(2,1)S(1)} %pad_maximum_fusion.refs_2_), channel_id=1, source_target_pairs={{0,14},{2,0},{4,2},{6,4},{8,6},{10,8},{12,10},{14,12},{1,15},{3,1}... | collective-permute-start | bytes 1572872 | tf_op jit(solution)/shard_map/ppermute | solution.py:138
  35.9 12.6 %collective-permute-done.2.refs_3_ = bf16[2,1024,128]{2,1,0:T(8,128)(2,1)} collective-permute-done((bf16[2,1024,128]{2,1,0:T(8,128)(2,1)S(1)}, bf16[2,1024,128]{2,1,0:T(8,128)(2,1)}, u32[]{:S(2)}, u32[]{:S(2)}) %collective-permute-start.2) | collective-permute-done | bytes 524320 | tf_op jit(solution)/shard_map/ppermute | solution.py:137
  48.5 6.8 %collective-permute-start.4 = (bf16[2,1024,128]{2,1,0:T(8,128)(2,1)}, bf16[2,1024,128]{2,1,0:T(8,128)(2,1)}, u32[]{:S(2)}, u32[]{:S(2)}) collective-permute-start(bf16[2,1024,128]{2,1,0:T(8,128)(2,1)} %collective-permute-done.2.refs_3_), channel_id=1, source_target_pairs={{0,2},{2,4},{4,6},{6,8},{8,10},{10,12},{12,14},{14,0},{1,3},{3,5},... | collective-permute-start | bytes 1572872 | tf_op jit(solution)/shard_map/ppermute | solution.py:137
  55.3 1.4 collective-permute-done.3.refs_4_
  56.6 6.1 %collective-permute-start.5 = (bf16[2,1024,128]{2,1,0:T(8,128)(2,1)}, bf16[2,1024,128]{2,1,0:T(8,128)(2,1)}, u32[]{:S(2)}, u32[]{:S(2)}) collective-permute-start(bf16[2,1024,128]{2,1,0:T(8,128)(2,1)} %collective-permute-done.3.refs_4_), channel_id=1, source_target_pairs={{0,14},{2,0},{4,2},{6,4},{8,6},{10,8},{12,10},{14,12},{1,15},{3,1}... | collective-permute-start | bytes 1572872 | tf_op jit(solution)/shard_map/ppermute | solution.py:138
  62.8 0.0 copy-done
  62.8 0.0 copy-done.11
  62.8 1.0 fusion.2.c_ref
  63.8 0.0 copy-done.1
  63.8 0.0 copy-done.2
  63.8 0.0 copy-done.3
  63.8 1.1 shard_map.77.l0
  65.0 1.2 shard_map.78.l1
  66.2 0.0 copy-start.4
  66.2 1.6 %shard_map.79.l2 = f32[512,128]{1,0:T(8,128)S(1)} custom-call(bf16[2048,128]{1,0:T(8,128)(2,1)S(1)} %copy-done.3, bf16[2048,128]{1,0:T(8,128)(2,1)S(1)} %copy-done.1, bf16[2048,128]{1,0:T(8,128)(2,1)S(1)} %copy-done.2, f32[2048,17]{1,0:T(8,128)S(1)} %fusion.2.c_ref), custom_call_target="tpu_custom_call" | custom-call | flops 402653184 | bytes 786432 | tf_op jit(solution)/shard_map/pallas_call | solution.py:70
  67.8 0.0 copy-start.6
  67.8 1.9 %shard_map.80.l3 = f32[512,128]{1,0:T(8,128)S(1)} custom-call(bf16[2048,128]{1,0:T(8,128)(2,1)S(1)} %copy-done.3, bf16[2048,128]{1,0:T(8,128)(2,1)S(1)} %copy-done.1, bf16[2048,128]{1,0:T(8,128)(2,1)S(1)} %copy-done.2, f32[2048,17]{1,0:T(8,128)S(1)} %fusion.2.c_ref), custom_call_target="tpu_custom_call" | custom-call | flops 536870912 | bytes 1048576 | tf_op jit(solution)/shard_map/pallas_call | solution.py:70
  69.8 0.0 copy-done.4
  69.8 0.0 copy-start.8
  69.8 0.7 copy-done.8
  70.5 4.8 %collective-permute-done.4.refs_5_ = bf16[2,1024,128]{2,1,0:T(8,128)(2,1)} collective-permute-done((bf16[2,1024,128]{2,1,0:T(8,128)(2,1)}, bf16[2,1024,128]{2,1,0:T(8,128)(2,1)}, u32[]{:S(2)}, u32[]{:S(2)}) %collective-permute-start.4) | collective-permute-done | bytes 524320 | tf_op jit(solution)/shard_map/ppermute | solution.py:137
  75.3 1.9 %collective-permute-start.6 = (bf16[2,1024,128]{2,1,0:T(8,128)(2,1)}, bf16[2,1024,128]{2,1,0:T(8,128)(2,1)S(1)}, u32[]{:S(2)}, u32[]{:S(2)}) collective-permute-start(bf16[2,1024,128]{2,1,0:T(8,128)(2,1)} %collective-permute-done.4.refs_5_), channel_id=1, source_target_pairs={{0,2},{2,4},{4,6},{6,8},{8,10},{10,12},{12,14},{14,0},{1,3},{3,5},... | collective-permute-start | bytes 1572872 | tf_op jit(solution)/shard_map/ppermute | solution.py:137
  77.2 0.0 copy-done.6
  77.2 6.7 %collective-permute-done.5.refs_6_ = bf16[2,1024,128]{2,1,0:T(8,128)(2,1)} collective-permute-done((bf16[2,1024,128]{2,1,0:T(8,128)(2,1)}, bf16[2,1024,128]{2,1,0:T(8,128)(2,1)}, u32[]{:S(2)}, u32[]{:S(2)}) %collective-permute-start.5) | collective-permute-done | bytes 524320 | tf_op jit(solution)/shard_map/ppermute | solution.py:138
  84.0 5.9 %collective-permute-start.7 = (bf16[2,1024,128]{2,1,0:T(8,128)(2,1)}, bf16[2,1024,128]{2,1,0:T(8,128)(2,1)S(1)}, u32[]{:S(2)}, u32[]{:S(2)}) collective-permute-start(bf16[2,1024,128]{2,1,0:T(8,128)(2,1)} %collective-permute-done.5.refs_6_), channel_id=1, source_target_pairs={{0,14},{2,0},{4,2},{6,4},{8,6},{10,8},{12,10},{14,12},{1,15},{3,1}... | collective-permute-start | bytes 1572872 | tf_op jit(solution)/shard_map/ppermute | solution.py:138
  89.9 0.0 all-to-all-done
  89.9 0.0 copy-start.5
  89.9 0.0 copy-start.7
  90.0 0.0 copy-start.9
  90.0 3.5 %fusion = f32[5,128,128]{2,0,1:T(8,128)S(1)} fusion(f32[32,128,128]{2,1,0:T(8,128)} %all-to-all-done, pred[5,32]{1,0:T(8,128)(4,1)S(1)} %stack.29), kind=kOutput, calls=%fused_computation | convolution fusion | flops 31457280 | bytes 2424992 | tf_op jit(solution)/shard_map/ji,ide->jde/dot_general | solution.py:258
  93.5 0.1 copy.30.hi_ref
  93.5 0.1 subtract_convert_fusion.lo_ref
  93.6 0.0 copy-done.5
  93.6 0.0 copy-done.7
  93.6 0.0 copy-done.9
  93.7 3.0 %shard_map.81 = bf16[2048,128]{1,0:T(8,128)(2,1)} custom-call(f32[512,128]{1,0:T(8,128)S(1)} %shard_map.77.l0, f32[512,128]{1,0:T(8,128)S(1)} %copy-done.5, f32[512,128]{1,0:T(8,128)S(1)} %copy-done.7, f32[512,128]{1,0:T(8,128)S(1)} %copy-done.9, bf16[2048,128]{1,0:T(8,128)(2,1)S(1)} %copy-done.3, f32[2048,17]{1,0:T(8,128)S(1)} %fusion.2.c_ref, ...), custom_call_target="tpu_custom_call" | custom-call | flops 671088640 | bytes 4194304 | tf_op jit(solution)/shard_map/pallas_call | solution.py:107
  96.6 1.1 constant_dynamic-slice_fusion.1
  97.7 3.4 %collective-permute-start = (bf16[1024,128]{1,0:T(8,128)(2,1)S(1)}, bf16[1024,128]{1,0:T(8,128)(2,1)S(1)}, u32[]{:S(2)}, u32[]{:S(2)}) collective-permute-start(bf16[1024,128]{1,0:T(8,128)(2,1)S(1)} %get-tuple-element.4), channel_id=1, source_target_pairs={{0,1},{1,0},{2,3},{3,2},{4,5},{5,4},{6,7},{7,6},{8,9},{9,8},{10,11... | collective-permute-start | bytes 786440 | tf_op jit(solution)/shard_map/ppermute | solution.py:125
  101.1 8.0 %collective-permute-done.6.refs_2_ = bf16[2,1024,128]{2,1,0:T(8,128)(2,1)S(1)} collective-permute-done((bf16[2,1024,128]{2,1,0:T(8,128)(2,1)}, bf16[2,1024,128]{2,1,0:T(8,128)(2,1)S(1)}, u32[]{:S(2)}, u32[]{:S(2)}) %collective-permute-start.6) | collective-permute-done | bytes 524320 | tf_op jit(solution)/shard_map/ppermute | solution.py:137
  109.2 1.9 %collective-permute-start.8 = (bf16[1,1024,128]{2,1,0:T(8,128)(2,1)S(1)}, bf16[1,1024,128]{2,1,0:T(8,128)(2,1)S(1)}, u32[]{:S(2)}, u32[]{:S(2)}) collective-permute-start(bf16[1,1024,128]{2,1,0:T(8,128)(2,1)S(1)} %slice.8), channel_id=1, source_target_pairs={{0,2},{2,4},{4,6},{6,8},{8,10},{10,12},{12,14},{14,0},{1,3},{3,5},... | collective-permute-start | bytes 786440 | tf_op jit(solution)/shard_map/ppermute | solution.py:140
  111.1 1.8 %collective-permute-done.7.refs_3_ = bf16[2,1024,128]{2,1,0:T(8,128)(2,1)S(1)} collective-permute-done((bf16[2,1024,128]{2,1,0:T(8,128)(2,1)}, bf16[2,1024,128]{2,1,0:T(8,128)(2,1)S(1)}, u32[]{:S(2)}, u32[]{:S(2)}) %collective-permute-start.7) | collective-permute-done | bytes 524320 | tf_op jit(solution)/shard_map/ppermute | solution.py:138
  113.0 4.1 %collective-permute-start.9 = (bf16[1,1024,128]{2,1,0:T(8,128)(2,1)S(1)}, bf16[1,1024,128]{2,1,0:T(8,128)(2,1)S(1)}, u32[]{:S(2)}, u32[]{:S(2)}) collective-permute-start(bf16[1,1024,128]{2,1,0:T(8,128)(2,1)S(1)} %slice.9), channel_id=1, source_target_pairs={{0,14},{2,0},{4,2},{6,4},{8,6},{10,8},{12,10},{14,12},{1,15},{3,1}... | collective-permute-start | bytes 786440 | tf_op jit(solution)/shard_map/ppermute | solution.py:141
  117.1 0.1 pad_add_fusion.where_ref
  117.2 1.7 %collective-permute-done.refs_1_ = bf16[1024,128]{1,0:T(8,128)(2,1)S(1)} collective-permute-done((bf16[1024,128]{1,0:T(8,128)(2,1)S(1)}, bf16[1024,128]{1,0:T(8,128)(2,1)S(1)}, u32[]{:S(2)}, u32[]{:S(2)}) %collective-permute-start) | collective-permute-done | bytes 262176 | tf_op jit(solution)/shard_map/ppermute | solution.py:125
  118.8 2.4 %shard_map.82.early_ref = bf16[10,128,256]{2,1,0:T(8,128)(2,1)S(1)} custom-call(s32[2]{0:T(128)S(1)} %pad_add_fusion.where_ref, bf16[1024,128]{1,0:T(8,128)(2,1)S(1)} %get-tuple-element.5.refs_0_, bf16[1024,128]{1,0:T(8,128)(2,1)S(1)} %collective-permute-done.refs_1_, bf16[2,1024,128]{2,1,0:T(8,128)(2,1)S(1)} %pad_maximum_fusion.refs_2_, ...), custom_call_target="tpu_custom_call" | custom-call | flops 671088640 | bytes 3145728 | tf_op jit(solution)/shard_map/pallas_call | solution.py:213
  121.3 6.2 %collective-permute-done.8.refs_4_ = bf16[1,1024,128]{2,1,0:T(8,128)(2,1)S(1)} collective-permute-done((bf16[1,1024,128]{2,1,0:T(8,128)(2,1)S(1)}, bf16[1,1024,128]{2,1,0:T(8,128)(2,1)S(1)}, u32[]{:S(2)}, u32[]{:S(2)}) %collective-permute-start.8) | collective-permute-done | bytes 262176 | tf_op jit(solution)/shard_map/ppermute | solution.py:140
  127.5 0.0 collective-permute-done.9.refs_5_
  127.5 1.2 shard_map.83
  128.7 28.5 %all_to_all.10 = bf16[64,64,128]{2,1,0:T(8,128)(2,1)S(1)} all-to-all(bf16[64,64,128]{2,1,0:T(8,128)(2,1)S(1)} %bitcast.12), channel_id=1, replica_groups=mesh['seq'=32,'zh'=8,'zl'=2] {'seq','zl'}, dimensions={0} | all-to-all | bytes 2097152 | tf_op jit(solution)/shard_map/all_to_all | solution.py:273
  157.2 0.2 convert_reduce_fusion
  157.4 0.6 broadcast_multiply_fusion
  (8 shorter events, 0.1 us)
Async XLA Ops:
  0.6 62.2 %copy-start = (f32[64,17]{0,1:T(8,128)S(1)}, f32[64,17]{0,1:T(8,128)}, u32[]{:S(2)}) copy-start(f32[64,17]{0,1:T(8,128)} %param.10) | copy-start | bytes 13060
  3.7 11.4 %copy-start.10 = (bf16[2048,128]{1,0:T(8,128)(2,1)S(1)}, bf16[2048,128]{1,0:T(8,128)(2,1)}, u32[]{:S(2)}) copy-start(bf16[2048,128]{1,0:T(8,128)(2,1)} %param.11) | copy-start | bytes 1572868
  3.7 86.2 %all-to-all-start = ((f32[32,128,128]{2,1,0:T(8,128)}), f32[32,128,128]{2,1,0:T(8,128)}, u32[]{:S(2)}, u32[]{:S(2)}) async-start(f32[32,128,128]{2,1,0:T(8,128)} %broadcast_in_dim.2), calls=%async_computation | async-start | bytes 4194304 | tf_op jit(solution)/shard_map/all_to_all | solution.py:247
  15.1 47.7 %copy-start.11 = (s32[2048]{0:T(1024)S(1)}, s32[2048]{0:T(1024)}, u32[]{:S(2)}) copy-start(s32[2048]{0:T(1024)} %param.9) | copy-start | bytes 24580
  15.1 48.7 %copy-start.1 = (bf16[2048,128]{1,0:T(8,128)(2,1)S(1)}, bf16[2048,128]{1,0:T(8,128)(2,1)}, u32[]{:S(2)}) copy-start(bf16[2048,128]{1,0:T(8,128)(2,1)} %k_ref.7) | copy-start | bytes 1572868
  15.1 48.7 %copy-start.2 = (bf16[2048,128]{1,0:T(8,128)(2,1)S(1)}, bf16[2048,128]{1,0:T(8,128)(2,1)}, u32[]{:S(2)}) copy-start(bf16[2048,128]{1,0:T(8,128)(2,1)} %v_ref.7) | copy-start | bytes 1572868
  15.1 48.7 %copy-start.3 = (bf16[2048,128]{1,0:T(8,128)(2,1)S(1)}, bf16[2048,128]{1,0:T(8,128)(2,1)}, u32[]{:S(2)}) copy-start(bf16[2048,128]{1,0:T(8,128)(2,1)} %q_ref.9) | copy-start | bytes 1572868
  15.2 9.6 %collective-permute-start.1 = (bf16[1024,128]{1,0:T(8,128)(2,1)S(1)}, bf16[1024,128]{1,0:T(8,128)(2,1)S(1)}, u32[]{:S(2)}, u32[]{:S(2)}) collective-permute-start(bf16[1024,128]{1,0:T(8,128)(2,1)S(1)} %get-tuple-element.3), channel_id=1, source_target_pairs={{0,1},{1,0},{2,3},{3,2},{4,5},{5,4},{6,7},{7,6},{8,9},{9,8},{10,11... | collective-permute-start | bytes 786440 | tf_op jit(solution)/shard_map/ppermute | solution.py:125
  24.9 23.7 %collective-permute-start.2 = (bf16[2,1024,128]{2,1,0:T(8,128)(2,1)S(1)}, bf16[2,1024,128]{2,1,0:T(8,128)(2,1)}, u32[]{:S(2)}, u32[]{:S(2)}) collective-permute-start(bf16[2,1024,128]{2,1,0:T(8,128)(2,1)S(1)} %pad_maximum_fusion.refs_2_), channel_id=1, source_target_pairs={{0,2},{2,4},{4,6},{6,8},{8,10},{10,12},{12,14},{14,0},{1,3},{3,5},... | collective-permute-start | bytes 1572872 | tf_op jit(solution)/shard_map/ppermute | solution.py:137
  27.7 28.9 %collective-permute-start.3 = (bf16[2,1024,128]{2,1,0:T(8,128)(2,1)S(1)}, bf16[2,1024,128]{2,1,0:T(8,128)(2,1)}, u32[]{:S(2)}, u32[]{:S(2)}) collective-permute-start(bf16[2,1024,128]{2,1,0:T(8,128)(2,1)S(1)} %pad_maximum_fusion.refs_2_), channel_id=1, source_target_pairs={{0,14},{2,0},{4,2},{6,4},{8,6},{10,8},{12,10},{14,12},{1,15},{3,1}... | collective-permute-start | bytes 1572872 | tf_op jit(solution)/shard_map/ppermute | solution.py:138
  48.5 26.8 %collective-permute-start.4 = (bf16[2,1024,128]{2,1,0:T(8,128)(2,1)}, bf16[2,1024,128]{2,1,0:T(8,128)(2,1)}, u32[]{:S(2)}, u32[]{:S(2)}) collective-permute-start(bf16[2,1024,128]{2,1,0:T(8,128)(2,1)} %collective-permute-done.2.refs_3_), channel_id=1, source_target_pairs={{0,2},{2,4},{4,6},{6,8},{8,10},{10,12},{12,14},{14,0},{1,3},{3,5},... | collective-permute-start | bytes 1572872 | tf_op jit(solution)/shard_map/ppermute | solution.py:137
  56.6 27.3 %collective-permute-start.5 = (bf16[2,1024,128]{2,1,0:T(8,128)(2,1)}, bf16[2,1024,128]{2,1,0:T(8,128)(2,1)}, u32[]{:S(2)}, u32[]{:S(2)}) collective-permute-start(bf16[2,1024,128]{2,1,0:T(8,128)(2,1)} %collective-permute-done.3.refs_4_), channel_id=1, source_target_pairs={{0,14},{2,0},{4,2},{6,4},{8,6},{10,8},{12,10},{14,12},{1,15},{3,1}... | collective-permute-start | bytes 1572872 | tf_op jit(solution)/shard_map/ppermute | solution.py:138
  66.2 3.6 %copy-start.4 = (f32[512,128]{1,0:T(8,128)}, f32[512,128]{1,0:T(8,128)S(1)}, u32[]{:S(2)}) copy-start(f32[512,128]{1,0:T(8,128)S(1)} %shard_map.78.l1) | copy-start | bytes 786436
  67.8 9.4 %copy-start.6 = (f32[512,128]{1,0:T(8,128)}, f32[512,128]{1,0:T(8,128)S(1)}, u32[]{:S(2)}) copy-start(f32[512,128]{1,0:T(8,128)S(1)} %shard_map.79.l2) | copy-start | bytes 786436
  69.8 0.7 copy-start.8
  75.3 33.9 %collective-permute-start.6 = (bf16[2,1024,128]{2,1,0:T(8,128)(2,1)}, bf16[2,1024,128]{2,1,0:T(8,128)(2,1)S(1)}, u32[]{:S(2)}, u32[]{:S(2)}) collective-permute-start(bf16[2,1024,128]{2,1,0:T(8,128)(2,1)} %collective-permute-done.4.refs_5_), channel_id=1, source_target_pairs={{0,2},{2,4},{4,6},{6,8},{8,10},{10,12},{12,14},{14,0},{1,3},{3,5},... | collective-permute-start | bytes 1572872 | tf_op jit(solution)/shard_map/ppermute | solution.py:137
  84.0 29.0 %collective-permute-start.7 = (bf16[2,1024,128]{2,1,0:T(8,128)(2,1)}, bf16[2,1024,128]{2,1,0:T(8,128)(2,1)S(1)}, u32[]{:S(2)}, u32[]{:S(2)}) collective-permute-start(bf16[2,1024,128]{2,1,0:T(8,128)(2,1)} %collective-permute-done.5.refs_6_), channel_id=1, source_target_pairs={{0,14},{2,0},{4,2},{6,4},{8,6},{10,8},{12,10},{14,12},{1,15},{3,1}... | collective-permute-start | bytes 1572872 | tf_op jit(solution)/shard_map/ppermute | solution.py:138
  89.9 3.7 %copy-start.5 = (f32[512,128]{1,0:T(8,128)S(1)}, f32[512,128]{1,0:T(8,128)}, u32[]{:S(2)}) copy-start(f32[512,128]{1,0:T(8,128)} %copy-done.4) | copy-start | bytes 786436
  89.9 3.7 %copy-start.7 = (f32[512,128]{1,0:T(8,128)S(1)}, f32[512,128]{1,0:T(8,128)}, u32[]{:S(2)}) copy-start(f32[512,128]{1,0:T(8,128)} %copy-done.6) | copy-start | bytes 786436
  90.0 3.7 %copy-start.9 = (f32[512,128]{1,0:T(8,128)S(1)}, f32[512,128]{1,0:T(8,128)}, u32[]{:S(2)}) copy-start(f32[512,128]{1,0:T(8,128)} %copy-done.8) | copy-start | bytes 786436
  97.7 21.1 %collective-permute-start = (bf16[1024,128]{1,0:T(8,128)(2,1)S(1)}, bf16[1024,128]{1,0:T(8,128)(2,1)S(1)}, u32[]{:S(2)}, u32[]{:S(2)}) collective-permute-start(bf16[1024,128]{1,0:T(8,128)(2,1)S(1)} %get-tuple-element.4), channel_id=1, source_target_pairs={{0,1},{1,0},{2,3},{3,2},{4,5},{5,4},{6,7},{7,6},{8,9},{9,8},{10,11... | collective-permute-start | bytes 786440 | tf_op jit(solution)/shard_map/ppermute | solution.py:125
  109.2 18.3 %collective-permute-start.8 = (bf16[1,1024,128]{2,1,0:T(8,128)(2,1)S(1)}, bf16[1,1024,128]{2,1,0:T(8,128)(2,1)S(1)}, u32[]{:S(2)}, u32[]{:S(2)}) collective-permute-start(bf16[1,1024,128]{2,1,0:T(8,128)(2,1)S(1)} %slice.8), channel_id=1, source_target_pairs={{0,2},{2,4},{4,6},{6,8},{8,10},{10,12},{12,14},{14,0},{1,3},{3,5},... | collective-permute-start | bytes 786440 | tf_op jit(solution)/shard_map/ppermute | solution.py:140
  113.0 14.5 %collective-permute-start.9 = (bf16[1,1024,128]{2,1,0:T(8,128)(2,1)S(1)}, bf16[1,1024,128]{2,1,0:T(8,128)(2,1)S(1)}, u32[]{:S(2)}, u32[]{:S(2)}) collective-permute-start(bf16[1,1024,128]{2,1,0:T(8,128)(2,1)S(1)} %slice.9), channel_id=1, source_target_pairs={{0,14},{2,0},{4,2},{6,4},{8,6},{10,8},{12,10},{14,12},{1,15},{3,1}... | collective-permute-start | bytes 786440 | tf_op jit(solution)/shard_map/ppermute | solution.py:141

commit v2 on v0

--- a/solution.py
+++ b/solution.py
@@ -11,8 +11,7 @@
 HIGHEST = lax.Precision.HIGHEST
 PIECE = 512
 TILE = 128
-RING_ROWS = 40
-STREAMS = 1
+GROUP = 4
 
 
 def dot_t(a, b):
@@ -115,60 +114,115 @@
     )(*pieces, queries, coeff, hi, lo)
 
 
-def ring_gather(shard, axis, streams):
-    size = lax.axis_size(axis)
-    right = [(i, (i + 1) % size) for i in range(size)]
-    left = [(i, (i - 1) % size) for i in range(size)]
-    rows = shard.shape[0] // streams
-    parts = []
-    for stream in range(streams):
-        own = shard[stream * rows : (stream + 1) * rows]
-        arrived = {0: own}
-        up, down = own, own
-        for step in range(1, size // 2):
-            up = lax.ppermute(up, axis, right)
-            down = lax.ppermute(down, axis, left)
-            arrived[size - step] = up
-            arrived[step] = down
-        if stream % 2 == 0:
-            arrived[size // 2] = lax.ppermute(up, axis, right)
-        else:
-            arrived[size // 2] = lax.ppermute(down, axis, left)
-        parts.append([arrived[k] for k in range(size)])
-    return parts
+def exchange(value):
+    size = lax.axis_size("zh")
+    own = lax.axis_index("zh")
+    rows = value.shape[0] // size
+    slots = [lax.dynamic_slice_in_dim(value, own * rows, rows, 0)]
+    for apart in range(1, size):
+        to = lax.rem(own + apart, size)
+        piece = lax.dynamic_slice_in_dim(value, to * rows, rows, 0)
+        slots.append(lax.ppermute(piece, "zh", [(i, (i + apart) % size) for i in range(size)]))
+    return slots
+
+
+def exchange_heads(summed):
+    size = lax.axis_size("zh")
+    own = lax.axis_index("zh")
+    sums = [lax.dynamic_index_in_dim(summed, own, 0, keepdims=False)]
+    for apart in range(1, size):
+        piece = lax.dynamic_index_in_dim(summed, lax.rem(own + apart, size), 0, keepdims=False)
+        sums.append(lax.ppermute(piece, "zh", [(i, (i + apart) % size) for i in range(size)]))
+    return sums
+
+
+def line_gather(own):
+    size = lax.axis_size("zl")
+    up, down = own, own
+    ups, downs = {}, {}
+    for step in range(1, size):
+        up = lax.ppermute(up, "zl", [(i, i + 1) for i in range(step - 1, size - 1)])
+        down = lax.ppermute(down, "zl", [(i, i - 1) for i in range(1, size - step + 1)])
+        ups[step], downs[step] = up, down
+    arrived = [(0, own)]
+    for step in range(1, size):
+        arrived.append((size - step, ups[step], downs[size - step]))
+    return arrived
+
+
+def level_sums(state):
+    size = lax.axis_size("seq")
+    index = lax.axis_index("seq")
+    sums = []
+    for bit in range(size.bit_length() - 1):
+        other = lax.ppermute(state, "seq", [(i, i ^ (1 << bit)) for i in range(size)])
+        later = jnp.bitwise_and(jnp.right_shift(index, bit), 1) == 1
+        sums.append(jnp.where(later, other, 0.0))
+        state = state + other
+    return jnp.stack(sums)
+
+
+def product_kernel(slots, away, where_ref, *refs):
+    b_refs, a_refs, out_ref = refs[:slots], refs[slots:-1], refs[-1]
+    zh, zl = where_ref[0], where_ref[1]
+    rows, width = out_ref.shape[-2:]
+    b = jnp.concatenate([ref[...] for ref in b_refs], axis=1)
+    lines = out_ref.shape[0] // slots
+    heads = [lax.rem(zh - d + slots, slots) for d in range(slots)]
+
+    def place(a, d, line):
+        product = lax.dot_general(
+            a, b, (((0,), (0,)), ((), ())), preferred_element_type=jnp.float32
+        ).astype(jnp.bfloat16)
+        block = heads[d] * lines + line
+        for half in range(2):
+            for e in range(slots):
+                out_ref[block, half, heads[e]] = product[
+                    half * rows : (half + 1) * rows, e * width : (e + 1) * width
+                ]
+
+    for d in range(slots):
+        place(a_refs[0][d], d, zl)
+    for k, distance in enumerate(away):
+        line = lax.rem(zl + distance, lines)
+        up_ref, down_ref = a_refs[1 + 2 * k], a_refs[2 + 2 * k]
+        passed_up = zl >= lines - distance
+        for d in range(slots):
+            place(jnp.where(passed_up, up_ref[d], down_ref[d]), d, line)
+
+
+def products(arrived, b_slots):
+    slots = len(b_slots)
+    rows, width = b_slots[0].shape
+    where = jnp.stack([lax.axis_index("zh"), lax.axis_index("zl")]).astype(jnp.int32)
+    own, rest = arrived[0][1], arrived[1:]
+    operands = [own]
+    for _, up, down in rest:
+        operands += [up, down]
+    smem = pl.BlockSpec(memory_space=pltpu.SMEM)
+    vmem = pl.BlockSpec(memory_space=pltpu.VMEM)
+    blocks = slots * len(arrived)
+    return pl.pallas_call(
+        functools.partial(product_kernel, slots, [away for away, *_ in rest]),
+        out_shape=jax.ShapeDtypeStruct((blocks, 2, slots, width // 2, width), jnp.bfloat16),
+        in_specs=[smem] + [vmem] * (slots + len(operands)),
+        out_specs=vmem,
+        compiler_params=pltpu.CompilerParams(vmem_limit_bytes=40 * 1024 * 1024),
+        cost_estimate=pl.CostEstimate(
+            flops=2 * blocks * rows * width * width * slots,
+            bytes_accessed=2 * (len(operands) * own.size + slots * rows * width),
+            transcendentals=0,
+        ),
+    )(where, *b_slots, *operands)
 
 
 def body(queries, keys, values, level_ids, level_table, out_cotangent):
     block_len, head_dim = queries.shape
     n_seq = lax.axis_size("seq")
-    n_head = lax.axis_size("head")
     local_bits = block_len.bit_length() - 1
     seq_bits = n_seq.bit_length() - 1
     table_rows = level_table.shape[0]
     own_index = lax.axis_index("seq")
-    own_head = lax.axis_index("head")
-
-    cot = out_cotangent.T.reshape(2, head_dim // 2, block_len)
-    ring_part = cot[:, :RING_ROWS].reshape(2 * RING_ROWS, block_len)
-    gather_part = cot[:, RING_ROWS:].reshape(head_dim - 2 * RING_ROWS, block_len)
-    gathered = lax.all_gather(gather_part, "head", axis=0)
-    ring = ring_gather(ring_part, "head", STREAMS)
-
-    state = lax.dot_general(
-        keys, values, (((0,), (0,)), ((), ())), preferred_element_type=jnp.float32
-    )
-    states = lax.all_to_all(
-        jnp.broadcast_to(state, (n_seq, head_dim, head_dim)), "seq", 0, 0, tiled=True
-    )
-    source = jnp.arange(n_seq, dtype=jnp.int32)
-    apart = jnp.bitwise_xor(own_index, source)
-    select = jnp.stack(
-        [
-            ((jnp.right_shift(apart, level) == 1) & (source < own_index)).astype(jnp.float32)
-            for level in range(seq_bits)
-        ]
-    )
-    level_states = jnp.einsum("ji,ide->jde", select, states, precision=HIGHEST)
 
     onehot = (level_ids[:, None] == jnp.arange(table_rows, dtype=jnp.int32)[None, :]).astype(
         jnp.float32
@@ -177,36 +231,34 @@
     pieces = [
         local_piece(piece, queries, keys, values, coeff) for piece in range(block_len // PIECE)
     ]
+
+    arrived = line_gather(jnp.stack(exchange(out_cotangent)))
+
+    state = lax.dot_general(
+        keys, values, (((0,), (0,)), ((), ())), preferred_element_type=jnp.float32
+    )
+    level_states = level_sums(state)
     attn_out = finish(pieces, queries, coeff, level_states, local_bits + 1)
 
     scale = (block_len * n_seq) ** (-0.5)
-
-    def own_share(products):
-        rows = products.shape[2]
-        sent = products.reshape(n_seq, rows, head_dim).astype(jnp.bfloat16)
-        arrived = lax.all_to_all(sent, "seq", 0, 0, tiled=True)
-        return arrived.astype(jnp.float32).sum(axis=0) * scale
-
-    streams = []
-    for parts in ring:
-        products = jnp.stack([dot(part, attn_out) for part in parts])
-        doubled = jnp.concatenate([products, products], axis=0).astype(jnp.bfloat16)
-        streams.append(lax.dynamic_slice_in_dim(doubled, n_head - own_head, n_head, 0))
-    products = jnp.concatenate(streams, axis=1).reshape(n_head, 2, RING_ROWS, head_dim)
-    upper = own_share(products)
-    rest = dot(gathered.reshape(-1, block_len), attn_out)
-    lower = own_share(rest.reshape(n_head, 2, head_dim // 2 - RING_ROWS, head_dim))
-    return attn_out, jnp.concatenate([upper, lower], axis=0)
+    partial = products(arrived, exchange(attn_out))
+    sent = partial.reshape(n_seq, -1, head_dim)
+    summed = lax.all_to_all(sent, "seq", 0, 0, tiled=True).astype(jnp.float32).sum(axis=0)
+    summed = summed.reshape(lax.axis_size("zh"), head_dim // 2, head_dim)
+    weight_grad = sum(exchange_heads(summed)) * scale
+    return attn_out, weight_grad
 
 
 def solution(mesh):
-    in_specs = (
-        P("seq", "head"),
-        P("seq", "head"),
-        P("seq", "head"),
-        P("seq"),
-        P(),
-        P("seq", "head"),
-    )
-    out_specs = (P("seq", "head"), P("seq", "head"))
-    return jax.shard_map(body, mesh=mesh, in_specs=in_specs, out_specs=out_specs, check_vma=False)
+    n_seq, n_head = mesh.devices.shape
+    mesh = jax.sharding.Mesh(
+        mesh.devices.reshape(n_seq, n_head // GROUP, GROUP), ("seq", "zh", "zl")
+    )
+    split = P("seq", ("zh", "zl"))
+    return jax.shard_map(
+        body,
+        mesh=mesh,
+        in_specs=(split, split, split, P("seq"), P(), split),
+        out_specs=(split, split),
+        check_vma=False,
+    )

time: 184 us -> 195 us (1.060)
  the two profiles are of different devices: /device:TPU:1 before, /device:TPU:96 now
where the time goes in v2:
time: 195 us; the launch traced here: 194 us
  starting transfers between devices  90.1 us (46%)
  waiting for transfers between devices  82.8 us (42%)
  Pallas kernels  13.3 us (7%)
  local copies, waits for them, and re-layouts  3.02 us (2%)
  matrix products  2.61 us (1%)
    ppermute x6, starting transfers between devices, exchange(): lax.ppermute(piece, 'zh', [(i, (i + apart) % size) for i in range(size)])  38.5 us
    ppermute x6, waiting for transfers between devices, exchange(): lax.ppermute(piece, 'zh', [(i, (i + apart) % size) for i in range(size)])  35.4 us
    all_to_all x1, waiting for transfers between devices, body(): lax.all_to_all(sent, 'seq', 0, 0, tiled=True).astype(jnp.float32)  30 us
    ppermute x5, starting transfers between devices, level_sums(): other = lax.ppermute(state, 'seq', [(i, i ^ 1 << bit) for i in range(size)])  18.9 us
    ppermute x3, starting transfers between devices, exchange_heads(): lax.ppermute(piece, 'zh', [(i, (i + apart) % size) for i in range(size)])  18 us
    ppermute x5, waiting for transfers between devices, level_sums(): other = lax.ppermute(state, 'seq', [(i, i ^ 1 << bit) for i in range(size)])  8.55 us
    ppermute x3, waiting for transfers between devices, exchange_heads(): lax.ppermute(piece, 'zh', [(i, (i + apart) % size) for i in range(size)])  6.58 us
    all_to_all x1, starting transfers between devices, body(): lax.all_to_all(sent, 'seq', 0, 0, tiled=True).astype(jnp.float32)  6.58 us
  transfers between devices with their start and end apart: 21, of which 10 were waited for; matrix products, arithmetic and copies ran while one was open for 2% of the time, Pallas kernels for 5%

profile of v2, /device:TPU:96, one launch (start us, length us, event | category | flops | bytes accessed | tf_op | source)
XLA Modules:
  0.0 194.1 jit_solution(1758078724755966131)
XLA Ops:
  0.6 0.0 copy-start
  0.7 1.6 fusion.5
  2.3 1.9 collective-permute-start
  4.3 1.1 dynamic-slice_bitcast_fusion
  5.4 9.1 %collective-permute-start.8 = (bf16[512,128]{1,0:T(8,128)(2,1)S(1)}, bf16[512,128]{1,0:T(8,128)(2,1)S(1)}, u32[]{:S(2)}, u32[]{:S(2)}) collective-permute-start(bf16[512,128]{1,0:T(8,128)(2,1)S(1)} %get-tuple-element.5), channel_id=1, source_target_pairs={{0,4},{4,8},{8,12},{12,0},{1,5},{5,9},{9,13},{13,1},{2,6},{6,10},{... | collective-permute-start | bytes 393224 | tf_op jit(solution)/shard_map/ppermute | solution.py:125
  14.5 2.9 %collective-permute-start.10 = (bf16[512,128]{1,0:T(8,128)(2,1)S(1)}, bf16[512,128]{1,0:T(8,128)(2,1)S(1)}, u32[]{:S(2)}, u32[]{:S(2)}) collective-permute-start(bf16[512,128]{1,0:T(8,128)(2,1)S(1)} %get-tuple-element.6), channel_id=1, source_target_pairs={{0,12},{4,0},{8,4},{12,8},{1,13},{5,1},{9,5},{13,9},{2,14},{6,2},{... | collective-permute-start | bytes 393224 | tf_op jit(solution)/shard_map/ppermute | solution.py:125
  17.4 10.8 %collective-permute-start.9 = (bf16[512,128]{1,0:T(8,128)(2,1)S(1)}, bf16[512,128]{1,0:T(8,128)(2,1)S(1)}, u32[]{:S(2)}, u32[]{:S(2)}) collective-permute-start(bf16[512,128]{1,0:T(8,128)(2,1)S(1)} %get-tuple-element.7), channel_id=1, source_target_pairs={{0,8},{4,12},{8,0},{12,4},{1,9},{5,13},{9,1},{13,5},{2,10},{6,14},... | collective-permute-start | bytes 393224 | tf_op jit(solution)/shard_map/ppermute | solution.py:125
  28.2 0.0 copy-done
  28.2 0.0 copy-done.6
  28.3 1.0 fusion.c_ref
  29.3 1.6 shard_map.79.l2
  30.9 0.0 collective-permute-done.8
  30.9 0.0 collective-permute-done.10
  30.9 19.1 %collective-permute-done.9 = bf16[512,128]{1,0:T(8,128)(2,1)S(1)} collective-permute-done((bf16[512,128]{1,0:T(8,128)(2,1)S(1)}, bf16[512,128]{1,0:T(8,128)(2,1)S(1)}, u32[]{:S(2)}, u32[]{:S(2)}) %collective-permute-start.9) | collective-permute-done | bytes 131104 | tf_op jit(solution)/shard_map/ppermute | solution.py:125
  50.0 0.1 pad_maximum_fusion.refs_4_
  50.1 2.1 %collective-permute-start.12 = (bf16[4,512,128]{2,1,0:T(8,128)(2,1)S(1)}, bf16[4,512,128]{2,1,0:T(8,128)(2,1)}, u32[]{:S(2)}, u32[]{:S(2)}) collective-permute-start(bf16[4,512,128]{2,1,0:T(8,128)(2,1)S(1)} %pad_maximum_fusion.refs_4_), channel_id=1, source_target_pairs={{1,0},{2,1},{3,2},{5,4},{6,5},{7,6},{9,8},{10,9},{11,10},{13,12},{... | collective-permute-start | bytes 1572872 | tf_op jit(solution)/shard_map/ppermute | solution.py:145
  52.2 1.3 collective-permute-start.11
  53.5 1.2 shard_map.78.l1
  54.7 0.0 copy-start.4
  54.7 0.7 copy-done.4
  55.4 1.1 shard_map.77.l0
  56.5 0.0 copy-start.5
  56.5 1.9 shard_map.80.l3
  58.4 0.0 collective-permute-done
  58.5 3.4 %collective-permute-start.1 = (f32[128,128]{1,0:T(8,128)S(1)}, f32[128,128]{1,0:T(8,128)S(1)}, u32[]{:S(2)}, u32[]{:S(2)}) collective-permute-start(f32[128,128]{1,0:T(8,128)S(1)} %add.65), channel_id=1, source_target_pairs={{0,32},{16,48},{32,0},{48,16},{64,96},{80,112},{96,64},{112,80},{1... | collective-permute-start | bytes 196616 | tf_op jit(solution)/shard_map/ppermute | solution.py:158
  61.9 2.7 %collective-permute-done.1 = f32[128,128]{1,0:T(8,128)S(1)} collective-permute-done((f32[128,128]{1,0:T(8,128)S(1)}, f32[128,128]{1,0:T(8,128)S(1)}, u32[]{:S(2)}, u32[]{:S(2)}) %collective-permute-start.1) | collective-permute-done | bytes 65568 | tf_op jit(solution)/shard_map/ppermute | solution.py:158
  64.6 4.9 %collective-permute-start.2 = (f32[128,128]{1,0:T(8,128)S(1)}, f32[128,128]{1,0:T(8,128)S(1)}, u32[]{:S(2)}, u32[]{:S(2)}) collective-permute-start(f32[128,128]{1,0:T(8,128)S(1)} %add.66), channel_id=1, source_target_pairs={{0,64},{16,80},{32,96},{48,112},{64,0},{80,16},{96,32},{112,48},{1... | collective-permute-start | bytes 196616 | tf_op jit(solution)/shard_map/ppermute | solution.py:158
  69.6 2.7 %collective-permute-done.2 = f32[128,128]{1,0:T(8,128)S(1)} collective-permute-done((f32[128,128]{1,0:T(8,128)S(1)}, f32[128,128]{1,0:T(8,128)S(1)}, u32[]{:S(2)}, u32[]{:S(2)}) %collective-permute-start.2) | collective-permute-done | bytes 65568 | tf_op jit(solution)/shard_map/ppermute | solution.py:158
  72.3 3.5 %collective-permute-start.3 = (f32[128,128]{1,0:T(8,128)S(1)}, f32[128,128]{1,0:T(8,128)S(1)}, u32[]{:S(2)}, u32[]{:S(2)}) collective-permute-start(f32[128,128]{1,0:T(8,128)S(1)} %add.67), channel_id=1, source_target_pairs={{0,128},{16,144},{32,160},{48,176},{64,192},{80,208},{96,224},{112... | collective-permute-start | bytes 196616 | tf_op jit(solution)/shard_map/ppermute | solution.py:158
  75.8 0.0 collective-permute-done.12.refs_10_
  75.8 0.7 collective-permute-start.13
  76.5 0.0 collective-permute-done.11.refs_5_
  76.5 1.3 collective-permute-start.15
  77.9 0.6 collective-permute-done.3
  78.5 5.1 %collective-permute-start.4 = (f32[128,128]{1,0:T(8,128)S(1)}, f32[128,128]{1,0:T(8,128)S(1)}, u32[]{:S(2)}, u32[]{:S(2)}) collective-permute-start(f32[128,128]{1,0:T(8,128)S(1)} %add.68), channel_id=1, source_target_pairs={{0,256},{16,272},{32,288},{48,304},{64,320},{80,336},{96,352},{112... | collective-permute-start | bytes 196616 | tf_op jit(solution)/shard_map/ppermute | solution.py:158
  83.6 2.5 %collective-permute-done.4 = f32[128,128]{1,0:T(8,128)S(1)} collective-permute-done((f32[128,128]{1,0:T(8,128)S(1)}, f32[128,128]{1,0:T(8,128)S(1)}, u32[]{:S(2)}, u32[]{:S(2)}) %collective-permute-start.4) | collective-permute-done | bytes 65568 | tf_op jit(solution)/shard_map/ppermute | solution.py:158
  86.2 0.0 collective-permute-done.13.refs_8_
  86.2 1.5 collective-permute-start.14
  87.7 2.3 %collective-permute-done.15.refs_7_ = bf16[4,512,128]{2,1,0:T(8,128)(2,1)} collective-permute-done((bf16[4,512,128]{2,1,0:T(8,128)(2,1)}, bf16[4,512,128]{2,1,0:T(8,128)(2,1)}, u32[]{:S(2)}, u32[]{:S(2)}) %collective-permute-start.15) | collective-permute-done | bytes 524320 | tf_op jit(solution)/shard_map/ppermute | solution.py:144
  89.9 1.3 collective-permute-start.16
  91.2 0.1 subtract_convert_fusion
  91.3 0.0 copy-done.5
  91.3 3.0 %shard_map.81 = bf16[2048,128]{1,0:T(8,128)(2,1)} custom-call(f32[512,128]{1,0:T(8,128)S(1)} %shard_map.77.l0, f32[512,128]{1,0:T(8,128)S(1)} %copy-done.5, f32[512,128]{1,0:T(8,128)S(1)} %shard_map.79.l2, f32[512,128]{1,0:T(8,128)S(1)} %shard_map.80.l3, bf16[2048,128]{1,0:T(8,128)(2,1)S(1)} %copy-done.3, f32[2048,17]{1,0:T(8,128)S(1)} %fusion.c_ref, ...), custom_call_target="tpu_custom_call" | custom-call | flops 671088640 | bytes 4194304 | tf_op jit(solution)/shard_map/pallas_call | solution.py:107
  94.2 1.1 constant_dynamic-slice_fusion.3
  95.4 4.4 %collective-permute-start.7 = (bf16[512,128]{1,0:T(8,128)(2,1)S(1)}, bf16[512,128]{1,0:T(8,128)(2,1)S(1)}, u32[]{:S(2)}, u32[]{:S(2)}) collective-permute-start(bf16[512,128]{1,0:T(8,128)(2,1)S(1)} %get-tuple-element.8), channel_id=1, source_target_pairs={{0,12},{4,0},{8,4},{12,8},{1,13},{5,1},{9,5},{13,9},{2,14},{6,2},{... | collective-permute-start | bytes 393224 | tf_op jit(solution)/shard_map/ppermute | solution.py:125
  99.8 6.0 %collective-permute-start.6 = (bf16[512,128]{1,0:T(8,128)(2,1)S(1)}, bf16[512,128]{1,0:T(8,128)(2,1)S(1)}, u32[]{:S(2)}, u32[]{:S(2)}) collective-permute-start(bf16[512,128]{1,0:T(8,128)(2,1)S(1)} %get-tuple-element.9), channel_id=1, source_target_pairs={{0,8},{4,12},{8,0},{12,4},{1,9},{5,13},{9,1},{13,5},{2,10},{6,14},... | collective-permute-start | bytes 393224 | tf_op jit(solution)/shard_map/ppermute | solution.py:125
  105.7 5.4 %collective-permute-start.5 = (bf16[512,128]{1,0:T(8,128)(2,1)S(1)}, bf16[512,128]{1,0:T(8,128)(2,1)S(1)}, u32[]{:S(2)}, u32[]{:S(2)}) collective-permute-start(bf16[512,128]{1,0:T(8,128)(2,1)S(1)} %get-tuple-element.10), channel_id=1, source_target_pairs={{0,4},{4,8},{8,12},{12,0},{1,5},{5,9},{9,13},{13,1},{2,6},{6,10},{... | collective-permute-start | bytes 393224 | tf_op jit(solution)/shard_map/ppermute | solution.py:125
  111.1 0.1 pad_add_fusion.where_ref
  111.2 0.0 collective-permute-done.7.refs_3_
  111.2 5.5 %collective-permute-done.6.refs_2_ = bf16[512,128]{1,0:T(8,128)(2,1)S(1)} collective-permute-done((bf16[512,128]{1,0:T(8,128)(2,1)S(1)}, bf16[512,128]{1,0:T(8,128)(2,1)S(1)}, u32[]{:S(2)}, u32[]{:S(2)}) %collective-permute-start.6) | collective-permute-done | bytes 131104 | tf_op jit(solution)/shard_map/ppermute | solution.py:125
  116.7 10.8 %collective-permute-done.5.refs_1_ = bf16[512,128]{1,0:T(8,128)(2,1)S(1)} collective-permute-done((bf16[512,128]{1,0:T(8,128)(2,1)S(1)}, bf16[512,128]{1,0:T(8,128)(2,1)S(1)}, u32[]{:S(2)}, u32[]{:S(2)}) %collective-permute-start.5) | collective-permute-done | bytes 131104 | tf_op jit(solution)/shard_map/ppermute | solution.py:125
  127.5 0.0 collective-permute-done.14.refs_6_
  127.5 0.0 collective-permute-done.16.refs_9_
  127.5 4.4 %shard_map.82 = bf16[16,2,4,64,128]{4,3,2,1,0:T(8,128)(2,1)} custom-call(s32[2]{0:T(128)S(1)} %pad_add_fusion.where_ref, bf16[512,128]{1,0:T(8,128)(2,1)S(1)} %get-tuple-element.11.refs_0_, bf16[512,128]{1,0:T(8,128)(2,1)S(1)} %collective-permute-done.5.refs_1_, bf16[512,128]{1,0:T(8,128)(2,1)S(1)} %collective-permute-done.6.refs_2_, ...), custom_call_target="tpu_custom_call" | custom-call | flops 1073741824 | bytes 4194304 | tf_op jit(solution)/shard_map/pallas_call | solution.py:205
  131.9 6.6 %all-to-all-start = ((bf16[32,256,128]{2,1,0:T(8,128)(2,1)}), bf16[32,256,128]{2,1,0:T(8,128)(2,1)S(1)}, u32[]{:S(2)}, u32[]{:S(2)}) async-start(bf16[32,256,128]{2,1,0:T(8,128)(2,1)} %bitcast.11), calls=%async_computation | async-start | bytes 4194304 | tf_op jit(solution)/shard_map/all_to_all | solution.py:246
  138.6 30.0 %all-to-all-done = bf16[32,256,128]{2,1,0:T(8,128)(2,1)S(1)} async-done(((bf16[32,256,128]{2,1,0:T(8,128)(2,1)}), bf16[32,256,128]{2,1,0:T(8,128)(2,1)S(1)}, u32[]{:S(2)}, u32[]{:S(2)}) %all-to-all-start) | async-done | bytes 2097184 | tf_op jit(solution)/shard_map/all_to_all | solution.py:246
  168.5 0.3 convert_reduce_fusion
  168.8 5.3 %collective-permute-start.17 = (f32[64,128]{1,0:T(8,128)S(1)}, f32[64,128]{1,0:T(8,128)S(1)}, u32[]{:S(2)}, u32[]{:S(2)}) collective-permute-start(f32[64,128]{1,0:T(8,128)S(1)} %get-tuple-element.12), channel_id=1, source_target_pairs={{0,4},{4,8},{8,12},{12,0},{1,5},{5,9},{9,13},{13,1},{2,6},{6,10},{... | collective-permute-start | bytes 98312 | tf_op jit(solution)/shard_map/ppermute | solution.py:135
  174.1 4.4 %collective-permute-start.19 = (f32[64,128]{1,0:T(8,128)S(1)}, f32[64,128]{1,0:T(8,128)S(1)}, u32[]{:S(2)}, u32[]{:S(2)}) collective-permute-start(f32[64,128]{1,0:T(8,128)S(1)} %get-tuple-element.13), channel_id=1, source_target_pairs={{0,12},{4,0},{8,4},{12,8},{1,13},{5,1},{9,5},{13,9},{2,14},{6,2},{... | collective-permute-start | bytes 98312 | tf_op jit(solution)/shard_map/ppermute | solution.py:135
  178.6 8.3 %collective-permute-start.18 = (f32[64,128]{1,0:T(8,128)S(1)}, f32[64,128]{1,0:T(8,128)S(1)}, u32[]{:S(2)}, u32[]{:S(2)}) collective-permute-start(f32[64,128]{1,0:T(8,128)S(1)} %get-tuple-element.14), channel_id=1, source_target_pairs={{0,8},{4,12},{8,0},{12,4},{1,9},{5,13},{9,1},{13,5},{2,10},{6,14},... | collective-permute-start | bytes 98312 | tf_op jit(solution)/shard_map/ppermute | solution.py:135
  186.9 0.0 collective-permute-done.17
  186.9 0.0 collective-permute-done.19
  186.9 6.6 %collective-permute-done.18 = f32[64,128]{1,0:T(8,128)S(1)} collective-permute-done((f32[64,128]{1,0:T(8,128)S(1)}, f32[64,128]{1,0:T(8,128)S(1)}, u32[]{:S(2)}, u32[]{:S(2)}) %collective-permute-start.18) | collective-permute-done | bytes 32800 | tf_op jit(solution)/shard_map/ppermute | solution.py:135
  193.5 0.6 fusion.4
  (17 shorter events, 0.1 us)
Async XLA Ops:
  0.6 27.6 %copy-start = (f32[64,17]{0,1:T(8,128)S(1)}, f32[64,17]{0,1:T(8,128)}, u32[]{:S(2)}) copy-start(f32[64,17]{0,1:T(8,128)} %param.10) | copy-start | bytes 13060
  0.6 28.6 %copy-start.2 = (bf16[2048,128]{1,0:T(8,128)(2,1)S(1)}, bf16[2048,128]{1,0:T(8,128)(2,1)}, u32[]{:S(2)}) copy-start(bf16[2048,128]{1,0:T(8,128)(2,1)} %v_ref.7) | copy-start | bytes 1572868
  0.7 28.6 %copy-start.1 = (bf16[2048,128]{1,0:T(8,128)(2,1)S(1)}, bf16[2048,128]{1,0:T(8,128)(2,1)}, u32[]{:S(2)}) copy-start(bf16[2048,128]{1,0:T(8,128)(2,1)} %k_ref.7) | copy-start | bytes 1572868
  0.7 27.6 %copy-start.6 = (s32[2048]{0:T(1024)S(1)}, s32[2048]{0:T(1024)}, u32[]{:S(2)}) copy-start(s32[2048]{0:T(1024)} %param.9) | copy-start | bytes 24580
  0.7 28.6 %copy-start.3 = (bf16[2048,128]{1,0:T(8,128)(2,1)S(1)}, bf16[2048,128]{1,0:T(8,128)(2,1)}, u32[]{:S(2)}) copy-start(bf16[2048,128]{1,0:T(8,128)(2,1)} %q_ref.9) | copy-start | bytes 1572868
  2.3 56.1 %collective-permute-start = (f32[128,128]{1,0:T(8,128)S(1)}, f32[128,128]{1,0:T(8,128)S(1)}, u32[]{:S(2)}, u32[]{:S(2)}) collective-permute-start(f32[128,128]{1,0:T(8,128)S(1)} %fusion.5), channel_id=1, source_target_pairs={{0,16},{16,0},{32,48},{48,32},{64,80},{80,64},{96,112},{112,96},{1... | collective-permute-start | bytes 196616 | tf_op jit(solution)/shard_map/ppermute | solution.py:158
  5.4 25.5 %collective-permute-start.8 = (bf16[512,128]{1,0:T(8,128)(2,1)S(1)}, bf16[512,128]{1,0:T(8,128)(2,1)S(1)}, u32[]{:S(2)}, u32[]{:S(2)}) collective-permute-start(bf16[512,128]{1,0:T(8,128)(2,1)S(1)} %get-tuple-element.5), channel_id=1, source_target_pairs={{0,4},{4,8},{8,12},{12,0},{1,5},{5,9},{9,13},{13,1},{2,6},{6,10},{... | collective-permute-start | bytes 393224 | tf_op jit(solution)/shard_map/ppermute | solution.py:125
  14.5 16.4 %collective-permute-start.10 = (bf16[512,128]{1,0:T(8,128)(2,1)S(1)}, bf16[512,128]{1,0:T(8,128)(2,1)S(1)}, u32[]{:S(2)}, u32[]{:S(2)}) collective-permute-start(bf16[512,128]{1,0:T(8,128)(2,1)S(1)} %get-tuple-element.6), channel_id=1, source_target_pairs={{0,12},{4,0},{8,4},{12,8},{1,13},{5,1},{9,5},{13,9},{2,14},{6,2},{... | collective-permute-start | bytes 393224 | tf_op jit(solution)/shard_map/ppermute | solution.py:125
  17.4 32.6 %collective-permute-start.9 = (bf16[512,128]{1,0:T(8,128)(2,1)S(1)}, bf16[512,128]{1,0:T(8,128)(2,1)S(1)}, u32[]{:S(2)}, u32[]{:S(2)}) collective-permute-start(bf16[512,128]{1,0:T(8,128)(2,1)S(1)} %get-tuple-element.7), channel_id=1, source_target_pairs={{0,8},{4,12},{8,0},{12,4},{1,9},{5,13},{9,1},{13,5},{2,10},{6,14},... | collective-permute-start | bytes 393224 | tf_op jit(solution)/shard_map/ppermute | solution.py:125
  50.1 25.7 %collective-permute-start.12 = (bf16[4,512,128]{2,1,0:T(8,128)(2,1)S(1)}, bf16[4,512,128]{2,1,0:T(8,128)(2,1)}, u32[]{:S(2)}, u32[]{:S(2)}) collective-permute-start(bf16[4,512,128]{2,1,0:T(8,128)(2,1)S(1)} %pad_maximum_fusion.refs_4_), channel_id=1, source_target_pairs={{1,0},{2,1},{3,2},{5,4},{6,5},{7,6},{9,8},{10,9},{11,10},{13,12},{... | collective-permute-start | bytes 1572872 | tf_op jit(solution)/shard_map/ppermute | solution.py:145
  52.2 24.4 %collective-permute-start.11 = (bf16[4,512,128]{2,1,0:T(8,128)(2,1)S(1)}, bf16[4,512,128]{2,1,0:T(8,128)(2,1)}, u32[]{:S(2)}, u32[]{:S(2)}) collective-permute-start(bf16[4,512,128]{2,1,0:T(8,128)(2,1)S(1)} %pad_maximum_fusion.refs_4_), channel_id=1, source_target_pairs={{0,1},{1,2},{2,3},{4,5},{5,6},{6,7},{8,9},{9,10},{10,11},{12,13},{... | collective-permute-start | bytes 1572872 | tf_op jit(solution)/shard_map/ppermute | solution.py:144
  54.7 0.7 copy-start.4
  56.5 34.8 %copy-start.5 = (f32[512,128]{1,0:T(8,128)S(1)}, f32[512,128]{1,0:T(8,128)}, u32[]{:S(2)}) copy-start(f32[512,128]{1,0:T(8,128)} %copy-done.4) | copy-start | bytes 786436
  58.5 6.2 %collective-permute-start.1 = (f32[128,128]{1,0:T(8,128)S(1)}, f32[128,128]{1,0:T(8,128)S(1)}, u32[]{:S(2)}, u32[]{:S(2)}) collective-permute-start(f32[128,128]{1,0:T(8,128)S(1)} %add.65), channel_id=1, source_target_pairs={{0,32},{16,48},{32,0},{48,16},{64,96},{80,112},{96,64},{112,80},{1... | collective-permute-start | bytes 196616 | tf_op jit(solution)/shard_map/ppermute | solution.py:158
  64.6 7.7 %collective-permute-start.2 = (f32[128,128]{1,0:T(8,128)S(1)}, f32[128,128]{1,0:T(8,128)S(1)}, u32[]{:S(2)}, u32[]{:S(2)}) collective-permute-start(f32[128,128]{1,0:T(8,128)S(1)} %add.66), channel_id=1, source_target_pairs={{0,64},{16,80},{32,96},{48,112},{64,0},{80,16},{96,32},{112,48},{1... | collective-permute-start | bytes 196616 | tf_op jit(solution)/shard_map/ppermute | solution.py:158
  72.3 6.2 %collective-permute-start.3 = (f32[128,128]{1,0:T(8,128)S(1)}, f32[128,128]{1,0:T(8,128)S(1)}, u32[]{:S(2)}, u32[]{:S(2)}) collective-permute-start(f32[128,128]{1,0:T(8,128)S(1)} %add.67), channel_id=1, source_target_pairs={{0,128},{16,144},{32,160},{48,176},{64,192},{80,208},{96,224},{112... | collective-permute-start | bytes 196616 | tf_op jit(solution)/shard_map/ppermute | solution.py:158
  75.8 10.3 %collective-permute-start.13 = (bf16[4,512,128]{2,1,0:T(8,128)(2,1)}, bf16[4,512,128]{2,1,0:T(8,128)(2,1)S(1)}, u32[]{:S(2)}, u32[]{:S(2)}) collective-permute-start(bf16[4,512,128]{2,1,0:T(8,128)(2,1)} %collective-permute-done.12.refs_10_), channel_id=1, source_target_pairs={{1,0},{2,1},{5,4},{6,5},{9,8},{10,9},{13,12},{14,13},{17,16},{18,1... | collective-permute-start | bytes 1572872 | tf_op jit(solution)/shard_map/ppermute | solution.py:145
  76.5 13.4 %collective-permute-start.15 = (bf16[4,512,128]{2,1,0:T(8,128)(2,1)}, bf16[4,512,128]{2,1,0:T(8,128)(2,1)}, u32[]{:S(2)}, u32[]{:S(2)}) collective-permute-start(bf16[4,512,128]{2,1,0:T(8,128)(2,1)} %collective-permute-done.11.refs_5_), channel_id=1, source_target_pairs={{1,2},{2,3},{5,6},{6,7},{9,10},{10,11},{13,14},{14,15},{17,18},{18... | collective-permute-start | bytes 1572872 | tf_op jit(solution)/shard_map/ppermute | solution.py:144
  78.5 7.7 %collective-permute-start.4 = (f32[128,128]{1,0:T(8,128)S(1)}, f32[128,128]{1,0:T(8,128)S(1)}, u32[]{:S(2)}, u32[]{:S(2)}) collective-permute-start(f32[128,128]{1,0:T(8,128)S(1)} %add.68), channel_id=1, source_target_pairs={{0,256},{16,272},{32,288},{48,304},{64,320},{80,336},{96,352},{112... | collective-permute-start | bytes 196616 | tf_op jit(solution)/shard_map/ppermute | solution.py:158
  86.2 41.4 %collective-permute-start.14 = (bf16[4,512,128]{2,1,0:T(8,128)(2,1)S(1)}, bf16[4,512,128]{2,1,0:T(8,128)(2,1)}, u32[]{:S(2)}, u32[]{:S(2)}) collective-permute-start(bf16[4,512,128]{2,1,0:T(8,128)(2,1)S(1)} %collective-permute-done.13.refs_8_), channel_id=1, source_target_pairs={{1,0},{5,4},{9,8},{13,12},{17,16},{21,20},{25,24},{29,28},{33,32},... | collective-permute-start | bytes 1572872 | tf_op jit(solution)/shard_map/ppermute | solution.py:145
  89.9 37.6 %collective-permute-start.16 = (bf16[4,512,128]{2,1,0:T(8,128)(2,1)}, bf16[4,512,128]{2,1,0:T(8,128)(2,1)}, u32[]{:S(2)}, u32[]{:S(2)}) collective-permute-start(bf16[4,512,128]{2,1,0:T(8,128)(2,1)} %collective-permute-done.15.refs_7_), channel_id=1, source_target_pairs={{2,3},{6,7},{10,11},{14,15},{18,19},{22,23},{26,27},{30,31},{34,35... | collective-permute-start | bytes 1572872 | tf_op jit(solution)/shard_map/ppermute | solution.py:144
  95.4 15.8 %collective-permute-start.7 = (bf16[512,128]{1,0:T(8,128)(2,1)S(1)}, bf16[512,128]{1,0:T(8,128)(2,1)S(1)}, u32[]{:S(2)}, u32[]{:S(2)}) collective-permute-start(bf16[512,128]{1,0:T(8,128)(2,1)S(1)} %get-tuple-element.8), channel_id=1, source_target_pairs={{0,12},{4,0},{8,4},{12,8},{1,13},{5,1},{9,5},{13,9},{2,14},{6,2},{... | collective-permute-start | bytes 393224 | tf_op jit(solution)/shard_map/ppermute | solution.py:125
  99.8 17.0 %collective-permute-start.6 = (bf16[512,128]{1,0:T(8,128)(2,1)S(1)}, bf16[512,128]{1,0:T(8,128)(2,1)S(1)}, u32[]{:S(2)}, u32[]{:S(2)}) collective-permute-start(bf16[512,128]{1,0:T(8,128)(2,1)S(1)} %get-tuple-element.9), channel_id=1, source_target_pairs={{0,8},{4,12},{8,0},{12,4},{1,9},{5,13},{9,1},{13,5},{2,10},{6,14},... | collective-permute-start | bytes 393224 | tf_op jit(solution)/shard_map/ppermute | solution.py:125
  105.7 21.8 %collective-permute-start.5 = (bf16[512,128]{1,0:T(8,128)(2,1)S(1)}, bf16[512,128]{1,0:T(8,128)(2,1)S(1)}, u32[]{:S(2)}, u32[]{:S(2)}) collective-permute-start(bf16[512,128]{1,0:T(8,128)(2,1)S(1)} %get-tuple-element.10), channel_id=1, source_target_pairs={{0,4},{4,8},{8,12},{12,0},{1,5},{5,9},{9,13},{13,1},{2,6},{6,10},{... | collective-permute-start | bytes 393224 | tf_op jit(solution)/shard_map/ppermute | solution.py:125
  131.9 36.6 %all-to-all-start = ((bf16[32,256,128]{2,1,0:T(8,128)(2,1)}), bf16[32,256,128]{2,1,0:T(8,128)(2,1)S(1)}, u32[]{:S(2)}, u32[]{:S(2)}) async-start(bf16[32,256,128]{2,1,0:T(8,128)(2,1)} %bitcast.11), calls=%async_computation | async-start | bytes 4194304 | tf_op jit(solution)/shard_map/all_to_all | solution.py:246
  168.8 18.0 %collective-permute-start.17 = (f32[64,128]{1,0:T(8,128)S(1)}, f32[64,128]{1,0:T(8,128)S(1)}, u32[]{:S(2)}, u32[]{:S(2)}) collective-permute-start(f32[64,128]{1,0:T(8,128)S(1)} %get-tuple-element.12), channel_id=1, source_target_pairs={{0,4},{4,8},{8,12},{12,0},{1,5},{5,9},{9,13},{13,1},{2,6},{6,10},{... | collective-permute-start | bytes 98312 | tf_op jit(solution)/shard_map/ppermute | solution.py:135
  174.1 12.7 %collective-permute-start.19 = (f32[64,128]{1,0:T(8,128)S(1)}, f32[64,128]{1,0:T(8,128)S(1)}, u32[]{:S(2)}, u32[]{:S(2)}) collective-permute-start(f32[64,128]{1,0:T(8,128)S(1)} %get-tuple-element.13), channel_id=1, source_target_pairs={{0,12},{4,0},{8,4},{12,8},{1,13},{5,1},{9,5},{13,9},{2,14},{6,2},{... | collective-permute-start | bytes 98312 | tf_op jit(solution)/shard_map/ppermute | solution.py:135
  178.6 14.9 %collective-permute-start.18 = (f32[64,128]{1,0:T(8,128)S(1)}, f32[64,128]{1,0:T(8,128)S(1)}, u32[]{:S(2)}, u32[]{:S(2)}) collective-permute-start(f32[64,128]{1,0:T(8,128)S(1)} %get-tuple-element.14), channel_id=1, source_target_pairs={{0,8},{4,12},{8,0},{12,4},{1,9},{5,13},{9,1},{13,5},{2,10},{6,14},... | collective-permute-start | bytes 98312 | tf_op jit(solution)/shard_map/ppermute | solution.py:135

commit v3 on v1

--- a/solution.py
+++ b/solution.py
@@ -126,20 +126,46 @@
     return slots
 
 
-def ring_gather(own):
+def ring_gather(slots, hold):
     size = lax.axis_size("zh")
     right = [(i, (i + 1) % size) for i in range(size)]
     left = [(i, (i - 1) % size) for i in range(size)]
-    half = own.shape[0] // 2
-    arrived = []
-    up, down = own, own
+    ups, downs = list(slots), list(slots)
+    arrived = [(0, slot, value) for slot, value in enumerate(slots)]
     for step in range(1, size // 2):
-        up = lax.ppermute(up, "zh", right)
-        down = lax.ppermute(down, "zh", left)
-        arrived += [(size - step, 0, up), (step, 0, down)]
-    arrived.append((size // 2, 0, lax.ppermute(up[:half], "zh", right)))
-    arrived.append((size // 2, half, lax.ppermute(down[half:], "zh", left)))
+        for slot in range(len(slots)):
+            up = lax.ppermute(ups[slot], "zh", right)
+            down = lax.ppermute(downs[slot], "zh", left)
+            up, down = hold(step, slot, up, down)
+            arrived += [(size - step, slot, up), (step, slot, down)]
+            ups[slot], downs[slot] = up, down
+    for slot in range(len(slots)):
+        source, way = (ups, right) if slot % 2 == 0 else (downs, left)
+        arrived.append((size // 2, slot, lax.ppermute(source[slot], "zh", way)))
     return arrived
+
+
+class LevelSums:
+    def __init__(self):
+        self.state = None
+        self.sums = []
+
+    def step(self, *beside):
+        size = lax.axis_size("seq")
+        bit = len(self.sums)
+        if 1 << bit >= size:
+            return beside
+        self.state, *beside = lax.optimization_barrier((self.state, *beside))
+        other = lax.ppermute(self.state, "seq", [(i, i ^ (1 << bit)) for i in range(size)])
+        later = jnp.bitwise_and(jnp.right_shift(lax.axis_index("seq"), bit), 1) == 1
+        self.sums.append(jnp.where(later, other, 0.0))
+        self.state = self.state + other
+        return beside
+
+    def finish(self):
+        while 1 << len(self.sums) < lax.axis_size("seq"):
+            self.step()
+        return jnp.stack(self.sums)
 
 
 def product_store(place, count, blocks, zh, zl, a_refs, b_refs, store):
@@ -147,7 +173,7 @@
     for (away, first, slots), a_ref in zip(blocks, a_refs):
         group = lax.rem(zh + away, count)
         for slot in range(slots):
-            a = a_ref[slot]
+            a = a_ref[...]
             product = lax.dot_general(
                 a, b, (((0,), (0,)), ((), ())), preferred_element_type=jnp.float32
             ).astype(jnp.bfloat16)
@@ -204,8 +230,8 @@
     place = len(b_slots)
     rows, width = b_slots[0].shape
     where = jnp.stack([lax.axis_index("zh"), lax.axis_index("zl")]).astype(jnp.int32)
-    early_blocks = [(away, first, a.shape[0]) for away, first, a in early]
-    late_blocks = [(away, first, a.shape[0]) for away, first, a in late]
+    early_blocks = [(away, first, 1) for away, first, _ in early]
+    late_blocks = [(away, first, 1) for away, first, _ in late]
     count = sum(slots for _, _, slots in early_blocks)
     smem = pl.BlockSpec(memory_space=pltpu.SMEM)
     vmem = pl.BlockSpec(memory_space=pltpu.VMEM)
@@ -238,25 +264,6 @@
     table_rows = level_table.shape[0]
     own_index = lax.axis_index("seq")
 
-    own = jnp.stack(exchange(out_cotangent))
-    blocks = [(0, 0, own)] + ring_gather(own)
-
-    state = lax.dot_general(
-        keys, values, (((0,), (0,)), ((), ())), preferred_element_type=jnp.float32
-    )
-    states = lax.all_to_all(
-        jnp.broadcast_to(state, (n_seq, head_dim, head_dim)), "seq", 0, 0, tiled=True
-    )
-    source = jnp.arange(n_seq, dtype=jnp.int32)
-    apart = jnp.bitwise_xor(own_index, source)
-    select = jnp.stack(
-        [
-            ((jnp.right_shift(apart, level) == 1) & (source < own_index)).astype(jnp.float32)
-            for level in range(seq_bits)
-        ]
-    )
-    level_states = jnp.einsum("ji,ide->jde", select, states, precision=HIGHEST)
-
     onehot = (level_ids[:, None] == jnp.arange(table_rows, dtype=jnp.int32)[None, :]).astype(
         jnp.float32
     )
@@ -264,10 +271,30 @@
     pieces = [
         local_piece(piece, queries, keys, values, coeff) for piece in range(block_len // PIECE)
     ]
+
+    slots = exchange(out_cotangent)
+    *slots[1:], pieces[0] = lax.optimization_barrier((*slots[1:], pieces[0]))
+    level_sums = LevelSums()
+
+    def hold(step, slot, up, down):
+        if (step, slot) == (1, 0):
+            up, down, *rest = lax.optimization_barrier((up, down, keys, values))
+            level_sums.state = lax.dot_general(
+                *rest, (((0,), (0,)), ((), ())), preferred_element_type=jnp.float32
+            )
+            level_sums.step()
+        elif (step, slot) in ((1, 1), (2, 0), (2, 1)):
+            (up,) = level_sums.step(up)
+            if (step, slot) == (2, 0):
+                (down,) = level_sums.step(down)
+        return up, down
+
+    blocks = ring_gather(slots, hold)
+    level_states = level_sums.finish()
     attn_out = finish(pieces, queries, coeff, level_states, local_bits + 1)
 
     scale = (block_len * n_seq) ** (-0.5)
-    late = 4
+    late = 6
     partial = products(blocks[:-late], blocks[-late:], exchange(attn_out), lax.axis_size("zh"))
     sent = partial.reshape(-1, head_dim // 2, head_dim)
     arrived = lax.all_to_all(sent, ("seq", "zl"), 0, 0, tiled=True)

time: 159 us -> 158 us (level)
  starting transfers between devices: 54.6 us -> 82.9 us
  waiting for transfers between devices: 50.8 us -> 28.5 us
  matrix products: 6.01 us -> 1.3 us
  blocking collectives: 28.5 us -> 24.8 us
  local copies, waits for them, and re-layouts: 3.54 us -> 5.21 us
    ppermute x8 -> x19, starting transfers between devices: 37.7 us -> 78.3 us  [the longest x6 37.1 us: ring_gather(): down = lax.ppermute(downs[slot], 'zh', left)]
    ppermute x8 -> x19, waiting for transfers between devices: 41.6 us -> 20.2 us  [the longest x6 8.58 us: ring_gather(): up = lax.ppermute(ups[slot], 'zh', right)]
    all_to_all x1 -> x0, starting transfers between devices: 11.3 us -> none  [body(): lax.all_to_all(jnp.broadcast_to(state, (n_seq, head_dim, head_dim)), 'seq...]
    dot_general x2 -> x1, matrix products: 5.05 us -> 0.34 us  [hold(): lax.dot_general(*rest, (((0,), (0,)), ((), ())), preferred_element_type=j...]
    all_to_all x1, blocking collectives: 28.5 us -> 24.8 us  [body(): arrived = lax.all_to_all(sent, ('seq', 'zl'), 0, 0, tiled=True)]
    unnamed x24 -> x34, local copies, waits for them, and re-layouts: 0.76 us -> 2.9 us
  transfers between devices with their start and end apart: 11 -> 21, of which waited for: 9 -> 8; matrix products, arithmetic and copies ran while one was open for 4% -> 2% of each run, Pallas kernels for 7% -> 7%
where the time goes in v3:
time: 158 us
  starting transfers between devices  82.9 us (52%)
  waiting for transfers between devices  28.5 us (18%)
  blocking collectives  24.8 us (16%)
  Pallas kernels  12.5 us (8%)
  local copies, waits for them, and re-layouts  5.21 us (3%)
    ppermute x6, starting transfers between devices, ring_gather(): down = lax.ppermute(downs[slot], 'zh', left)  37.1 us
    all_to_all x1, blocking collectives, body(): arrived = lax.all_to_all(sent, ('seq', 'zl'), 0, 0, tiled=True)  24.8 us
    ppermute x5, starting transfers between devices, step(): lax.ppermute(self.state, 'seq', [(i, i ^ 1 << bit) for i in range(size)])  18.4 us
    ppermute x6, starting transfers between devices, ring_gather(): up = lax.ppermute(ups[slot], 'zh', right)  15.3 us
    ppermute x6, waiting for transfers between devices, ring_gather(): up = lax.ppermute(ups[slot], 'zh', right)  8.58 us
    ppermute x2, waiting for transfers between devices, exchange(): lax.ppermute(piece, 'zl', [(i, (i + apart) % size) for i in range(size)])  8.29 us
    ppermute x2, starting transfers between devices, ring_gather(): arrived.append((size // 2, slot, lax.ppermute(source[slot], 'zh', way)))  7.6 us
    pallas_call x4, Pallas kernels, local_piece(): pl.pallas_call(functools.partial(local_kernel, piece), out_shape=jax.Shap...  5.88 us
  transfers between devices with their start and end apart: 21, of which 8 were waited for; matrix products, arithmetic and copies ran while one was open for 2% of the time, Pallas kernels for 7%

profile of v3, /device:TPU:1, one launch (start us, length us, event | category | flops | bytes accessed | tf_op | source)
XLA Modules:
  0.0 157.5 jit_solution(17088620934273823813)
XLA Ops:
  0.6 0.0 copy-start
  0.6 0.0 copy-start.16
  0.7 1.2 constant_dynamic-slice_fusion.2
  1.9 5.7 %collective-permute-start.1 = (bf16[1024,128]{1,0:T(8,128)(2,1)S(1)}, bf16[1024,128]{1,0:T(8,128)(2,1)S(1)}, u32[]{:S(2)}, u32[]{:S(2)}) collective-permute-start(bf16[1024,128]{1,0:T(8,128)(2,1)S(1)} %get-tuple-element.34.refs_2_), channel_id=1, source_target_pairs={{0,2},{2,4},{4,6},{6,8},{8,10},{10,12},{12,14},{14,0},{1,3},{3,5},... | collective-permute-start | bytes 786440 | tf_op jit(solution)/shard_map/ppermute | solution.py:137
  7.6 8.6 %collective-permute-start.2 = (bf16[1024,128]{1,0:T(8,128)(2,1)S(1)}, bf16[1024,128]{1,0:T(8,128)(2,1)S(1)}, u32[]{:S(2)}, u32[]{:S(2)}) collective-permute-start(bf16[1024,128]{1,0:T(8,128)(2,1)S(1)} %get-tuple-element.34.refs_2_), channel_id=1, source_target_pairs={{0,14},{2,0},{4,2},{6,4},{8,6},{10,8},{12,10},{14,12},{1,15},{3,1}... | collective-permute-start | bytes 786440 | tf_op jit(solution)/shard_map/ppermute | solution.py:138
  16.2 2.6 %collective-permute-start = (bf16[1024,128]{1,0:T(8,128)(2,1)S(1)}, bf16[1024,128]{1,0:T(8,128)(2,1)}, u32[]{:S(2)}, u32[]{:S(2)}) collective-permute-start(bf16[1024,128]{1,0:T(8,128)(2,1)S(1)} %get-tuple-element.35), channel_id=1, source_target_pairs={{0,1},{1,0},{2,3},{3,2},{4,5},{5,4},{6,7},{7,6},{8,9},{9,8},{10,11... | collective-permute-start | bytes 786440 | tf_op jit(solution)/shard_map/ppermute | solution.py:125
  18.9 1.0 fusion.c_ref
  19.9 1.1 shard_map.77.l0
  21.0 0.8 collective-permute-done.1.refs_4_
  21.8 3.3 %collective-permute-done.2.refs_5_ = bf16[1024,128]{1,0:T(8,128)(2,1)S(1)} collective-permute-done((bf16[1024,128]{1,0:T(8,128)(2,1)S(1)}, bf16[1024,128]{1,0:T(8,128)(2,1)S(1)}, u32[]{:S(2)}, u32[]{:S(2)}) %collective-permute-start.2) | collective-permute-done | bytes 262176 | tf_op jit(solution)/shard_map/ppermute | solution.py:138
  25.1 8.3 %collective-permute-done.refs_3_ = bf16[1024,128]{1,0:T(8,128)(2,1)} collective-permute-done((bf16[1024,128]{1,0:T(8,128)(2,1)S(1)}, bf16[1024,128]{1,0:T(8,128)(2,1)}, u32[]{:S(2)}, u32[]{:S(2)}) %collective-permute-start) | collective-permute-done | bytes 262176 | tf_op jit(solution)/shard_map/ppermute | solution.py:125
  33.4 1.9 %collective-permute-start.4 = (bf16[1024,128]{1,0:T(8,128)(2,1)}, bf16[1024,128]{1,0:T(8,128)(2,1)}, u32[]{:S(2)}, u32[]{:S(2)}) collective-permute-start(bf16[1024,128]{1,0:T(8,128)(2,1)} %collective-permute-done.refs_3_), channel_id=1, source_target_pairs={{0,2},{2,4},{4,6},{6,8},{8,10},{10,12},{12,14},{14,0},{1,3},{3,5},... | collective-permute-start | bytes 786440 | tf_op jit(solution)/shard_map/ppermute | solution.py:137
  35.3 0.3 fusion.2
  35.7 2.8 %collective-permute-start.3 = (f32[128,128]{1,0:T(8,128)S(1)}, f32[128,128]{1,0:T(8,128)S(1)}, u32[]{:S(2)}, u32[]{:S(2)}) collective-permute-start(f32[128,128]{1,0:T(8,128)S(1)} %fusion.2), channel_id=1, source_target_pairs={{0,16},{16,0},{32,48},{48,32},{64,80},{80,64},{96,112},{112,96},{1... | collective-permute-start | bytes 196616 | tf_op jit(solution)/shard_map/ppermute | solution.py:159
  38.5 1.9 %shard_map.80.l3 = f32[512,128]{1,0:T(8,128)S(1)} custom-call(bf16[2048,128]{1,0:T(8,128)(2,1)S(1)} %copy-done.3, bf16[2048,128]{1,0:T(8,128)(2,1)S(1)} %copy-done.1, bf16[2048,128]{1,0:T(8,128)(2,1)S(1)} %copy-done.2, f32[2048,17]{1,0:T(8,128)S(1)} %fusion.c_ref), custom_call_target="tpu_custom_call" | custom-call | flops 536870912 | bytes 1048576 | tf_op jit(solution)/shard_map/pallas_call | solution.py:70
  40.4 1.2 shard_map.78.l1
  41.6 5.7 %collective-permute-start.13 = (bf16[1024,128]{1,0:T(8,128)(2,1)}, bf16[1024,128]{1,0:T(8,128)(2,1)S(1)}, u32[]{:S(2)}, u32[]{:S(2)}) collective-permute-start(bf16[1024,128]{1,0:T(8,128)(2,1)} %collective-permute-done.refs_3_), channel_id=1, source_target_pairs={{0,14},{2,0},{4,2},{6,4},{8,6},{10,8},{12,10},{14,12},{1,15},{3,1}... | collective-permute-start | bytes 786440 | tf_op jit(solution)/shard_map/ppermute | solution.py:138
  47.3 1.9 %collective-permute-start.6 = (bf16[1024,128]{1,0:T(8,128)(2,1)S(1)}, bf16[1024,128]{1,0:T(8,128)(2,1)S(1)}, u32[]{:S(2)}, u32[]{:S(2)}) collective-permute-start(bf16[1024,128]{1,0:T(8,128)(2,1)S(1)} %copy-done.5), channel_id=1, source_target_pairs={{0,2},{2,4},{4,6},{6,8},{8,10},{10,12},{12,14},{14,0},{1,3},{3,5},... | collective-permute-start | bytes 786440 | tf_op jit(solution)/shard_map/ppermute | solution.py:137
  49.3 1.7 %shard_map.79.l2 = f32[512,128]{1,0:T(8,128)S(1)} custom-call(bf16[2048,128]{1,0:T(8,128)(2,1)S(1)} %copy-done.3, bf16[2048,128]{1,0:T(8,128)(2,1)S(1)} %copy-done.1, bf16[2048,128]{1,0:T(8,128)(2,1)S(1)} %copy-done.2, f32[2048,17]{1,0:T(8,128)S(1)} %fusion.c_ref), custom_call_target="tpu_custom_call" | custom-call | flops 402653184 | bytes 786432 | tf_op jit(solution)/shard_map/pallas_call | solution.py:70
  50.9 5.5 %collective-permute-start.8 = (bf16[1024,128]{1,0:T(8,128)(2,1)S(1)}, bf16[1024,128]{1,0:T(8,128)(2,1)S(1)}, u32[]{:S(2)}, u32[]{:S(2)}) collective-permute-start(bf16[1024,128]{1,0:T(8,128)(2,1)S(1)} %copy-done.8), channel_id=1, source_target_pairs={{0,14},{2,0},{4,2},{6,4},{8,6},{10,8},{12,10},{14,12},{1,15},{3,1}... | collective-permute-start | bytes 786440 | tf_op jit(solution)/shard_map/ppermute | solution.py:138
  56.4 0.0 collective-permute-done.3
  56.5 0.0 collective-permute-done.4.refs_6_
  56.5 3.1 %collective-permute-start.5 = (f32[128,128]{1,0:T(8,128)S(1)}, f32[128,128]{1,0:T(8,128)S(1)}, u32[]{:S(2)}, u32[]{:S(2)}) collective-permute-start(f32[128,128]{1,0:T(8,128)S(1)} %add.27), channel_id=1, source_target_pairs={{0,32},{16,48},{32,0},{48,16},{64,96},{80,112},{96,64},{112,80},{1... | collective-permute-start | bytes 196616 | tf_op jit(solution)/shard_map/ppermute | solution.py:159
  59.6 1.9 %collective-permute-start.10 = (bf16[1024,128]{1,0:T(8,128)(2,1)}, bf16[1024,128]{1,0:T(8,128)(2,1)S(1)}, u32[]{:S(2)}, u32[]{:S(2)}) collective-permute-start(bf16[1024,128]{1,0:T(8,128)(2,1)} %collective-permute-done.4.refs_6_), channel_id=1, source_target_pairs={{0,2},{2,4},{4,6},{6,8},{8,10},{10,12},{12,14},{14,0},{1,3},{3,5},... | collective-permute-start | bytes 786440 | tf_op jit(solution)/shard_map/ppermute | solution.py:137
  61.5 0.0 collective-permute-done.13.refs_7_
  61.6 5.5 %collective-permute-start.14 = (bf16[1024,128]{1,0:T(8,128)(2,1)S(1)}, bf16[1024,128]{1,0:T(8,128)(2,1)S(1)}, u32[]{:S(2)}, u32[]{:S(2)}) collective-permute-start(bf16[1024,128]{1,0:T(8,128)(2,1)S(1)} %collective-permute-done.13.refs_7_), channel_id=1, source_target_pairs={{0,14},{2,0},{4,2},{6,4},{8,6},{10,8},{12,10},{14,12},{1,15},{3,1}... | collective-permute-start | bytes 786440 | tf_op jit(solution)/shard_map/ppermute | solution.py:138
  67.0 0.0 collective-permute-done.5
  67.1 0.0 collective-permute-done.6.refs_8_
  67.1 4.4 %collective-permute-start.7 = (f32[128,128]{1,0:T(8,128)S(1)}, f32[128,128]{1,0:T(8,128)S(1)}, u32[]{:S(2)}, u32[]{:S(2)}) collective-permute-start(f32[128,128]{1,0:T(8,128)S(1)} %add.28), channel_id=1, source_target_pairs={{0,64},{16,80},{32,96},{48,112},{64,0},{80,16},{96,32},{112,48},{1... | collective-permute-start | bytes 196616 | tf_op jit(solution)/shard_map/ppermute | solution.py:159
  71.5 1.9 %collective-permute-start.15 = (bf16[1024,128]{1,0:T(8,128)(2,1)S(1)}, bf16[1024,128]{1,0:T(8,128)(2,1)}, u32[]{:S(2)}, u32[]{:S(2)}) collective-permute-start(bf16[1024,128]{1,0:T(8,128)(2,1)S(1)} %collective-permute-done.6.refs_8_), channel_id=1, source_target_pairs={{0,2},{2,4},{4,6},{6,8},{8,10},{10,12},{12,14},{14,0},{1,3},{3,5},... | collective-permute-start | bytes 786440 | tf_op jit(solution)/shard_map/ppermute | solution.py:137
  73.4 0.5 collective-permute-done.7
  73.9 0.0 collective-permute-done.8.refs_9_
  73.9 3.2 %collective-permute-start.9 = (f32[128,128]{1,0:T(8,128)S(1)}, f32[128,128]{1,0:T(8,128)S(1)}, u32[]{:S(2)}, u32[]{:S(2)}) collective-permute-start(f32[128,128]{1,0:T(8,128)S(1)} %add.29), channel_id=1, source_target_pairs={{0,128},{16,144},{32,160},{48,176},{64,192},{80,208},{96,224},{112... | collective-permute-start | bytes 196616 | tf_op jit(solution)/shard_map/ppermute | solution.py:159
  77.2 2.1 %collective-permute-done.9 = f32[128,128]{1,0:T(8,128)S(1)} collective-permute-done((f32[128,128]{1,0:T(8,128)S(1)}, f32[128,128]{1,0:T(8,128)S(1)}, u32[]{:S(2)}, u32[]{:S(2)}) %collective-permute-start.9) | collective-permute-done | bytes 65568 | tf_op jit(solution)/shard_map/ppermute | solution.py:159
  79.2 0.0 collective-permute-done.10.refs_10_
  79.3 4.8 %collective-permute-start.11 = (f32[128,128]{1,0:T(8,128)S(1)}, f32[128,128]{1,0:T(8,128)S(1)}, u32[]{:S(2)}, u32[]{:S(2)}) collective-permute-start(f32[128,128]{1,0:T(8,128)S(1)} %add.30), channel_id=1, source_target_pairs={{0,256},{16,272},{32,288},{48,304},{64,320},{80,336},{96,352},{112... | collective-permute-start | bytes 196616 | tf_op jit(solution)/shard_map/ppermute | solution.py:159
  84.1 0.2 collective-permute-done.14.refs_11_
  84.3 4.8 %collective-permute-start.18 = (bf16[1024,128]{1,0:T(8,128)(2,1)S(1)}, bf16[1024,128]{1,0:T(8,128)(2,1)}, u32[]{:S(2)}, u32[]{:S(2)}) collective-permute-start(bf16[1024,128]{1,0:T(8,128)(2,1)S(1)} %collective-permute-done.14.refs_11_), channel_id=1, source_target_pairs={{0,14},{2,0},{4,2},{6,4},{8,6},{10,8},{12,10},{14,12},{1,15},{3,1}... | collective-permute-start | bytes 786440 | tf_op jit(solution)/shard_map/ppermute | solution.py:138
  89.1 0.0 collective-permute-done.11
  89.2 0.1 subtract_convert_fusion
  89.2 3.0 %shard_map.81 = bf16[2048,128]{1,0:T(8,128)(2,1)} custom-call(f32[512,128]{1,0:T(8,128)S(1)} %shard_map.77.l0, f32[512,128]{1,0:T(8,128)S(1)} %shard_map.78.l1, f32[512,128]{1,0:T(8,128)S(1)} %shard_map.79.l2, f32[512,128]{1,0:T(8,128)S(1)} %shard_map.80.l3, bf16[2048,128]{1,0:T(8,128)(2,1)S(1)} %copy-done.3, f32[2048,17]{1,0:T(8,128)S(1)} %fusion.c_ref, ...), custom_call_target="tpu_custom_call" | custom-call | flops 671088640 | bytes 4194304 | tf_op jit(solution)/shard_map/pallas_call | solution.py:107
  92.2 1.1 constant_dynamic-slice_fusion
  93.3 1.9 %collective-permute-start.12 = (bf16[1024,128]{1,0:T(8,128)(2,1)S(1)}, bf16[1024,128]{1,0:T(8,128)(2,1)S(1)}, u32[]{:S(2)}, u32[]{:S(2)}) collective-permute-start(bf16[1024,128]{1,0:T(8,128)(2,1)S(1)} %get-tuple-element.32), channel_id=1, source_target_pairs={{0,1},{1,0},{2,3},{3,2},{4,5},{5,4},{6,7},{7,6},{8,9},{9,8},{10,11... | collective-permute-start | bytes 786440 | tf_op jit(solution)/shard_map/ppermute | solution.py:125
  95.3 7.0 %collective-permute-start.16 = (bf16[1024,128]{1,0:T(8,128)(2,1)S(1)}, bf16[1024,128]{1,0:T(8,128)(2,1)S(1)}, u32[]{:S(2)}, u32[]{:S(2)}) collective-permute-start(bf16[1024,128]{1,0:T(8,128)(2,1)S(1)} %collective-permute-done.8.refs_9_), channel_id=1, source_target_pairs={{0,14},{2,0},{4,2},{6,4},{8,6},{10,8},{12,10},{14,12},{1,15},{3,1}... | collective-permute-start | bytes 786440 | tf_op jit(solution)/shard_map/ppermute | solution.py:138
  102.3 1.9 %collective-permute-start.17 = (bf16[1024,128]{1,0:T(8,128)(2,1)S(1)}, bf16[1024,128]{1,0:T(8,128)(2,1)S(1)}, u32[]{:S(2)}, u32[]{:S(2)}) collective-permute-start(bf16[1024,128]{1,0:T(8,128)(2,1)S(1)} %collective-permute-done.10.refs_10_), channel_id=1, source_target_pairs={{0,2},{2,4},{4,6},{6,8},{8,10},{10,12},{12,14},{14,0},{1,3},{3,5},... | collective-permute-start | bytes 786440 | tf_op jit(solution)/shard_map/ppermute | solution.py:137
  104.2 0.0 collective-permute-done.15.refs_2_
  104.2 2.2 %collective-permute-start.19 = (bf16[1024,128]{1,0:T(8,128)(2,1)}, bf16[1024,128]{1,0:T(8,128)(2,1)S(1)}, u32[]{:S(2)}, u32[]{:S(2)}) collective-permute-start(bf16[1024,128]{1,0:T(8,128)(2,1)} %collective-permute-done.15.refs_2_), channel_id=1, source_target_pairs={{0,2},{2,4},{4,6},{6,8},{8,10},{10,12},{12,14},{14,0},{1,3},{3,5},... | collective-permute-start | bytes 786440 | tf_op jit(solution)/shard_map/ppermute | solution.py:144
  106.4 0.0 collective-permute-done.18.refs_5_
  106.4 5.4 %collective-permute-start.20 = (bf16[1024,128]{1,0:T(8,128)(2,1)}, bf16[1024,128]{1,0:T(8,128)(2,1)S(1)}, u32[]{:S(2)}, u32[]{:S(2)}) collective-permute-start(bf16[1024,128]{1,0:T(8,128)(2,1)} %collective-permute-done.18.refs_5_), channel_id=1, source_target_pairs={{0,14},{2,0},{4,2},{6,4},{8,6},{10,8},{12,10},{14,12},{1,15},{3,1}... | collective-permute-start | bytes 786440 | tf_op jit(solution)/shard_map/ppermute | solution.py:144
  111.8 0.1 pad_add_fusion.where_ref
  111.9 0.0 collective-permute-done.12.refs_1_
  111.9 0.0 copy-done.6
  111.9 0.9 copy-done.11
  112.9 0.9 copy-done.13
  113.8 0.9 copy-done.15
  114.8 2.0 %shard_map.82.early_ref = bf16[10,128,256]{2,1,0:T(8,128)(2,1)S(1)} custom-call(s32[2]{0:T(128)S(1)} %pad_add_fusion.where_ref, bf16[1024,128]{1,0:T(8,128)(2,1)S(1)} %get-tuple-element.33.refs_0_, bf16[1024,128]{1,0:T(8,128)(2,1)S(1)} %collective-permute-done.12.refs_1_, bf16[1024,128]{1,0:T(8,128)(2,1)S(1)} %get-tuple-element.34.refs_2_, ...), custom_call_target="tpu_custom_call" | custom-call | flops 671088640 | bytes 3145728 | tf_op jit(solution)/shard_map/pallas_call | solution.py:239
  116.8 0.0 collective-permute-done.16.refs_3_
  116.8 7.8 %collective-permute-done.17.refs_4_ = bf16[1024,128]{1,0:T(8,128)(2,1)S(1)} collective-permute-done((bf16[1024,128]{1,0:T(8,128)(2,1)S(1)}, bf16[1024,128]{1,0:T(8,128)(2,1)S(1)}, u32[]{:S(2)}, u32[]{:S(2)}) %collective-permute-start.17) | collective-permute-done | bytes 262176 | tf_op jit(solution)/shard_map/ppermute | solution.py:137
  124.6 5.6 %collective-permute-done.19.refs_6_ = bf16[1024,128]{1,0:T(8,128)(2,1)S(1)} collective-permute-done((bf16[1024,128]{1,0:T(8,128)(2,1)}, bf16[1024,128]{1,0:T(8,128)(2,1)S(1)}, u32[]{:S(2)}, u32[]{:S(2)}) %collective-permute-start.19) | collective-permute-done | bytes 262176 | tf_op jit(solution)/shard_map/ppermute | solution.py:144
  130.2 0.0 collective-permute-done.20.refs_7_
  130.2 1.7 %shard_map.83 = bf16[16,2,2,64,128]{4,3,2,1,0:T(8,128)(2,1)S(1)} custom-call(s32[2]{0:T(128)S(1)} %pad_add_fusion.where_ref, bf16[10,128,256]{2,1,0:T(8,128)(2,1)S(1)} %shard_map.82.early_ref, bf16[1024,128]{1,0:T(8,128)(2,1)S(1)} %get-tuple-element.33.refs_0_, bf16[1024,128]{1,0:T(8,128)(2,1)S(1)} %collective-permute-done.12.refs_1_, ...), custom_call_target="tpu_custom_call" | custom-call | flops 402653184 | bytes 2097152 | tf_op jit(solution)/shard_map/pallas_call | solution.py:247
  131.9 24.8 %all_to_all.5 = bf16[64,64,128]{2,1,0:T(8,128)(2,1)S(1)} all-to-all(bf16[64,64,128]{2,1,0:T(8,128)(2,1)S(1)} %bitcast.16), channel_id=1, replica_groups=mesh['seq'=32,'zh'=8,'zl'=2] {'seq','zl'}, dimensions={0} | all-to-all | bytes 2097152 | tf_op jit(solution)/shard_map/all_to_all | solution.py:300
  156.7 0.2 convert_reduce_fusion
  156.9 0.6 broadcast_multiply_fusion
  (37 shorter events, 0.1 us)
Async XLA Ops:
  0.6 18.2 %copy-start = (f32[64,17]{0,1:T(8,128)S(1)}, f32[64,17]{0,1:T(8,128)}, u32[]{:S(2)}) copy-start(f32[64,17]{0,1:T(8,128)} %param.10) | copy-start | bytes 13060
  0.6 18.2 %copy-start.16 = (s32[2048]{0:T(1024)S(1)}, s32[2048]{0:T(1024)}, u32[]{:S(2)}) copy-start(s32[2048]{0:T(1024)} %param.9) | copy-start | bytes 24580
  0.7 19.2 %copy-start.1 = (bf16[2048,128]{1,0:T(8,128)(2,1)S(1)}, bf16[2048,128]{1,0:T(8,128)(2,1)}, u32[]{:S(2)}) copy-start(bf16[2048,128]{1,0:T(8,128)(2,1)} %k_ref.7) | copy-start | bytes 1572868
  0.7 19.2 %copy-start.2 = (bf16[2048,128]{1,0:T(8,128)(2,1)S(1)}, bf16[2048,128]{1,0:T(8,128)(2,1)}, u32[]{:S(2)}) copy-start(bf16[2048,128]{1,0:T(8,128)(2,1)} %v_ref.7) | copy-start | bytes 1572868
  0.7 19.2 %copy-start.3 = (bf16[2048,128]{1,0:T(8,128)(2,1)S(1)}, bf16[2048,128]{1,0:T(8,128)(2,1)}, u32[]{:S(2)}) copy-start(bf16[2048,128]{1,0:T(8,128)(2,1)} %q_ref.9) | copy-start | bytes 1572868
  1.9 19.9 %collective-permute-start.1 = (bf16[1024,128]{1,0:T(8,128)(2,1)S(1)}, bf16[1024,128]{1,0:T(8,128)(2,1)S(1)}, u32[]{:S(2)}, u32[]{:S(2)}) collective-permute-start(bf16[1024,128]{1,0:T(8,128)(2,1)S(1)} %get-tuple-element.34.refs_2_), channel_id=1, source_target_pairs={{0,2},{2,4},{4,6},{6,8},{8,10},{10,12},{12,14},{14,0},{1,3},{3,5},... | collective-permute-start | bytes 786440 | tf_op jit(solution)/shard_map/ppermute | solution.py:137
  7.6 17.5 %collective-permute-start.2 = (bf16[1024,128]{1,0:T(8,128)(2,1)S(1)}, bf16[1024,128]{1,0:T(8,128)(2,1)S(1)}, u32[]{:S(2)}, u32[]{:S(2)}) collective-permute-start(bf16[1024,128]{1,0:T(8,128)(2,1)S(1)} %get-tuple-element.34.refs_2_), channel_id=1, source_target_pairs={{0,14},{2,0},{4,2},{6,4},{8,6},{10,8},{12,10},{14,12},{1,15},{3,1}... | collective-permute-start | bytes 786440 | tf_op jit(solution)/shard_map/ppermute | solution.py:138
  16.2 17.2 %collective-permute-start = (bf16[1024,128]{1,0:T(8,128)(2,1)S(1)}, bf16[1024,128]{1,0:T(8,128)(2,1)}, u32[]{:S(2)}, u32[]{:S(2)}) collective-permute-start(bf16[1024,128]{1,0:T(8,128)(2,1)S(1)} %get-tuple-element.35), channel_id=1, source_target_pairs={{0,1},{1,0},{2,3},{3,2},{4,5},{5,4},{6,7},{7,6},{8,9},{9,8},{10,11... | collective-permute-start | bytes 786440 | tf_op jit(solution)/shard_map/ppermute | solution.py:125
  21.8 13.8 %copy-start.4 = (bf16[1024,128]{1,0:T(8,128)(2,1)}, bf16[1024,128]{1,0:T(8,128)(2,1)S(1)}, u32[]{:S(2)}) copy-start(bf16[1024,128]{1,0:T(8,128)(2,1)S(1)} %collective-permute-done.1.refs_4_) | copy-start | bytes 786436
  25.1 13.4 %copy-start.7 = (bf16[1024,128]{1,0:T(8,128)(2,1)}, bf16[1024,128]{1,0:T(8,128)(2,1)S(1)}, u32[]{:S(2)}) copy-start(bf16[1024,128]{1,0:T(8,128)(2,1)S(1)} %collective-permute-done.2.refs_5_) | copy-start | bytes 786436
  33.4 23.1 %collective-permute-start.4 = (bf16[1024,128]{1,0:T(8,128)(2,1)}, bf16[1024,128]{1,0:T(8,128)(2,1)}, u32[]{:S(2)}, u32[]{:S(2)}) collective-permute-start(bf16[1024,128]{1,0:T(8,128)(2,1)} %collective-permute-done.refs_3_), channel_id=1, source_target_pairs={{0,2},{2,4},{4,6},{6,8},{8,10},{10,12},{12,14},{14,0},{1,3},{3,5},... | collective-permute-start | bytes 786440 | tf_op jit(solution)/shard_map/ppermute | solution.py:137
  35.7 20.8 %collective-permute-start.3 = (f32[128,128]{1,0:T(8,128)S(1)}, f32[128,128]{1,0:T(8,128)S(1)}, u32[]{:S(2)}, u32[]{:S(2)}) collective-permute-start(f32[128,128]{1,0:T(8,128)S(1)} %fusion.2), channel_id=1, source_target_pairs={{0,16},{16,0},{32,48},{48,32},{64,80},{80,64},{96,112},{112,96},{1... | collective-permute-start | bytes 196616 | tf_op jit(solution)/shard_map/ppermute | solution.py:159
  40.4 6.9 %copy-start.5 = (bf16[1024,128]{1,0:T(8,128)(2,1)S(1)}, bf16[1024,128]{1,0:T(8,128)(2,1)}, u32[]{:S(2)}) copy-start(bf16[1024,128]{1,0:T(8,128)(2,1)} %copy-done.4) | copy-start | bytes 786436
  41.6 9.3 %copy-start.8 = (bf16[1024,128]{1,0:T(8,128)(2,1)S(1)}, bf16[1024,128]{1,0:T(8,128)(2,1)}, u32[]{:S(2)}) copy-start(bf16[1024,128]{1,0:T(8,128)(2,1)} %copy-done.7) | copy-start | bytes 786436
  41.6 19.9 %collective-permute-start.13 = (bf16[1024,128]{1,0:T(8,128)(2,1)}, bf16[1024,128]{1,0:T(8,128)(2,1)S(1)}, u32[]{:S(2)}, u32[]{:S(2)}) collective-permute-start(bf16[1024,128]{1,0:T(8,128)(2,1)} %collective-permute-done.refs_3_), channel_id=1, source_target_pairs={{0,14},{2,0},{4,2},{6,4},{8,6},{10,8},{12,10},{14,12},{1,15},{3,1}... | collective-permute-start | bytes 786440 | tf_op jit(solution)/shard_map/ppermute | solution.py:138
  47.3 19.7 %collective-permute-start.6 = (bf16[1024,128]{1,0:T(8,128)(2,1)S(1)}, bf16[1024,128]{1,0:T(8,128)(2,1)S(1)}, u32[]{:S(2)}, u32[]{:S(2)}) collective-permute-start(bf16[1024,128]{1,0:T(8,128)(2,1)S(1)} %copy-done.5), channel_id=1, source_target_pairs={{0,2},{2,4},{4,6},{6,8},{8,10},{10,12},{12,14},{14,0},{1,3},{3,5},... | collective-permute-start | bytes 786440 | tf_op jit(solution)/shard_map/ppermute | solution.py:137
  50.9 23.0 %collective-permute-start.8 = (bf16[1024,128]{1,0:T(8,128)(2,1)S(1)}, bf16[1024,128]{1,0:T(8,128)(2,1)S(1)}, u32[]{:S(2)}, u32[]{:S(2)}) collective-permute-start(bf16[1024,128]{1,0:T(8,128)(2,1)S(1)} %copy-done.8), channel_id=1, source_target_pairs={{0,14},{2,0},{4,2},{6,4},{8,6},{10,8},{12,10},{14,12},{1,15},{3,1}... | collective-permute-start | bytes 786440 | tf_op jit(solution)/shard_map/ppermute | solution.py:138
  56.5 10.6 %collective-permute-start.5 = (f32[128,128]{1,0:T(8,128)S(1)}, f32[128,128]{1,0:T(8,128)S(1)}, u32[]{:S(2)}, u32[]{:S(2)}) collective-permute-start(f32[128,128]{1,0:T(8,128)S(1)} %add.27), channel_id=1, source_target_pairs={{0,32},{16,48},{32,0},{48,16},{64,96},{80,112},{96,64},{112,80},{1... | collective-permute-start | bytes 196616 | tf_op jit(solution)/shard_map/ppermute | solution.py:159
  59.6 19.6 %collective-permute-start.10 = (bf16[1024,128]{1,0:T(8,128)(2,1)}, bf16[1024,128]{1,0:T(8,128)(2,1)S(1)}, u32[]{:S(2)}, u32[]{:S(2)}) collective-permute-start(bf16[1024,128]{1,0:T(8,128)(2,1)} %collective-permute-done.4.refs_6_), channel_id=1, source_target_pairs={{0,2},{2,4},{4,6},{6,8},{8,10},{10,12},{12,14},{14,0},{1,3},{3,5},... | collective-permute-start | bytes 786440 | tf_op jit(solution)/shard_map/ppermute | solution.py:137
  61.6 30.6 %copy-start.10 = (bf16[1024,128]{1,0:T(8,128)(2,1)}, bf16[1024,128]{1,0:T(8,128)(2,1)S(1)}, u32[]{:S(2)}) copy-start(bf16[1024,128]{1,0:T(8,128)(2,1)S(1)} %collective-permute-done.13.refs_7_) | copy-start | bytes 786436
  61.6 22.7 %collective-permute-start.14 = (bf16[1024,128]{1,0:T(8,128)(2,1)S(1)}, bf16[1024,128]{1,0:T(8,128)(2,1)S(1)}, u32[]{:S(2)}, u32[]{:S(2)}) collective-permute-start(bf16[1024,128]{1,0:T(8,128)(2,1)S(1)} %collective-permute-done.13.refs_7_), channel_id=1, source_target_pairs={{0,14},{2,0},{4,2},{6,4},{8,6},{10,8},{12,10},{14,12},{1,15},{3,1}... | collective-permute-start | bytes 786440 | tf_op jit(solution)/shard_map/ppermute | solution.py:138
  67.1 25.1 %copy-start.12 = (bf16[1024,128]{1,0:T(8,128)(2,1)}, bf16[1024,128]{1,0:T(8,128)(2,1)S(1)}, u32[]{:S(2)}) copy-start(bf16[1024,128]{1,0:T(8,128)(2,1)S(1)} %collective-permute-done.6.refs_8_) | copy-start | bytes 786436
  67.1 6.8 %collective-permute-start.7 = (f32[128,128]{1,0:T(8,128)S(1)}, f32[128,128]{1,0:T(8,128)S(1)}, u32[]{:S(2)}, u32[]{:S(2)}) collective-permute-start(f32[128,128]{1,0:T(8,128)S(1)} %add.28), channel_id=1, source_target_pairs={{0,64},{16,80},{32,96},{48,112},{64,0},{80,16},{96,32},{112,48},{1... | collective-permute-start | bytes 196616 | tf_op jit(solution)/shard_map/ppermute | solution.py:159
  71.5 32.7 %collective-permute-start.15 = (bf16[1024,128]{1,0:T(8,128)(2,1)S(1)}, bf16[1024,128]{1,0:T(8,128)(2,1)}, u32[]{:S(2)}, u32[]{:S(2)}) collective-permute-start(bf16[1024,128]{1,0:T(8,128)(2,1)S(1)} %collective-permute-done.6.refs_8_), channel_id=1, source_target_pairs={{0,2},{2,4},{4,6},{6,8},{8,10},{10,12},{12,14},{14,0},{1,3},{3,5},... | collective-permute-start | bytes 786440 | tf_op jit(solution)/shard_map/ppermute | solution.py:137
  73.9 5.3 %collective-permute-start.9 = (f32[128,128]{1,0:T(8,128)S(1)}, f32[128,128]{1,0:T(8,128)S(1)}, u32[]{:S(2)}, u32[]{:S(2)}) collective-permute-start(f32[128,128]{1,0:T(8,128)S(1)} %add.29), channel_id=1, source_target_pairs={{0,128},{16,144},{32,160},{48,176},{64,192},{80,208},{96,224},{112... | collective-permute-start | bytes 196616 | tf_op jit(solution)/shard_map/ppermute | solution.py:159
  79.3 9.9 %collective-permute-start.11 = (f32[128,128]{1,0:T(8,128)S(1)}, f32[128,128]{1,0:T(8,128)S(1)}, u32[]{:S(2)}, u32[]{:S(2)}) collective-permute-start(f32[128,128]{1,0:T(8,128)S(1)} %add.30), channel_id=1, source_target_pairs={{0,256},{16,272},{32,288},{48,304},{64,320},{80,336},{96,352},{112... | collective-permute-start | bytes 196616 | tf_op jit(solution)/shard_map/ppermute | solution.py:159
  84.3 7.9 %copy-start.14 = (bf16[1024,128]{1,0:T(8,128)(2,1)}, bf16[1024,128]{1,0:T(8,128)(2,1)S(1)}, u32[]{:S(2)}) copy-start(bf16[1024,128]{1,0:T(8,128)(2,1)S(1)} %collective-permute-done.14.refs_11_) | copy-start | bytes 786436
  84.3 22.1 %collective-permute-start.18 = (bf16[1024,128]{1,0:T(8,128)(2,1)S(1)}, bf16[1024,128]{1,0:T(8,128)(2,1)}, u32[]{:S(2)}, u32[]{:S(2)}) collective-permute-start(bf16[1024,128]{1,0:T(8,128)(2,1)S(1)} %collective-permute-done.14.refs_11_), channel_id=1, source_target_pairs={{0,14},{2,0},{4,2},{6,4},{8,6},{10,8},{12,10},{14,12},{1,15},{3,1}... | collective-permute-start | bytes 786440 | tf_op jit(solution)/shard_map/ppermute | solution.py:138
  92.2 19.7 %copy-start.6 = (bf16[1024,128]{1,0:T(8,128)(2,1)S(1)}, bf16[1024,128]{1,0:T(8,128)(2,1)}, u32[]{:S(2)}) copy-start(bf16[1024,128]{1,0:T(8,128)(2,1)} %copy-done.4) | copy-start | bytes 786436
  92.2 19.7 %copy-start.9 = (bf16[1024,128]{1,0:T(8,128)(2,1)S(1)}, bf16[1024,128]{1,0:T(8,128)(2,1)}, u32[]{:S(2)}) copy-start(bf16[1024,128]{1,0:T(8,128)(2,1)} %copy-done.7) | copy-start | bytes 786436
  93.3 18.6 %collective-permute-start.12 = (bf16[1024,128]{1,0:T(8,128)(2,1)S(1)}, bf16[1024,128]{1,0:T(8,128)(2,1)S(1)}, u32[]{:S(2)}, u32[]{:S(2)}) collective-permute-start(bf16[1024,128]{1,0:T(8,128)(2,1)S(1)} %get-tuple-element.32), channel_id=1, source_target_pairs={{0,1},{1,0},{2,3},{3,2},{4,5},{5,4},{6,7},{7,6},{8,9},{9,8},{10,11... | collective-permute-start | bytes 786440 | tf_op jit(solution)/shard_map/ppermute | solution.py:125
  95.3 21.5 %collective-permute-start.16 = (bf16[1024,128]{1,0:T(8,128)(2,1)S(1)}, bf16[1024,128]{1,0:T(8,128)(2,1)S(1)}, u32[]{:S(2)}, u32[]{:S(2)}) collective-permute-start(bf16[1024,128]{1,0:T(8,128)(2,1)S(1)} %collective-permute-done.8.refs_9_), channel_id=1, source_target_pairs={{0,14},{2,0},{4,2},{6,4},{8,6},{10,8},{12,10},{14,12},{1,15},{3,1}... | collective-permute-start | bytes 786440 | tf_op jit(solution)/shard_map/ppermute | solution.py:138
  102.3 22.3 %collective-permute-start.17 = (bf16[1024,128]{1,0:T(8,128)(2,1)S(1)}, bf16[1024,128]{1,0:T(8,128)(2,1)S(1)}, u32[]{:S(2)}, u32[]{:S(2)}) collective-permute-start(bf16[1024,128]{1,0:T(8,128)(2,1)S(1)} %collective-permute-done.10.refs_10_), channel_id=1, source_target_pairs={{0,2},{2,4},{4,6},{6,8},{8,10},{10,12},{12,14},{14,0},{1,3},{3,5},... | collective-permute-start | bytes 786440 | tf_op jit(solution)/shard_map/ppermute | solution.py:137
  104.2 26.0 %collective-permute-start.19 = (bf16[1024,128]{1,0:T(8,128)(2,1)}, bf16[1024,128]{1,0:T(8,128)(2,1)S(1)}, u32[]{:S(2)}, u32[]{:S(2)}) collective-permute-start(bf16[1024,128]{1,0:T(8,128)(2,1)} %collective-permute-done.15.refs_2_), channel_id=1, source_target_pairs={{0,2},{2,4},{4,6},{6,8},{8,10},{10,12},{12,14},{14,0},{1,3},{3,5},... | collective-permute-start | bytes 786440 | tf_op jit(solution)/shard_map/ppermute | solution.py:144
  106.4 23.8 %collective-permute-start.20 = (bf16[1024,128]{1,0:T(8,128)(2,1)}, bf16[1024,128]{1,0:T(8,128)(2,1)S(1)}, u32[]{:S(2)}, u32[]{:S(2)}) collective-permute-start(bf16[1024,128]{1,0:T(8,128)(2,1)} %collective-permute-done.18.refs_5_), channel_id=1, source_target_pairs={{0,14},{2,0},{4,2},{6,4},{8,6},{10,8},{12,10},{14,12},{1,15},{3,1}... | collective-permute-start | bytes 786440 | tf_op jit(solution)/shard_map/ppermute | solution.py:144
  111.9 1.0 copy-start.11
  112.9 0.9 copy-start.13
  113.8 0.9 copy-start.15

commit v4 on v3

--- a/solution.py
+++ b/solution.py
@@ -273,7 +273,7 @@
     ]
 
     slots = exchange(out_cotangent)
-    *slots[1:], pieces[0] = lax.optimization_barrier((*slots[1:], pieces[0]))
+    slots[0], *slots[1:] = lax.optimization_barrier(tuple(slots))
     level_sums = LevelSums()
 
     def hold(step, slot, up, down):

time: 158 us -> 164 us (1.038)
  starting transfers between devices: 82.9 us -> 89.1 us
  blocking collectives: 24.8 us -> 28.5 us
  waiting for transfers between devices: 28.5 us -> 25.5 us
    ppermute x6, starting transfers between devices: 37.1 us -> 24.6 us  [ring_gather(): down = lax.ppermute(downs[slot], 'zh', left)]
    ppermute x6, starting transfers between devices: 15.3 us -> 25.3 us  [ring_gather(): up = lax.ppermute(ups[slot], 'zh', right)]
    ppermute x6, waiting for transfers between devices: 8.58 us -> 0.02 us  [ring_gather(): up = lax.ppermute(ups[slot], 'zh', right)]
    ppermute x2, starting transfers between devices: 4.57 us -> 11.9 us  [exchange(): lax.ppermute(piece, 'zl', [(i, (i + apart) % size) for i in range(size)])]
    ppermute x2, waiting for transfers between devices: 5.62 us -> 11.3 us  [ring_gather(): arrived.append((size // 2, slot, lax.ppermute(source[slot], 'zh', way)))]
    ppermute x2, waiting for transfers between devices: 8.29 us -> 3.85 us  [exchange(): lax.ppermute(piece, 'zl', [(i, (i + apart) % size) for i in range(size)])]
    all_to_all x1, blocking collectives: 24.8 us -> 28.5 us  [body(): arrived = lax.all_to_all(sent, ('seq', 'zl'), 0, 0, tiled=True)]
    ppermute x6, waiting for transfers between devices: 3.46 us -> 6.54 us  [ring_gather(): down = lax.ppermute(downs[slot], 'zh', left)]
  transfers between devices with their start and end apart: 21 -> 21, of which waited for: 8 -> 6; matrix products, arithmetic and copies ran while one was open for 2% -> 2% of each run, Pallas kernels for 7% -> 7%
where the time goes in v4:
time: 164 us; the launch traced here: 163 us
  starting transfers between devices  89.1 us (54%)
  blocking collectives  28.5 us (17%)
  waiting for transfers between devices  25.5 us (16%)
  Pallas kernels  12.7 us (8%)
  local copies, waits for them, and re-layouts  3.65 us (2%)
    all_to_all x1, blocking collectives, body(): arrived = lax.all_to_all(sent, ('seq', 'zl'), 0, 0, tiled=True)  28.5 us
    ppermute x6, starting transfers between devices, ring_gather(): up = lax.ppermute(ups[slot], 'zh', right)  25.3 us
    ppermute x6, starting transfers between devices, ring_gather(): down = lax.ppermute(downs[slot], 'zh', left)  24.6 us
    ppermute x5, starting transfers between devices, step(): lax.ppermute(self.state, 'seq', [(i, i ^ 1 << bit) for i in range(size)])  19.8 us
    ppermute x2, starting transfers between devices, exchange(): lax.ppermute(piece, 'zl', [(i, (i + apart) % size) for i in range(size)])  11.9 us
    ppermute x2, waiting for transfers between devices, ring_gather(): arrived.append((size // 2, slot, lax.ppermute(source[slot], 'zh', way)))  11.3 us
    ppermute x2, starting transfers between devices, ring_gather(): arrived.append((size // 2, slot, lax.ppermute(source[slot], 'zh', way)))  7.39 us
    ppermute x6, waiting for transfers between devices, ring_gather(): down = lax.ppermute(downs[slot], 'zh', left)  6.54 us
  transfers between devices with their start and end apart: 21, of which 6 were waited for; matrix products, arithmetic and copies ran while one was open for 2% of the time, Pallas kernels for 7%

profile of v4, /device:TPU:1, one launch (start us, length us, event | category | flops | bytes accessed | tf_op | source)
XLA Modules:
  0.0 163.0 jit_solution(17896344285335868524)
XLA Ops:
  0.6 0.0 copy-start
  0.6 0.0 copy-start.12
  0.7 0.0 copy-start.1
  0.7 0.0 copy-start.2
  0.7 1.2 constant_dynamic-slice_fusion.2
  1.9 4.4 %collective-permute-start = (bf16[1024,128]{1,0:T(8,128)(2,1)S(1)}, bf16[1024,128]{1,0:T(8,128)(2,1)}, u32[]{:S(2)}, u32[]{:S(2)}) collective-permute-start(bf16[1024,128]{1,0:T(8,128)(2,1)S(1)} %get-tuple-element.34), channel_id=1, source_target_pairs={{0,1},{1,0},{2,3},{3,2},{4,5},{5,4},{6,7},{7,6},{8,9},{9,8},{10,11... | collective-permute-start | bytes 786440 | tf_op jit(solution)/shard_map/ppermute | solution.py:125
  6.3 3.9 %collective-permute-done.refs_3_ = bf16[1024,128]{1,0:T(8,128)(2,1)} collective-permute-done((bf16[1024,128]{1,0:T(8,128)(2,1)S(1)}, bf16[1024,128]{1,0:T(8,128)(2,1)}, u32[]{:S(2)}, u32[]{:S(2)}) %collective-permute-start) | collective-permute-done | bytes 262176 | tf_op jit(solution)/shard_map/ppermute | solution.py:125
  10.1 7.0 %collective-permute-start.1 = (bf16[1024,128]{1,0:T(8,128)(2,1)S(1)}, bf16[1024,128]{1,0:T(8,128)(2,1)S(1)}, u32[]{:S(2)}, u32[]{:S(2)}) collective-permute-start(bf16[1024,128]{1,0:T(8,128)(2,1)S(1)} %get-tuple-element.16.refs_2_), channel_id=1, source_target_pairs={{0,2},{2,4},{4,6},{6,8},{8,10},{10,12},{12,14},{14,0},{1,3},{3,5},... | collective-permute-start | bytes 786440 | tf_op jit(solution)/shard_map/ppermute | solution.py:137
  17.2 8.2 %collective-permute-start.2 = (bf16[1024,128]{1,0:T(8,128)(2,1)S(1)}, bf16[1024,128]{1,0:T(8,128)(2,1)S(1)}, u32[]{:S(2)}, u32[]{:S(2)}) collective-permute-start(bf16[1024,128]{1,0:T(8,128)(2,1)S(1)} %get-tuple-element.16.refs_2_), channel_id=1, source_target_pairs={{0,14},{2,0},{4,2},{6,4},{8,6},{10,8},{12,10},{14,12},{1,15},{3,1}... | collective-permute-start | bytes 786440 | tf_op jit(solution)/shard_map/ppermute | solution.py:138
  25.4 1.0 fusion.c_ref
  26.4 1.9 %shard_map.80.l3 = f32[512,128]{1,0:T(8,128)S(1)} custom-call(bf16[2048,128]{1,0:T(8,128)(2,1)S(1)} %copy-done.3, bf16[2048,128]{1,0:T(8,128)(2,1)S(1)} %copy-done.1, bf16[2048,128]{1,0:T(8,128)(2,1)S(1)} %copy-done.2, f32[2048,17]{1,0:T(8,128)S(1)} %fusion.c_ref), custom_call_target="tpu_custom_call" | custom-call | flops 536870912 | bytes 1048576 | tf_op jit(solution)/shard_map/pallas_call | solution.py:70
  28.3 1.9 %collective-permute-start.4 = (bf16[1024,128]{1,0:T(8,128)(2,1)}, bf16[1024,128]{1,0:T(8,128)(2,1)}, u32[]{:S(2)}, u32[]{:S(2)}) collective-permute-start(bf16[1024,128]{1,0:T(8,128)(2,1)} %collective-permute-done.refs_3_), channel_id=1, source_target_pairs={{0,2},{2,4},{4,6},{6,8},{8,10},{10,12},{12,14},{14,0},{1,3},{3,5},... | collective-permute-start | bytes 786440 | tf_op jit(solution)/shard_map/ppermute | solution.py:137
  30.2 5.5 %collective-permute-start.13 = (bf16[1024,128]{1,0:T(8,128)(2,1)}, bf16[1024,128]{1,0:T(8,128)(2,1)}, u32[]{:S(2)}, u32[]{:S(2)}) collective-permute-start(bf16[1024,128]{1,0:T(8,128)(2,1)} %collective-permute-done.refs_3_), channel_id=1, source_target_pairs={{0,14},{2,0},{4,2},{6,4},{8,6},{10,8},{12,10},{14,12},{1,15},{3,1}... | collective-permute-start | bytes 786440 | tf_op jit(solution)/shard_map/ppermute | solution.py:138
  35.7 0.0 collective-permute-done.1.refs_4_
  35.7 0.0 collective-permute-done.2.refs_5_
  35.8 0.3 fusion.2
  36.1 0.3 copy-done.4
  36.5 4.3 %collective-permute-start.3 = (f32[128,128]{1,0:T(8,128)S(1)}, f32[128,128]{1,0:T(8,128)S(1)}, u32[]{:S(2)}, u32[]{:S(2)}) collective-permute-start(f32[128,128]{1,0:T(8,128)S(1)} %fusion.2), channel_id=1, source_target_pairs={{0,16},{16,0},{32,48},{48,32},{64,80},{80,64},{96,112},{112,96},{1... | collective-permute-start | bytes 196616 | tf_op jit(solution)/shard_map/ppermute | solution.py:159
  40.8 1.1 shard_map.77.l0
  41.9 1.2 shard_map.78.l1
  43.1 4.1 %collective-permute-start.6 = (bf16[1024,128]{1,0:T(8,128)(2,1)S(1)}, bf16[1024,128]{1,0:T(8,128)(2,1)S(1)}, u32[]{:S(2)}, u32[]{:S(2)}) collective-permute-start(bf16[1024,128]{1,0:T(8,128)(2,1)S(1)} %copy-done.5), channel_id=1, source_target_pairs={{0,2},{2,4},{4,6},{6,8},{8,10},{10,12},{12,14},{14,0},{1,3},{3,5},... | collective-permute-start | bytes 786440 | tf_op jit(solution)/shard_map/ppermute | solution.py:137
  47.3 1.7 %shard_map.79.l2 = f32[512,128]{1,0:T(8,128)S(1)} custom-call(bf16[2048,128]{1,0:T(8,128)(2,1)S(1)} %copy-done.3, bf16[2048,128]{1,0:T(8,128)(2,1)S(1)} %copy-done.1, bf16[2048,128]{1,0:T(8,128)(2,1)S(1)} %copy-done.2, f32[2048,17]{1,0:T(8,128)S(1)} %fusion.c_ref), custom_call_target="tpu_custom_call" | custom-call | flops 402653184 | bytes 786432 | tf_op jit(solution)/shard_map/pallas_call | solution.py:70
  49.0 3.4 %collective-permute-start.8 = (bf16[1024,128]{1,0:T(8,128)(2,1)S(1)}, bf16[1024,128]{1,0:T(8,128)(2,1)S(1)}, u32[]{:S(2)}, u32[]{:S(2)}) collective-permute-start(bf16[1024,128]{1,0:T(8,128)(2,1)S(1)} %copy-done.8), channel_id=1, source_target_pairs={{0,14},{2,0},{4,2},{6,4},{8,6},{10,8},{12,10},{14,12},{1,15},{3,1}... | collective-permute-start | bytes 786440 | tf_op jit(solution)/shard_map/ppermute | solution.py:138
  52.3 0.0 collective-permute-done.13.refs_7_
  52.3 3.4 %collective-permute-start.14 = (bf16[1024,128]{1,0:T(8,128)(2,1)}, bf16[1024,128]{1,0:T(8,128)(2,1)S(1)}, u32[]{:S(2)}, u32[]{:S(2)}) collective-permute-start(bf16[1024,128]{1,0:T(8,128)(2,1)} %collective-permute-done.13.refs_7_), channel_id=1, source_target_pairs={{0,14},{2,0},{4,2},{6,4},{8,6},{10,8},{12,10},{14,12},{1,15},{3,1}... | collective-permute-start | bytes 786440 | tf_op jit(solution)/shard_map/ppermute | solution.py:138
  55.7 0.0 collective-permute-done.3
  55.7 0.0 collective-permute-done.4.refs_6_
  55.8 3.1 %collective-permute-start.5 = (f32[128,128]{1,0:T(8,128)S(1)}, f32[128,128]{1,0:T(8,128)S(1)}, u32[]{:S(2)}, u32[]{:S(2)}) collective-permute-start(f32[128,128]{1,0:T(8,128)S(1)} %add.27), channel_id=1, source_target_pairs={{0,32},{16,48},{32,0},{48,16},{64,96},{80,112},{96,64},{112,80},{1... | collective-permute-start | bytes 196616 | tf_op jit(solution)/shard_map/ppermute | solution.py:159
  58.9 2.9 %collective-permute-start.10 = (bf16[1024,128]{1,0:T(8,128)(2,1)}, bf16[1024,128]{1,0:T(8,128)(2,1)}, u32[]{:S(2)}, u32[]{:S(2)}) collective-permute-start(bf16[1024,128]{1,0:T(8,128)(2,1)} %collective-permute-done.4.refs_6_), channel_id=1, source_target_pairs={{0,2},{2,4},{4,6},{6,8},{8,10},{10,12},{12,14},{14,0},{1,3},{3,5},... | collective-permute-start | bytes 786440 | tf_op jit(solution)/shard_map/ppermute | solution.py:137
  61.8 0.0 collective-permute-done.5
  61.8 0.0 collective-permute-done.6.refs_8_
  61.8 4.4 %collective-permute-start.7 = (f32[128,128]{1,0:T(8,128)S(1)}, f32[128,128]{1,0:T(8,128)S(1)}, u32[]{:S(2)}, u32[]{:S(2)}) collective-permute-start(f32[128,128]{1,0:T(8,128)S(1)} %add.28), channel_id=1, source_target_pairs={{0,64},{16,80},{32,96},{48,112},{64,0},{80,16},{96,32},{112,48},{1... | collective-permute-start | bytes 196616 | tf_op jit(solution)/shard_map/ppermute | solution.py:159
  66.2 5.5 %collective-permute-start.15 = (bf16[1024,128]{1,0:T(8,128)(2,1)S(1)}, bf16[1024,128]{1,0:T(8,128)(2,1)}, u32[]{:S(2)}, u32[]{:S(2)}) collective-permute-start(bf16[1024,128]{1,0:T(8,128)(2,1)S(1)} %collective-permute-done.6.refs_8_), channel_id=1, source_target_pairs={{0,2},{2,4},{4,6},{6,8},{8,10},{10,12},{12,14},{14,0},{1,3},{3,5},... | collective-permute-start | bytes 786440 | tf_op jit(solution)/shard_map/ppermute | solution.py:137
  71.7 6.5 %collective-permute-done.14.refs_11_ = bf16[1024,128]{1,0:T(8,128)(2,1)S(1)} collective-permute-done((bf16[1024,128]{1,0:T(8,128)(2,1)}, bf16[1024,128]{1,0:T(8,128)(2,1)S(1)}, u32[]{:S(2)}, u32[]{:S(2)}) %collective-permute-start.14) | collective-permute-done | bytes 262176 | tf_op jit(solution)/shard_map/ppermute | solution.py:138
  78.2 1.9 %collective-permute-start.18 = (bf16[1024,128]{1,0:T(8,128)(2,1)S(1)}, bf16[1024,128]{1,0:T(8,128)(2,1)}, u32[]{:S(2)}, u32[]{:S(2)}) collective-permute-start(bf16[1024,128]{1,0:T(8,128)(2,1)S(1)} %collective-permute-done.14.refs_11_), channel_id=1, source_target_pairs={{0,14},{2,0},{4,2},{6,4},{8,6},{10,8},{12,10},{14,12},{1,15},{3,1}... | collective-permute-start | bytes 786440 | tf_op jit(solution)/shard_map/ppermute | solution.py:138
  80.1 0.0 collective-permute-done.7
  80.2 0.0 collective-permute-done.8.refs_9_
  80.2 3.2 %collective-permute-start.9 = (f32[128,128]{1,0:T(8,128)S(1)}, f32[128,128]{1,0:T(8,128)S(1)}, u32[]{:S(2)}, u32[]{:S(2)}) collective-permute-start(f32[128,128]{1,0:T(8,128)S(1)} %add.29), channel_id=1, source_target_pairs={{0,128},{16,144},{32,160},{48,176},{64,192},{80,208},{96,224},{112... | collective-permute-start | bytes 196616 | tf_op jit(solution)/shard_map/ppermute | solution.py:159
  83.4 2.2 %collective-permute-done.9 = f32[128,128]{1,0:T(8,128)S(1)} collective-permute-done((f32[128,128]{1,0:T(8,128)S(1)}, f32[128,128]{1,0:T(8,128)S(1)}, u32[]{:S(2)}, u32[]{:S(2)}) %collective-permute-start.9) | collective-permute-done | bytes 65568 | tf_op jit(solution)/shard_map/ppermute | solution.py:159
  85.6 0.0 collective-permute-done.10.refs_10_
  85.6 4.8 %collective-permute-start.11 = (f32[128,128]{1,0:T(8,128)S(1)}, f32[128,128]{1,0:T(8,128)S(1)}, u32[]{:S(2)}, u32[]{:S(2)}) collective-permute-start(f32[128,128]{1,0:T(8,128)S(1)} %add.30), channel_id=1, source_target_pairs={{0,256},{16,272},{32,288},{48,304},{64,320},{80,336},{96,352},{112... | collective-permute-start | bytes 196616 | tf_op jit(solution)/shard_map/ppermute | solution.py:159
  90.5 1.6 %collective-permute-done.11 = f32[128,128]{1,0:T(8,128)S(1)} collective-permute-done((f32[128,128]{1,0:T(8,128)S(1)}, f32[128,128]{1,0:T(8,128)S(1)}, u32[]{:S(2)}, u32[]{:S(2)}) %collective-permute-start.11) | collective-permute-done | bytes 65568 | tf_op jit(solution)/shard_map/ppermute | solution.py:159
  92.1 0.1 subtract_convert_fusion
  92.2 3.0 %shard_map.81 = bf16[2048,128]{1,0:T(8,128)(2,1)} custom-call(f32[512,128]{1,0:T(8,128)S(1)} %shard_map.77.l0, f32[512,128]{1,0:T(8,128)S(1)} %shard_map.78.l1, f32[512,128]{1,0:T(8,128)S(1)} %shard_map.79.l2, f32[512,128]{1,0:T(8,128)S(1)} %shard_map.80.l3, bf16[2048,128]{1,0:T(8,128)(2,1)S(1)} %copy-done.3, f32[2048,17]{1,0:T(8,128)S(1)} %fusion.c_ref, ...), custom_call_target="tpu_custom_call" | custom-call | flops 671088640 | bytes 4194304 | tf_op jit(solution)/shard_map/pallas_call | solution.py:107
  95.2 1.1 constant_dynamic-slice_fusion
  96.3 7.5 %collective-permute-start.12 = (bf16[1024,128]{1,0:T(8,128)(2,1)S(1)}, bf16[1024,128]{1,0:T(8,128)(2,1)S(1)}, u32[]{:S(2)}, u32[]{:S(2)}) collective-permute-start(bf16[1024,128]{1,0:T(8,128)(2,1)S(1)} %get-tuple-element.32), channel_id=1, source_target_pairs={{0,1},{1,0},{2,3},{3,2},{4,5},{5,4},{6,7},{7,6},{8,9},{9,8},{10,11... | collective-permute-start | bytes 786440 | tf_op jit(solution)/shard_map/ppermute | solution.py:125
  103.9 2.3 %collective-permute-start.16 = (bf16[1024,128]{1,0:T(8,128)(2,1)S(1)}, bf16[1024,128]{1,0:T(8,128)(2,1)S(1)}, u32[]{:S(2)}, u32[]{:S(2)}) collective-permute-start(bf16[1024,128]{1,0:T(8,128)(2,1)S(1)} %collective-permute-done.8.refs_9_), channel_id=1, source_target_pairs={{0,14},{2,0},{4,2},{6,4},{8,6},{10,8},{12,10},{14,12},{1,15},{3,1}... | collective-permute-start | bytes 786440 | tf_op jit(solution)/shard_map/ppermute | solution.py:138
  106.2 3.9 %collective-permute-start.17 = (bf16[1024,128]{1,0:T(8,128)(2,1)}, bf16[1024,128]{1,0:T(8,128)(2,1)S(1)}, u32[]{:S(2)}, u32[]{:S(2)}) collective-permute-start(bf16[1024,128]{1,0:T(8,128)(2,1)} %collective-permute-done.10.refs_10_), channel_id=1, source_target_pairs={{0,2},{2,4},{4,6},{6,8},{8,10},{10,12},{12,14},{14,0},{1,3},{3,5},... | collective-permute-start | bytes 786440 | tf_op jit(solution)/shard_map/ppermute | solution.py:137
  110.1 0.0 collective-permute-done.15.refs_2_
  110.1 1.9 %collective-permute-start.19 = (bf16[1024,128]{1,0:T(8,128)(2,1)}, bf16[1024,128]{1,0:T(8,128)(2,1)S(1)}, u32[]{:S(2)}, u32[]{:S(2)}) collective-permute-start(bf16[1024,128]{1,0:T(8,128)(2,1)} %collective-permute-done.15.refs_2_), channel_id=1, source_target_pairs={{0,2},{2,4},{4,6},{6,8},{8,10},{10,12},{12,14},{14,0},{1,3},{3,5},... | collective-permute-start | bytes 786440 | tf_op jit(solution)/shard_map/ppermute | solution.py:144
  112.0 0.0 collective-permute-done.18.refs_5_
  112.0 5.5 %collective-permute-start.20 = (bf16[1024,128]{1,0:T(8,128)(2,1)}, bf16[1024,128]{1,0:T(8,128)(2,1)S(1)}, u32[]{:S(2)}, u32[]{:S(2)}) collective-permute-start(bf16[1024,128]{1,0:T(8,128)(2,1)} %collective-permute-done.18.refs_5_), channel_id=1, source_target_pairs={{0,14},{2,0},{4,2},{6,4},{8,6},{10,8},{12,10},{14,12},{1,15},{3,1}... | collective-permute-start | bytes 786440 | tf_op jit(solution)/shard_map/ppermute | solution.py:144
  117.5 0.1 pad_add_fusion.where_ref
  117.6 0.0 collective-permute-done.12.refs_1_
  117.6 0.9 copy-done.11
  118.5 2.1 %shard_map.82.early_ref = bf16[10,128,256]{2,1,0:T(8,128)(2,1)S(1)} custom-call(s32[2]{0:T(128)S(1)} %pad_add_fusion.where_ref, bf16[1024,128]{1,0:T(8,128)(2,1)S(1)} %get-tuple-element.33.refs_0_, bf16[1024,128]{1,0:T(8,128)(2,1)S(1)} %collective-permute-done.12.refs_1_, bf16[1024,128]{1,0:T(8,128)(2,1)S(1)} %get-tuple-element.16.refs_2_, ...), custom_call_target="tpu_custom_call" | custom-call | flops 671088640 | bytes 3145728 | tf_op jit(solution)/shard_map/pallas_call | solution.py:239
  120.7 0.0 collective-permute-done.16.refs_3_
  120.7 0.0 collective-permute-done.17.refs_4_
  120.7 4.2 %collective-permute-done.19.refs_6_ = bf16[1024,128]{1,0:T(8,128)(2,1)S(1)} collective-permute-done((bf16[1024,128]{1,0:T(8,128)(2,1)}, bf16[1024,128]{1,0:T(8,128)(2,1)S(1)}, u32[]{:S(2)}, u32[]{:S(2)}) %collective-permute-start.19) | collective-permute-done | bytes 262176 | tf_op jit(solution)/shard_map/ppermute | solution.py:144
  124.9 7.1 %collective-permute-done.20.refs_7_ = bf16[1024,128]{1,0:T(8,128)(2,1)S(1)} collective-permute-done((bf16[1024,128]{1,0:T(8,128)(2,1)}, bf16[1024,128]{1,0:T(8,128)(2,1)S(1)}, u32[]{:S(2)}, u32[]{:S(2)}) %collective-permute-start.20) | collective-permute-done | bytes 262176 | tf_op jit(solution)/shard_map/ppermute | solution.py:144
  131.9 1.7 %shard_map.83 = bf16[16,2,2,64,128]{4,3,2,1,0:T(8,128)(2,1)S(1)} custom-call(s32[2]{0:T(128)S(1)} %pad_add_fusion.where_ref, bf16[10,128,256]{2,1,0:T(8,128)(2,1)S(1)} %shard_map.82.early_ref, bf16[1024,128]{1,0:T(8,128)(2,1)S(1)} %get-tuple-element.33.refs_0_, bf16[1024,128]{1,0:T(8,128)(2,1)S(1)} %collective-permute-done.12.refs_1_, ...), custom_call_target="tpu_custom_call" | custom-call | flops 402653184 | bytes 2097152 | tf_op jit(solution)/shard_map/pallas_call | solution.py:247
  133.7 28.5 %all_to_all.5 = bf16[64,64,128]{2,1,0:T(8,128)(2,1)S(1)} all-to-all(bf16[64,64,128]{2,1,0:T(8,128)(2,1)S(1)} %bitcast.16), channel_id=1, replica_groups=mesh['seq'=32,'zh'=8,'zl'=2] {'seq','zl'}, dimensions={0} | all-to-all | bytes 2097152 | tf_op jit(solution)/shard_map/all_to_all | solution.py:300
  162.2 0.2 convert_reduce_fusion
  162.4 0.6 broadcast_multiply_fusion
  (29 shorter events, 0.1 us)
Async XLA Ops:
  0.6 24.8 %copy-start = (f32[64,17]{0,1:T(8,128)S(1)}, f32[64,17]{0,1:T(8,128)}, u32[]{:S(2)}) copy-start(f32[64,17]{0,1:T(8,128)} %param.10) | copy-start | bytes 13060
  0.6 24.7 %copy-start.12 = (s32[2048]{0:T(1024)S(1)}, s32[2048]{0:T(1024)}, u32[]{:S(2)}) copy-start(s32[2048]{0:T(1024)} %param.9) | copy-start | bytes 24580
  0.7 25.7 %copy-start.1 = (bf16[2048,128]{1,0:T(8,128)(2,1)S(1)}, bf16[2048,128]{1,0:T(8,128)(2,1)}, u32[]{:S(2)}) copy-start(bf16[2048,128]{1,0:T(8,128)(2,1)} %k_ref.7) | copy-start | bytes 1572868
  0.7 25.7 %copy-start.2 = (bf16[2048,128]{1,0:T(8,128)(2,1)S(1)}, bf16[2048,128]{1,0:T(8,128)(2,1)}, u32[]{:S(2)}) copy-start(bf16[2048,128]{1,0:T(8,128)(2,1)} %v_ref.7) | copy-start | bytes 1572868
  0.7 25.7 %copy-start.3 = (bf16[2048,128]{1,0:T(8,128)(2,1)S(1)}, bf16[2048,128]{1,0:T(8,128)(2,1)}, u32[]{:S(2)}) copy-start(bf16[2048,128]{1,0:T(8,128)(2,1)} %q_ref.9) | copy-start | bytes 1572868
  1.9 8.2 %collective-permute-start = (bf16[1024,128]{1,0:T(8,128)(2,1)S(1)}, bf16[1024,128]{1,0:T(8,128)(2,1)}, u32[]{:S(2)}, u32[]{:S(2)}) collective-permute-start(bf16[1024,128]{1,0:T(8,128)(2,1)S(1)} %get-tuple-element.34), channel_id=1, source_target_pairs={{0,1},{1,0},{2,3},{3,2},{4,5},{5,4},{6,7},{7,6},{8,9},{9,8},{10,11... | collective-permute-start | bytes 786440 | tf_op jit(solution)/shard_map/ppermute | solution.py:125
  10.1 25.6 %collective-permute-start.1 = (bf16[1024,128]{1,0:T(8,128)(2,1)S(1)}, bf16[1024,128]{1,0:T(8,128)(2,1)S(1)}, u32[]{:S(2)}, u32[]{:S(2)}) collective-permute-start(bf16[1024,128]{1,0:T(8,128)(2,1)S(1)} %get-tuple-element.16.refs_2_), channel_id=1, source_target_pairs={{0,2},{2,4},{4,6},{6,8},{8,10},{10,12},{12,14},{14,0},{1,3},{3,5},... | collective-permute-start | bytes 786440 | tf_op jit(solution)/shard_map/ppermute | solution.py:137
  17.2 18.6 %collective-permute-start.2 = (bf16[1024,128]{1,0:T(8,128)(2,1)S(1)}, bf16[1024,128]{1,0:T(8,128)(2,1)S(1)}, u32[]{:S(2)}, u32[]{:S(2)}) collective-permute-start(bf16[1024,128]{1,0:T(8,128)(2,1)S(1)} %get-tuple-element.16.refs_2_), channel_id=1, source_target_pairs={{0,14},{2,0},{4,2},{6,4},{8,6},{10,8},{12,10},{14,12},{1,15},{3,1}... | collective-permute-start | bytes 786440 | tf_op jit(solution)/shard_map/ppermute | solution.py:138
  28.3 27.4 %collective-permute-start.4 = (bf16[1024,128]{1,0:T(8,128)(2,1)}, bf16[1024,128]{1,0:T(8,128)(2,1)}, u32[]{:S(2)}, u32[]{:S(2)}) collective-permute-start(bf16[1024,128]{1,0:T(8,128)(2,1)} %collective-permute-done.refs_3_), channel_id=1, source_target_pairs={{0,2},{2,4},{4,6},{6,8},{8,10},{10,12},{12,14},{14,0},{1,3},{3,5},... | collective-permute-start | bytes 786440 | tf_op jit(solution)/shard_map/ppermute | solution.py:137
  30.2 22.1 %collective-permute-start.13 = (bf16[1024,128]{1,0:T(8,128)(2,1)}, bf16[1024,128]{1,0:T(8,128)(2,1)}, u32[]{:S(2)}, u32[]{:S(2)}) collective-permute-start(bf16[1024,128]{1,0:T(8,128)(2,1)} %collective-permute-done.refs_3_), channel_id=1, source_target_pairs={{0,14},{2,0},{4,2},{6,4},{8,6},{10,8},{12,10},{14,12},{1,15},{3,1}... | collective-permute-start | bytes 786440 | tf_op jit(solution)/shard_map/ppermute | solution.py:138
  35.7 0.7 copy-start.4
  35.8 5.0 %copy-start.7 = (bf16[1024,128]{1,0:T(8,128)(2,1)}, bf16[1024,128]{1,0:T(8,128)(2,1)S(1)}, u32[]{:S(2)}) copy-start(bf16[1024,128]{1,0:T(8,128)(2,1)S(1)} %collective-permute-done.2.refs_5_) | copy-start | bytes 786436
  36.5 19.3 %collective-permute-start.3 = (f32[128,128]{1,0:T(8,128)S(1)}, f32[128,128]{1,0:T(8,128)S(1)}, u32[]{:S(2)}, u32[]{:S(2)}) collective-permute-start(f32[128,128]{1,0:T(8,128)S(1)} %fusion.2), channel_id=1, source_target_pairs={{0,16},{16,0},{32,48},{48,32},{64,80},{80,64},{96,112},{112,96},{1... | collective-permute-start | bytes 196616 | tf_op jit(solution)/shard_map/ppermute | solution.py:159
  41.9 1.2 copy-start.5
  43.1 5.8 %copy-start.8 = (bf16[1024,128]{1,0:T(8,128)(2,1)S(1)}, bf16[1024,128]{1,0:T(8,128)(2,1)}, u32[]{:S(2)}) copy-start(bf16[1024,128]{1,0:T(8,128)(2,1)} %copy-done.7) | copy-start | bytes 786436
  43.1 18.7 %collective-permute-start.6 = (bf16[1024,128]{1,0:T(8,128)(2,1)S(1)}, bf16[1024,128]{1,0:T(8,128)(2,1)S(1)}, u32[]{:S(2)}, u32[]{:S(2)}) collective-permute-start(bf16[1024,128]{1,0:T(8,128)(2,1)S(1)} %copy-done.5), channel_id=1, source_target_pairs={{0,2},{2,4},{4,6},{6,8},{8,10},{10,12},{12,14},{14,0},{1,3},{3,5},... | collective-permute-start | bytes 786440 | tf_op jit(solution)/shard_map/ppermute | solution.py:137
  49.0 31.2 %collective-permute-start.8 = (bf16[1024,128]{1,0:T(8,128)(2,1)S(1)}, bf16[1024,128]{1,0:T(8,128)(2,1)S(1)}, u32[]{:S(2)}, u32[]{:S(2)}) collective-permute-start(bf16[1024,128]{1,0:T(8,128)(2,1)S(1)} %copy-done.8), channel_id=1, source_target_pairs={{0,14},{2,0},{4,2},{6,4},{8,6},{10,8},{12,10},{14,12},{1,15},{3,1}... | collective-permute-start | bytes 786440 | tf_op jit(solution)/shard_map/ppermute | solution.py:138
  52.3 25.9 %collective-permute-start.14 = (bf16[1024,128]{1,0:T(8,128)(2,1)}, bf16[1024,128]{1,0:T(8,128)(2,1)S(1)}, u32[]{:S(2)}, u32[]{:S(2)}) collective-permute-start(bf16[1024,128]{1,0:T(8,128)(2,1)} %collective-permute-done.13.refs_7_), channel_id=1, source_target_pairs={{0,14},{2,0},{4,2},{6,4},{8,6},{10,8},{12,10},{14,12},{1,15},{3,1}... | collective-permute-start | bytes 786440 | tf_op jit(solution)/shard_map/ppermute | solution.py:138
  55.8 6.0 %collective-permute-start.5 = (f32[128,128]{1,0:T(8,128)S(1)}, f32[128,128]{1,0:T(8,128)S(1)}, u32[]{:S(2)}, u32[]{:S(2)}) collective-permute-start(f32[128,128]{1,0:T(8,128)S(1)} %add.27), channel_id=1, source_target_pairs={{0,32},{16,48},{32,0},{48,16},{64,96},{80,112},{96,64},{112,80},{1... | collective-permute-start | bytes 196616 | tf_op jit(solution)/shard_map/ppermute | solution.py:159
  58.9 26.7 %collective-permute-start.10 = (bf16[1024,128]{1,0:T(8,128)(2,1)}, bf16[1024,128]{1,0:T(8,128)(2,1)}, u32[]{:S(2)}, u32[]{:S(2)}) collective-permute-start(bf16[1024,128]{1,0:T(8,128)(2,1)} %collective-permute-done.4.refs_6_), channel_id=1, source_target_pairs={{0,2},{2,4},{4,6},{6,8},{8,10},{10,12},{12,14},{14,0},{1,3},{3,5},... | collective-permute-start | bytes 786440 | tf_op jit(solution)/shard_map/ppermute | solution.py:137
  61.8 33.4 %copy-start.10 = (bf16[1024,128]{1,0:T(8,128)(2,1)}, bf16[1024,128]{1,0:T(8,128)(2,1)S(1)}, u32[]{:S(2)}) copy-start(bf16[1024,128]{1,0:T(8,128)(2,1)S(1)} %collective-permute-done.6.refs_8_) | copy-start | bytes 786436
  61.8 18.3 %collective-permute-start.7 = (f32[128,128]{1,0:T(8,128)S(1)}, f32[128,128]{1,0:T(8,128)S(1)}, u32[]{:S(2)}, u32[]{:S(2)}) collective-permute-start(f32[128,128]{1,0:T(8,128)S(1)} %add.28), channel_id=1, source_target_pairs={{0,64},{16,80},{32,96},{48,112},{64,0},{80,16},{96,32},{112,48},{1... | collective-permute-start | bytes 196616 | tf_op jit(solution)/shard_map/ppermute | solution.py:159
  66.2 43.9 %collective-permute-start.15 = (bf16[1024,128]{1,0:T(8,128)(2,1)S(1)}, bf16[1024,128]{1,0:T(8,128)(2,1)}, u32[]{:S(2)}, u32[]{:S(2)}) collective-permute-start(bf16[1024,128]{1,0:T(8,128)(2,1)S(1)} %collective-permute-done.6.refs_8_), channel_id=1, source_target_pairs={{0,2},{2,4},{4,6},{6,8},{8,10},{10,12},{12,14},{14,0},{1,3},{3,5},... | collective-permute-start | bytes 786440 | tf_op jit(solution)/shard_map/ppermute | solution.py:137
  78.2 33.8 %collective-permute-start.18 = (bf16[1024,128]{1,0:T(8,128)(2,1)S(1)}, bf16[1024,128]{1,0:T(8,128)(2,1)}, u32[]{:S(2)}, u32[]{:S(2)}) collective-permute-start(bf16[1024,128]{1,0:T(8,128)(2,1)S(1)} %collective-permute-done.14.refs_11_), channel_id=1, source_target_pairs={{0,14},{2,0},{4,2},{6,4},{8,6},{10,8},{12,10},{14,12},{1,15},{3,1}... | collective-permute-start | bytes 786440 | tf_op jit(solution)/shard_map/ppermute | solution.py:138
  80.2 5.4 %collective-permute-start.9 = (f32[128,128]{1,0:T(8,128)S(1)}, f32[128,128]{1,0:T(8,128)S(1)}, u32[]{:S(2)}, u32[]{:S(2)}) collective-permute-start(f32[128,128]{1,0:T(8,128)S(1)} %add.29), channel_id=1, source_target_pairs={{0,128},{16,144},{32,160},{48,176},{64,192},{80,208},{96,224},{112... | collective-permute-start | bytes 196616 | tf_op jit(solution)/shard_map/ppermute | solution.py:159
  85.6 6.5 %collective-permute-start.11 = (f32[128,128]{1,0:T(8,128)S(1)}, f32[128,128]{1,0:T(8,128)S(1)}, u32[]{:S(2)}, u32[]{:S(2)}) collective-permute-start(f32[128,128]{1,0:T(8,128)S(1)} %add.30), channel_id=1, source_target_pairs={{0,256},{16,272},{32,288},{48,304},{64,320},{80,336},{96,352},{112... | collective-permute-start | bytes 196616 | tf_op jit(solution)/shard_map/ppermute | solution.py:159
  95.2 22.4 %copy-start.6 = (bf16[1024,128]{1,0:T(8,128)(2,1)S(1)}, bf16[1024,128]{1,0:T(8,128)(2,1)}, u32[]{:S(2)}) copy-start(bf16[1024,128]{1,0:T(8,128)(2,1)} %copy-done.4) | copy-start | bytes 786436
  95.2 22.4 %copy-start.9 = (bf16[1024,128]{1,0:T(8,128)(2,1)S(1)}, bf16[1024,128]{1,0:T(8,128)(2,1)}, u32[]{:S(2)}) copy-start(bf16[1024,128]{1,0:T(8,128)(2,1)} %copy-done.7) | copy-start | bytes 786436
  96.3 21.3 %collective-permute-start.12 = (bf16[1024,128]{1,0:T(8,128)(2,1)S(1)}, bf16[1024,128]{1,0:T(8,128)(2,1)S(1)}, u32[]{:S(2)}, u32[]{:S(2)}) collective-permute-start(bf16[1024,128]{1,0:T(8,128)(2,1)S(1)} %get-tuple-element.32), channel_id=1, source_target_pairs={{0,1},{1,0},{2,3},{3,2},{4,5},{5,4},{6,7},{7,6},{8,9},{9,8},{10,11... | collective-permute-start | bytes 786440 | tf_op jit(solution)/shard_map/ppermute | solution.py:125
  103.9 16.8 %collective-permute-start.16 = (bf16[1024,128]{1,0:T(8,128)(2,1)S(1)}, bf16[1024,128]{1,0:T(8,128)(2,1)S(1)}, u32[]{:S(2)}, u32[]{:S(2)}) collective-permute-start(bf16[1024,128]{1,0:T(8,128)(2,1)S(1)} %collective-permute-done.8.refs_9_), channel_id=1, source_target_pairs={{0,14},{2,0},{4,2},{6,4},{8,6},{10,8},{12,10},{14,12},{1,15},{3,1}... | collective-permute-start | bytes 786440 | tf_op jit(solution)/shard_map/ppermute | solution.py:138
  106.2 14.5 %collective-permute-start.17 = (bf16[1024,128]{1,0:T(8,128)(2,1)}, bf16[1024,128]{1,0:T(8,128)(2,1)S(1)}, u32[]{:S(2)}, u32[]{:S(2)}) collective-permute-start(bf16[1024,128]{1,0:T(8,128)(2,1)} %collective-permute-done.10.refs_10_), channel_id=1, source_target_pairs={{0,2},{2,4},{4,6},{6,8},{8,10},{10,12},{12,14},{14,0},{1,3},{3,5},... | collective-permute-start | bytes 786440 | tf_op jit(solution)/shard_map/ppermute | solution.py:137
  110.1 14.8 %collective-permute-start.19 = (bf16[1024,128]{1,0:T(8,128)(2,1)}, bf16[1024,128]{1,0:T(8,128)(2,1)S(1)}, u32[]{:S(2)}, u32[]{:S(2)}) collective-permute-start(bf16[1024,128]{1,0:T(8,128)(2,1)} %collective-permute-done.15.refs_2_), channel_id=1, source_target_pairs={{0,2},{2,4},{4,6},{6,8},{8,10},{10,12},{12,14},{14,0},{1,3},{3,5},... | collective-permute-start | bytes 786440 | tf_op jit(solution)/shard_map/ppermute | solution.py:144
  112.0 19.9 %collective-permute-start.20 = (bf16[1024,128]{1,0:T(8,128)(2,1)}, bf16[1024,128]{1,0:T(8,128)(2,1)S(1)}, u32[]{:S(2)}, u32[]{:S(2)}) collective-permute-start(bf16[1024,128]{1,0:T(8,128)(2,1)} %collective-permute-done.18.refs_5_), channel_id=1, source_target_pairs={{0,14},{2,0},{4,2},{6,4},{8,6},{10,8},{12,10},{14,12},{1,15},{3,1}... | collective-permute-start | bytes 786440 | tf_op jit(solution)/shard_map/ppermute | solution.py:144
  117.6 1.0 copy-start.11
